TPU v7x, 128 devices: a whole 4x4x4 slice. The times are simulated.
128 devices in a mesh: ctx: 16 (over z, y_hi, core), shard: 8 (over x, y_lo).
Axes of the slice: x: 4, y: 4 (y_hi: 2, y_lo: 2; y = y_hi * 2 + y_lo), z: 4, core: 2. Of those that a mesh axis runs over, the one named last changes fastest.
Arguments:
- tokens: bfloat16 [16, 16, 64, 1024], P('ctx', 'shard'), may hold values from -6 to 6
- lengths: int32 [16], P('shard'), may hold values from 256 to 1024, as said below
- block_pairs: int32 [16], replicated, may hold values from 0 to 15, each once
- ln1_gain: bfloat16 [1024], P('shard'), may hold values from 0.5 to 1.5
- ln1_bias: bfloat16 [1024], P('shard'), may hold values from -1.1953125 to 1.1953125
- w_qkv: bfloat16 [1024, 3072], P('shard'), may hold values from -0.1875 to 0.1875
- query_bias: bfloat16 [1024], P('shard'), may hold values from -1.796875 to 1.796875
- value_bias: bfloat16 [1024], P('shard'), may hold values from -0.59765625 to 0.59765625
- w_out: bfloat16 [1024, 1024], P('shard'), may hold values from -0.75 to 0.75
- out_bias: bfloat16 [1024], P('shard'), may hold values from -0.59765625 to 0.59765625
- ln2_gain: bfloat16 [1024], P('shard'), may hold values from 0.5 to 1.5
- ln2_bias: bfloat16 [1024], P('shard'), may hold values from -1.1953125 to 1.1953125
- w_fc1: bfloat16 [1024, 4096], P('shard'), may hold values from -0.1875 to 0.1875
- fc1_bias: bfloat16 [4096], P('shard'), may hold values from -1.796875 to 1.796875
- w_fc2: bfloat16 [4096, 1024], P('shard'), may hold values from -0.09375 to 0.09375
- fc2_bias: bfloat16 [1024], P('shard'), may hold values from -0.59765625 to 0.59765625
- out_cotangent: bfloat16 [16, 16, 64, 1024], P('ctx', 'shard'), may hold values from -6 to 6
Outputs:
- layer_out: bfloat16 [16, 16, 64, 1024], P('ctx', 'shard')
- input_grad: bfloat16 [16, 16, 64, 1024], P('ctx', 'shard')
- grad_ln1_gain: float32 [1024], P(('ctx', 'shard'))
- grad_ln1_bias: float32 [1024], P(('ctx', 'shard'))
- grad_w_qkv: float32 [1024, 3072], P(('ctx', 'shard'))
- grad_query_bias: float32 [1024], P(('ctx', 'shard'))
- grad_value_bias: float32 [1024], P(('ctx', 'shard'))
- grad_w_out: float32 [1024, 1024], P(('ctx', 'shard'))
- grad_out_bias: float32 [1024], P(('ctx', 'shard'))
- grad_ln2_gain: float32 [1024], P(('ctx', 'shard'))
- grad_ln2_bias: float32 [1024], P(('ctx', 'shard'))
- grad_w_fc1: float32 [1024, 4096], P(('ctx', 'shard'))
- grad_fc1_bias: float32 [4096], P(('ctx', 'shard'))
- grad_w_fc2: float32 [4096, 1024], P(('ctx', 'shard'))
- grad_fc2_bias: float32 [1024], P(('ctx', 'shard'))
Inputs may be any that keep to these rules, and one draw needn't show every extreme that they name: `lengths`: of the two slots on each index of shard, one, drawn from the seed, is full with 1024 valid tokens; the other has a drawn length, and some slot has exactly 256. Index c of ctx holds causal blocks block_pairs[c] and 31 - block_pairs[c] of every slot; each lower block is held once.
All inputs are finite; a program needn't handle non-finite values.
Results may differ from a plain program's by a relative error of at most 0.019.
Values may be sent and summed in bfloat16 or wider, within the bound.
A program may use at most 192 MiB of HBM per device.

v0:
```python
import jax
import jax.numpy as jnp
from jax import lax
from jax.sharding import PartitionSpec as P

HEADS = 16
HEAD_DIM = 64


eps_norm = 1e-05
negative = -1e30


def exact_gelu(inputs):
    return jax.nn.gelu(inputs, approximate=False)


def norm_parts(inputs):
    centre = inputs - jnp.mean(inputs, axis=-1, keepdims=True)
    spread = jnp.mean(centre * centre, axis=-1, keepdims=True)
    inverse = lax.rsqrt(spread + eps_norm)
    return (centre * inverse, inverse)


def norm_back(grad_normed, normed, inverse, gain):
    scaled = grad_normed * gain
    centred = scaled - jnp.mean(scaled, axis=-1, keepdims=True)
    return inverse * (centred - normed * jnp.mean(scaled * normed, axis=-1, keepdims=True))


def scores_of(query4, key4, allowed, score_scale):
    raw_scores = (
        jnp.einsum("sqhd,skhd->shqk", query4, key4, preferred_element_type=jnp.float32)
        * score_scale
    )
    return jnp.where(allowed[:, None], raw_scores, negative)


def outer_sum(left, right):
    return jnp.einsum("rd,re->de", left, right, preferred_element_type=jnp.float32)


def shards(
    tokens,
    lengths,
    block_pairs,
    ln1_gain,
    ln1_bias,
    w_qkv,
    query_bias,
    value_bias,
    w_out,
    out_bias,
    ln2_gain,
    ln2_bias,
    w_fc1,
    fc1_bias,
    w_fc2,
    fc2_bias,
    out_cotangent,
):
    slot_rows = tokens.shape[2]
    model_width = tokens.shape[3]
    ctx_count = lax.axis_size("ctx")
    block_rows = slot_rows // 2
    row_count = 2 * slot_rows
    key_count = ctx_count * slot_rows
    score_scale = HEAD_DIM ** (-0.5)
    device = lax.axis_index("ctx")
    row_index = jnp.arange(slot_rows)
    half_index = row_index // block_rows
    within = row_index % block_rows
    blocks = jnp.where(
        half_index[None, :] == 0, block_pairs[:, None], 2 * ctx_count - 1 - block_pairs[:, None]
    )
    key_place = blocks * block_rows + within[None, :]
    is_mine = (jnp.arange(ctx_count) == device)[:, None]
    query_place = jnp.sum(jnp.where(is_mine, key_place, 0), axis=0)
    key_place = key_place.reshape(key_count)
    allowed = (key_place[None, None, :] < lengths[:, None, None]) & (
        key_place[None, None, :] <= query_place[None, :, None]
    )
    row_valid = (query_place[None, :] < lengths[:, None]).astype(jnp.float32).reshape(row_count, 1)
    residual = tokens.reshape(row_count, model_width).astype(jnp.float32)
    gain_one, bias_one, bias_query, bias_value, bias_out, qkv_weight, out_weight = (
        lax.all_gather(ln1_gain, "shard", axis=0, tiled=True),
        lax.all_gather(ln1_bias, "shard", axis=0, tiled=True),
        lax.all_gather(query_bias, "shard", axis=0, tiled=True),
        lax.all_gather(value_bias, "shard", axis=0, tiled=True),
        lax.all_gather(out_bias, "shard", axis=0, tiled=True),
        lax.all_gather(w_qkv, "shard", axis=0, tiled=True),
        lax.all_gather(w_out, "shard", axis=0, tiled=True),
    )
    gain_one = gain_one.astype(jnp.float32)
    bias_one = bias_one.astype(jnp.float32)
    bias_query = bias_query.astype(jnp.float32)
    bias_value = bias_value.astype(jnp.float32)
    bias_out = bias_out.astype(jnp.float32)
    normed_one, inverse_one = norm_parts(residual)
    attn_in = (normed_one * gain_one + bias_one).astype(jnp.bfloat16)
    qkv_dot = jnp.dot(attn_in, qkv_weight, preferred_element_type=jnp.float32)
    query_low = (qkv_dot[:, :model_width] + bias_query).astype(jnp.bfloat16)
    key_low = qkv_dot[:, model_width : 2 * model_width].astype(jnp.bfloat16)
    value_low = (qkv_dot[:, 2 * model_width :] + bias_value).astype(jnp.bfloat16)
    key_value = jnp.concatenate([key_low, value_low], axis=1).reshape(2, slot_rows, 2 * model_width)
    gathered = lax.all_gather(key_value, "ctx", axis=1, tiled=True)
    query4 = query_low.reshape(2, slot_rows, HEADS, HEAD_DIM)
    key4 = gathered[:, :, :model_width].reshape(2, key_count, HEADS, HEAD_DIM)
    value4 = gathered[:, :, model_width:].reshape(2, key_count, HEADS, HEAD_DIM)
    scores = scores_of(query4, key4, allowed, score_scale)
    row_max = jnp.max(scores, axis=-1, keepdims=True)
    powers = jnp.exp(scores - row_max)
    row_total = jnp.sum(powers, axis=-1, keepdims=True)
    probs_first = (powers / row_total).astype(jnp.bfloat16)
    log_total = row_max + jnp.log(row_total)
    attended = jnp.einsum(
        "shqk,skhd->sqhd", probs_first, value4, preferred_element_type=jnp.float32
    )
    mixed_low = attended.reshape(row_count, model_width).astype(jnp.bfloat16)
    hidden = residual + (
        jnp.dot(mixed_low, out_weight, preferred_element_type=jnp.float32) + bias_out
    )
    gain_two, bias_two, bias_up, bias_down, up_weight, down_weight = (
        lax.all_gather(ln2_gain, "shard", axis=0, tiled=True),
        lax.all_gather(ln2_bias, "shard", axis=0, tiled=True),
        lax.all_gather(fc1_bias, "shard", axis=0, tiled=True),
        lax.all_gather(fc2_bias, "shard", axis=0, tiled=True),
        lax.all_gather(w_fc1, "shard", axis=0, tiled=True),
        lax.all_gather(w_fc2, "shard", axis=0, tiled=True),
    )
    gain_two = gain_two.astype(jnp.float32)
    bias_two = bias_two.astype(jnp.float32)
    bias_up = bias_up.astype(jnp.float32)
    bias_down = bias_down.astype(jnp.float32)
    normed_two, inverse_two = norm_parts(hidden)
    mlp_in = (normed_two * gain_two + bias_two).astype(jnp.bfloat16)
    pre_act = jnp.dot(mlp_in, up_weight, preferred_element_type=jnp.float32) + bias_up
    activated, gelu_pull = jax.vjp(exact_gelu, pre_act)
    act_low = activated.astype(jnp.bfloat16)
    mlp_out = jnp.dot(act_low, down_weight, preferred_element_type=jnp.float32) + bias_down
    layer_out = (row_valid * (hidden + mlp_out)).astype(jnp.bfloat16).reshape(tokens.shape)
    grad_out = out_cotangent.reshape(row_count, model_width).astype(jnp.float32) * row_valid
    grad_out_low = grad_out.astype(jnp.bfloat16)
    grad_down_b = jnp.sum(grad_out, axis=0)
    grad_act = jnp.einsum(
        "rd,fd->rf", grad_out_low, down_weight, preferred_element_type=jnp.float32
    )
    grad_pre = gelu_pull(grad_act)[0]
    grad_up_b = jnp.sum(grad_pre, axis=0)
    grad_pre_low = grad_pre.astype(jnp.bfloat16)
    grad_mlp_in = jnp.einsum(
        "rf,df->rd", grad_pre_low, up_weight, preferred_element_type=jnp.float32
    )
    grad_gain_two = jnp.sum(grad_mlp_in * normed_two, axis=0)
    grad_bias_two = jnp.sum(grad_mlp_in, axis=0)
    grad_hidden = grad_out + norm_back(grad_mlp_in, normed_two, inverse_two, gain_two)
    grad_down_w = outer_sum(act_low, grad_out_low)
    grad_up_w = outer_sum(mlp_in, grad_pre_low)
    mlp_sums = (
        lax.psum_scatter(grad_gain_two, ("ctx", "shard"), scatter_dimension=0, tiled=True),
        lax.psum_scatter(grad_bias_two, ("ctx", "shard"), scatter_dimension=0, tiled=True),
        lax.psum_scatter(grad_up_w, ("ctx", "shard"), scatter_dimension=0, tiled=True),
        lax.psum_scatter(grad_up_b, ("ctx", "shard"), scatter_dimension=0, tiled=True),
        lax.psum_scatter(grad_down_w, ("ctx", "shard"), scatter_dimension=0, tiled=True),
        lax.psum_scatter(grad_down_b, ("ctx", "shard"), scatter_dimension=0, tiled=True),
    )
    hidden_low = grad_hidden.astype(jnp.bfloat16)
    grad_out_b = jnp.sum(grad_hidden, axis=0)
    grad_mixed = jnp.einsum(
        "re,de->rd", hidden_low, out_weight, preferred_element_type=jnp.float32
    ).astype(jnp.bfloat16)
    grad_mixed4 = grad_mixed.reshape(2, slot_rows, HEADS, HEAD_DIM)
    scores_back = scores_of(query4, key4, allowed, score_scale)
    probs = jnp.exp(scores_back - log_total)
    probs_back = probs.astype(jnp.bfloat16)
    grad_probs = jnp.einsum(
        "sqhd,skhd->shqk", grad_mixed4, value4, preferred_element_type=jnp.float32
    )
    row_delta = jnp.sum(probs * grad_probs, axis=-1, keepdims=True)
    grad_scores = (probs * (grad_probs - row_delta)).astype(jnp.bfloat16)
    grad_query = (
        jnp.einsum(
            "shqk,skhd->sqhd", grad_scores, key4, preferred_element_type=jnp.float32
        ).reshape(row_count, model_width)
        * score_scale
    )
    grad_bias_query = jnp.sum(grad_query, axis=0)
    grad_key_part = (
        jnp.einsum("shqk,sqhd->kshd", grad_scores, query4, preferred_element_type=jnp.float32)
        * score_scale
    )
    grad_value_part = jnp.einsum(
        "shqk,sqhd->kshd", probs_back, grad_mixed4, preferred_element_type=jnp.float32
    )
    owned = jnp.swapaxes(
        lax.psum_scatter(
            jnp.concatenate(
                [
                    grad_key_part.reshape(slot_rows * lax.axis_size("ctx"), 2, model_width),
                    grad_value_part.reshape(slot_rows * lax.axis_size("ctx"), 2, model_width),
                ],
                axis=2,
            ).astype(jnp.bfloat16),
            "ctx",
            scatter_dimension=0,
            tiled=True,
        ).astype(jnp.float32),
        0,
        1,
    )
    grad_key = owned[:, :, :model_width].reshape(row_count, model_width)
    grad_value = owned[:, :, model_width:].reshape(row_count, model_width)
    grad_bias_value = jnp.sum(grad_value, axis=0)
    grad_qkv = jnp.concatenate([grad_query, grad_key, grad_value], axis=1).astype(jnp.bfloat16)
    grad_attn_in = jnp.einsum("re,de->rd", grad_qkv, qkv_weight, preferred_element_type=jnp.float32)
    grad_gain_one = jnp.sum(grad_attn_in * normed_one, axis=0)
    grad_bias_one = jnp.sum(grad_attn_in, axis=0)
    input_grad = (
        (grad_hidden + norm_back(grad_attn_in, normed_one, inverse_one, gain_one))
        .astype(jnp.bfloat16)
        .reshape(tokens.shape)
    )
    grad_qkv_w = outer_sum(attn_in, grad_qkv)
    grad_out_w = outer_sum(mixed_low, hidden_low)
    attn_sums = (
        lax.psum_scatter(grad_gain_one, ("ctx", "shard"), scatter_dimension=0, tiled=True),
        lax.psum_scatter(grad_bias_one, ("ctx", "shard"), scatter_dimension=0, tiled=True),
        lax.psum_scatter(grad_qkv_w, ("ctx", "shard"), scatter_dimension=0, tiled=True),
        lax.psum_scatter(grad_bias_query, ("ctx", "shard"), scatter_dimension=0, tiled=True),
        lax.psum_scatter(grad_bias_value, ("ctx", "shard"), scatter_dimension=0, tiled=True),
        lax.psum_scatter(grad_out_w, ("ctx", "shard"), scatter_dimension=0, tiled=True),
        lax.psum_scatter(grad_out_b, ("ctx", "shard"), scatter_dimension=0, tiled=True),
    )
    return (
        layer_out,
        input_grad,
        attn_sums[0],
        attn_sums[1],
        attn_sums[2],
        attn_sums[3],
        attn_sums[4],
        attn_sums[5],
        attn_sums[6],
        mlp_sums[0],
        mlp_sums[1],
        mlp_sums[2],
        mlp_sums[3],
        mlp_sums[4],
        mlp_sums[5],
    )


def solution(mesh):
    return jax.shard_map(
        shards,
        mesh=mesh,
        in_specs=(
            P("ctx", "shard", None, None),
            P("shard"),
            P(),
            P("shard"),
            P("shard"),
            P("shard", None),
            P("shard"),
            P("shard"),
            P("shard", None),
            P("shard"),
            P("shard"),
            P("shard"),
            P("shard", None),
            P("shard"),
            P("shard", None),
            P("shard"),
            P("ctx", "shard", None, None),
        ),
        out_specs=(
            P("ctx", "shard", None, None),
            P("ctx", "shard", None, None),
            P(("ctx", "shard")),
            P(("ctx", "shard")),
            P(("ctx", "shard"), None),
            P(("ctx", "shard")),
            P(("ctx", "shard")),
            P(("ctx", "shard"), None),
            P(("ctx", "shard")),
            P(("ctx", "shard")),
            P(("ctx", "shard")),
            P(("ctx", "shard"), None),
            P(("ctx", "shard")),
            P(("ctx", "shard"), None),
            P(("ctx", "shard")),
        ),
        check_vma=False,
    )
```

profile of v0, /device:TPU:0, one launch (start us, length us, event | category | flops | bytes accessed | tf_op | source)
XLA Modules:
  0.0 3440.2 jit_solution(3017760245282090610)
XLA Ops:
  7.2 0.7 all-gather.15.cloned.1.call-update
  8.0 1.1 convert_reduce_fusion.1
  9.1 1.2 multiply_reduce_fusion.7
  10.4 19.2 all-gather
  29.5 23.6 all-gather.1
  53.1 19.9 all-gather.3
  73.1 24.0 all-gather.2
  97.1 1.2 add_convert_fusion.2
  98.3 43.1 %all-gather.15.cloned.1.call-done = bf16[1024,3072]{1,0:T(8,128)(2,1)} async-done(((bf16[128,3072]{1,0:T(8,128)(2,1)}), bf16[1024,3072]{1,0:T(8,128)(2,1)}) %all-gather.15.cloned.1.call-update) | async-done | bytes 6291472 | tf_op jit(solution)/shard_map/all_gather | solution.py:91
  141.4 3.8 fusion.45
  145.4 0.8 pad_maximum_fusion.2
  146.3 0.7 all-gather.19.cloned.1.call-update
  148.3 17.5 all-gather.4
  165.7 15.0 all-gather.5
  180.7 17.0 all-gather.6
  198.1 23.8 all-gather.7
  222.2 0.8 fusion.28
  223.9 6.0 fusion.40
  229.9 6.2 copy.59
  236.1 6.2 copy.58
  242.4 3.9 fusion.43
  246.3 1.5 fusion
  247.8 2.8 copy-done
  250.6 1.0 copy-done.3
  251.5 2.0 fusion.17
  254.4 17.3 all-gather.19.cloned.1.call-done
  271.7 2.1 fusion.44
  274.1 167.8 %all-gather.21.cloned.1.call-done = bf16[1024,4096]{1,0:T(8,128)(2,1)} async-done(((bf16[128,4096]{1,0:T(8,128)(2,1)}), bf16[1024,4096]{1,0:T(8,128)(2,1)}) %all-gather.21.cloned.1.call-update) | async-done | bytes 8388624 | tf_op jit(solution)/shard_map/all_gather | solution.py:128
  441.9 4.7 convolution_add_fusion
  446.6 170.5 %all-gather.23.cloned.1.call-done = bf16[4096,1024]{1,0:T(8,128)(2,1)} async-done(((bf16[512,1024]{1,0:T(8,128)(2,1)}), bf16[4096,1024]{1,0:T(8,128)(2,1)}) %all-gather.23.cloned.1.call-update) | async-done | bytes 8388624 | tf_op jit(solution)/shard_map/all_gather | solution.py:129
  617.1 10.8 fusion.37
  627.9 3.0 multiply_reduce_fusion.2
  631.2 0.8 convolution_convert_fusion
  632.9 6.9 fusion.6
  639.8 6.7 multiply_reduce_fusion
  646.5 6.2 copy.67
  652.7 6.7 multiply_convert_fusion.1
  659.4 3.3 multiply_convert_fusion
  662.7 6.2 copy.66
  668.9 8.1 pad_maximum_fusion
  677.1 0.9 copy-done.16
  678.0 2.7 fusion.31
  681.0 0.9 copy-done.9
  681.9 8.2 fusion.24
  690.2 2.6 multiply_convert_fusion.2
  692.8 9.8 fusion.46
  702.7 5.5 fusion.41
  708.9 76.1 %reduce-scatter.6.cloned.1.call-done = bf16[64,2,2048]{2,0,1:T(8,128)(2,1)} async-done(((bf16[1024,2,2048]{2,0,1:T(8,128)(2,1)}), bf16[64,2,2048]{2,0,1:T(8,128)(2,1)}) %reduce-scatter.6.cloned.1.call-update) | async-done | bytes 524304 | tf_op jit(solution)/shard_map/reduce_scatter | solution.py:196
  785.1 1.1 fusion.42
  786.1 6.3 fusion.29
  792.5 0.6 copy-done.27
  793.1 17.6 all-gather.8
  810.9 5.5 fusion.20
  816.5 5.1 multiply_reduce_fusion.3
  821.6 63.6 %all-reduce.9 = (f32[1024]{0:T(1024)S(1)}, f32[1024]{0:T(1024)S(1)}, f32[1024]{0:T(1024)S(1)}, f32[1024]{0:T(1024)S(1)}, f32[1024]{0:T(1024)S(1)}, /*index=5*/f3...) all-reduce(f32[1024]{0:T(1024)S(1)} %get-tuple-element.17, ...), channel_id=3, replica_groups=mesh['ctx'=16,'shard'=8] {'ctx','shard'}, use_global_device_ids=true, to_apply=%region_14.15.clone | all-reduce | flops 12288 | bytes 98304
  885.2 0.6 dynamic-slice
  885.8 0.6 dynamic-slice.1
  888.7 0.6 dynamic-slice.6
  889.9 0.6 dynamic-slice.7
  890.5 1.0 add_convert_fusion
  891.4 540.2 %reduce-scatter.10.cloned.1.call-done = f32[8,1024]{1,0:T(8,128)} async-done(((f32[1024,1024]{1,0:T(8,128)}), f32[8,1024]{1,0:T(8,128)}) %reduce-scatter.10.cloned.1.call-update) | async-done | bytes 32784 | tf_op jit(solution)/shard_map/reduce_scatter | solution.py:231
  1431.7 668.7 %reduce-scatter.12.cloned.1.call-done = f32[8,4096]{1,0:T(8,128)} async-done(((f32[1024,4096]{1,0:T(8,128)}), f32[8,4096]{1,0:T(8,128)}) %reduce-scatter.12.cloned.1.call-update) | async-done | bytes 131088 | tf_op jit(solution)/shard_map/reduce_scatter | solution.py:162
  2100.4 671.3 %reduce-scatter.14.cloned.1.call-done = f32[32,1024]{1,0:T(8,128)} async-done(((f32[4096,1024]{1,0:T(8,128)}), f32[32,1024]{1,0:T(8,128)}) %reduce-scatter.14.cloned.1.call-update) | async-done | bytes 131088 | tf_op jit(solution)/shard_map/reduce_scatter | solution.py:164
  2771.6 661.3 %reduce-scatter.8.cloned.1.call-done = f32[8,3072]{1,0:T(8,128)} async-done(((f32[1024,3072]{1,0:T(8,128)}), f32[8,3072]{1,0:T(8,128)}) %reduce-scatter.8.cloned.1.call-update) | async-done | bytes 98320 | tf_op jit(solution)/shard_map/reduce_scatter | solution.py:228
  (121 shorter events, 9.7 us)
Async XLA Ops:
  7.2 134.2 %all-gather.15.cloned.1.call-start = ((), (), s32[]{:S(2)}) async-start(), calls=%async_computation.5 | async-start | bytes 7077888 | tf_op jit(solution)/shard_map/all_gather | solution.py:91
  7.9 216.0 %all-gather.17.cloned.1.call-start = ((), (), s32[]{:S(2)}) async-start(), calls=%async_computation.6 | async-start | bytes 8912896 | tf_op jit(solution)/shard_map/all_gather | solution.py:106
  98.3 46.9 %copy-start.10 = (bf16[128,1024]{1,0:T(8,128)(2,1)}, bf16[128,1024]{1,0:T(8,128)(2,1)S(1)}, u32[]{:S(2)}) copy-start(bf16[128,1024]{1,0:T(8,128)(2,1)S(1)} %add_convert_fusion.2) | copy-start | bytes 786436
  145.3 2.9 copy-start.22
  145.4 2.9 copy-start.23
  145.4 20.4 copy-start.24
  145.4 35.4 %copy-start.25 = (bf16[128]{0:T(256)(128)(2,1)S(1)}, bf16[128]{0:T(256)(128)(2,1)}, u32[]{:S(2)}) copy-start(bf16[128]{0:T(256)(128)(2,1)} %param.28) | copy-start | bytes 772
  145.4 52.4 %copy-start.26 = (s32[16]{0:T(128)S(1)}, s32[16]{0:T(128)}, u32[]{:S(2)}) copy-start(s32[16]{0:T(128)} %param.19) | copy-start | bytes 196
  145.4 52.6 %copy-start.21 = (s32[2]{0:T(128)S(1)}, s32[2]{0:T(128)}, u32[]{:S(2)}) copy-start(s32[2]{0:T(128)} %param.18) | copy-start | bytes 28
  145.4 76.8 %copy-start.12 = (bf16[1,2,64,1024]{3,2,1,0:T(8,128)(2,1)S(1)}, bf16[1,2,64,1024]{3,2,1,0:T(8,128)(2,1)}, u32[]{:S(2)}) copy-start(bf16[1,2,64,1024]{3,2,1,0:T(8,128)(2,1)} %param.33) | copy-start | bytes 786436
  146.3 125.4 %all-gather.19.cloned.1.call-start = ((), (), s32[]{:S(2)}) async-start(), calls=%async_computation.7 | async-start | bytes 2359296 | tf_op jit(solution)/shard_map/all_gather | solution.py:92
  147.0 294.8 %all-gather.21.cloned.1.call-start = ((), (), s32[]{:S(2)}) async-start(), calls=%async_computation.8 | async-start | bytes 9437184 | tf_op jit(solution)/shard_map/all_gather | solution.py:128
  147.6 469.5 %all-gather.23.cloned.1.call-start = ((), (), s32[]{:S(2)}) async-start(), calls=%async_computation.9 | async-start | bytes 9437184 | tf_op jit(solution)/shard_map/all_gather | solution.py:129
  148.2 636.9 %reduce-scatter.6.cloned.1.call-start = ((), (), s32[]{:S(2)}) async-start(), calls=%async_computation.10 | async-start | bytes 8912896 | tf_op jit(solution)/shard_map/reduce_scatter | solution.py:196
  246.3 4.3 copy-start
  246.3 5.2 copy-start.3
  251.5 20.2 copy-start.7
  254.4 187.5 %copy-start.15 = (bf16[128,1024]{1,0:T(8,128)(2,1)}, bf16[128,1024]{1,0:T(8,128)(2,1)S(1)}, u32[]{:S(2)}) copy-start(bf16[128,1024]{1,0:T(8,128)(2,1)S(1)} %convert_element_type.129) | copy-start | bytes 786436
  446.6 181.3 %copy-start.5 = (f32[128,4096]{1,0:T(8,128)}, f32[128,4096]{1,0:T(8,128)S(1)}, u32[]{:S(2)}) copy-start(f32[128,4096]{1,0:T(8,128)S(1)} %convolution_add_fusion) | copy-start | bytes 6291460
  617.1 10.8 copy-start.1
  627.9 3.1 copy-start.8
  627.9 3.1 copy-start.13
  627.9 3.3 copy-start.6
  632.9 6.9 copy-start.4
  659.4 3.3 copy-start.2
  677.0 0.9 copy-start.16
  677.1 754.6 %reduce-scatter.10.cloned.1.call-start = ((), (), s32[]{:S(2)}) async-start(), calls=%async_computation.12 | async-start | bytes 4227072 | tf_op jit(solution)/shard_map/reduce_scatter | solution.py:231
  680.7 1.2 copy-start.9
  680.7 1419.6 %reduce-scatter.12.cloned.1.call-start = ((), (), s32[]{:S(2)}) async-start(), calls=%async_computation.13 | async-start | bytes 16908288 | tf_op jit(solution)/shard_map/reduce_scatter | solution.py:162
  690.1 2081.5 %reduce-scatter.14.cloned.1.call-start = ((), (), s32[]{:S(2)}) async-start(), calls=%async_computation.14 | async-start | bytes 16908288 | tf_op jit(solution)/shard_map/reduce_scatter | solution.py:164
  690.2 2.7 copy-start.18
  702.6 2730.3 %reduce-scatter.8.cloned.1.call-start = ((), (), s32[]{:S(2)}) async-start(), calls=%async_computation.11 | async-start | bytes 12681216 | tf_op jit(solution)/shard_map/reduce_scatter | solution.py:228
  708.2 77.9 %copy-start.11 = (bf16[128,1024]{1,0:T(8,128)(2,1)S(1)}, bf16[128,1024]{1,0:T(8,128)(2,1)}, u32[]{:S(2)}) copy-start(bf16[128,1024]{1,0:T(8,128)(2,1)} %copy-done.10) | copy-start | bytes 786436
  708.9 83.5 %copy-start.19 = (bf16[128,1024]{1,0:T(8,128)(2,1)}, bf16[128,1024]{1,0:T(8,128)(2,1)S(1)}, u32[]{:S(2)}) copy-start(bf16[128,1024]{1,0:T(8,128)(2,1)S(1)} %mul.218) | copy-start | bytes 786436
  792.4 0.7 copy-start.27
  792.4 18.3 copy-start.14
  810.9 5.5 copy-start.17
  810.9 5.5 copy-start.20
Sparse Core Ops, SparseCore 0:
  9.7 131.7 all-gather.14
  146.4 74.8 all-gather.16
  223.0 48.7 all-gather.18
  273.2 168.5 all-gather.20
  443.3 173.6 all-gather.22
  677.2 107.8 reduce-scatter.5
  788.0 643.6 reduce-scatter.9
  1434.8 665.5 reduce-scatter.11
  2103.5 668.1 reduce-scatter.13
  2774.6 658.3 reduce-scatter.7
where the time goes:
time: 3440 us
  waiting for transfers between devices  3020 us (88%)
  blocking collectives  241 us (7%)
  matrix products  91.1 us (3%)
  local copies, waits for them, and re-layouts  46.9 us (1%)
    reduce_scatter x1, waiting for transfers between devices, shards(): lax.psum_scatter(grad_down_w, ('ctx', 'shard'), scatter_dimension=0, tile...  671 us
    reduce_scatter x1, waiting for transfers between devices, shards(): lax.psum_scatter(grad_up_w, ('ctx', 'shard'), scatter_dimension=0, tiled=...  669 us
    reduce_scatter x1, waiting for transfers between devices, shards(): lax.psum_scatter(grad_qkv_w, ('ctx', 'shard'), scatter_dimension=0, tiled...  661 us
    reduce_scatter x1, waiting for transfers between devices, shards(): lax.psum_scatter(grad_out_w, ('ctx', 'shard'), scatter_dimension=0, tiled...  540 us
    all_gather x1, waiting for transfers between devices, shards(): lax.all_gather(w_fc2, 'shard', axis=0, tiled=True)  170 us
    all_gather x1, waiting for transfers between devices, shards(): lax.all_gather(w_fc1, 'shard', axis=0, tiled=True)  168 us
    reduce_scatter x1, waiting for transfers between devices, shards(): lax.psum_scatter(jnp.concatenate([grad_key_part.reshape(slot_rows * lax.a...  76.1 us
  transfers between devices with their start and end apart: 10, of which 9 were waited for; matrix products, arithmetic and copies ran while one was open for 3% of the time, Pallas kernels for 0%

commit v1 on v0

v1 whole, which is shorter than its diff:
```python
import jax
import jax.numpy as jnp
from jax import lax
from jax.experimental import pallas as pl
from jax.experimental.pallas import tpu as pltpu
from jax.sharding import PartitionSpec as P

HEADS = 16
HEAD_DIM = 64
MESH = pl.DeviceIdType.MESH
ANY = pl.ANY
VMEM = pltpu.VMEM
F32 = jnp.float32
BF16 = jnp.bfloat16

eps_norm = 1e-05
negative = -1e30


def place():
    c, s = lax.axis_index("ctx"), lax.axis_index("shard")
    return c, s, lax.rem(c, 2), s // 2, lax.rem(s, 2)


def sibling(c):
    return c + 1 - 2 * lax.rem(c, 2)


def send(src, dst, sems, idx, device):
    copy = pltpu.make_async_remote_copy(
        src_ref=src,
        dst_ref=dst,
        send_sem=sems[0].at[idx],
        recv_sem=sems[1].at[idx],
        device_id=device,
        device_id_type=MESH,
    )
    copy.start()
    return copy


def arrived(dst, sems, idx, c, s):
    pltpu.make_async_remote_copy(
        src_ref=dst,
        dst_ref=dst,
        send_sem=sems[0].at[idx],
        recv_sem=sems[1].at[idx],
        device_id=(c, s),
        device_id_type=MESH,
    ).wait_recv()


def greet(devices):
    barrier = pltpu.get_barrier_semaphore()
    for device in devices:
        pl.semaphore_signal(barrier, inc=1, device_id=device, device_id_type=MESH)
    pl.semaphore_wait(barrier, len(devices))


def sem_pair(count):
    return [pltpu.SemaphoreType.DMA((count,)), pltpu.SemaphoreType.DMA((count,))]


def comm_call(kernel, name, cid, outs, sems, ins, spaces=None, out_spaces=None, scratch=()):
    scratches = list(scratch)
    for count in sems:
        scratches += sem_pair(count)
    return pl.pallas_call(
        kernel,
        name=name,
        out_shape=[jax.ShapeDtypeStruct(shape, dtype) for shape, dtype in outs],
        in_specs=[pl.BlockSpec(memory_space=space) for space in (spaces or [ANY] * len(ins))],
        out_specs=[
            pl.BlockSpec(memory_space=space) for space in (out_spaces or [ANY] * len(outs))
        ],
        scratch_shapes=scratches + [pltpu.SemaphoreType.DMA((8,))],
        compiler_params=pltpu.CompilerParams(
            collective_id=cid, has_side_effects=True, vmem_limit_bytes=56 << 20
        ),
    )(*ins)


def half_rows(core, rows):
    return pl.ds(pl.multiple_of(core * rows, rows), rows)


def gather_first(tok, wq, small, tok_all, wq_all, small_all, a0, a1, b0, b1, d0, d1, e0, e1, local):
    c, s, core, x, yl = place()
    sib = (sibling(c), s)
    greet([(c, lax.rem(s + k, 8)) for k in range(1, 8)] + [sib])
    rows = half_rows(core, 64)
    out = []
    for k in range(1, 8):
        peer = lax.rem(s + k, 8)
        out.append(send(small, small_all.at[s], (a0, a1), k - 1, (c, peer)))
    for k in range(1, 8):
        peer = lax.rem(s + k, 8)
        out.append(
            send(wq.at[peer // 2, rows], wq_all.at[s, rows], (b0, b1), k - 1, (c, peer))
        )
    for k in range(1, 4):
        peer = lax.rem(x + k, 4)
        out.append(send(tok, tok_all.at[x], (d0, d1), k - 1, (c, 2 * peer + yl)))
    own = [
        pltpu.make_async_copy(tok, tok_all.at[x], local.at[0]),
        pltpu.make_async_copy(wq.at[x], wq_all.at[s], local.at[1]),
        pltpu.make_async_copy(small, small_all.at[s], local.at[2]),
    ]
    for copy in own:
        copy.start()
    for k in range(1, 8):
        origin = lax.rem(s - k + 8, 8)
        block = wq_all.at[origin, rows]
        arrived(block, (b0, b1), k - 1, c, s)
        out.append(send(block, block, (e0, e1), k - 1, sib))
    other = half_rows(1 - core, 64)
    for k in range(1, 8):
        origin = lax.rem(s - k + 8, 8)
        arrived(wq_all.at[origin, other], (e0, e1), k - 1, c, s)
        arrived(small_all.at[origin], (a0, a1), k - 1, c, s)
    for k in range(1, 4):
        arrived(tok_all.at[lax.rem(x - k + 4, 4)], (d0, d1), k - 1, c, s)
    for copy in out:
        copy.wait_send()
    for copy in own:
        copy.wait()


def gather_rest(
    qkv, wo, wf1, wf2, cot,
    parts, wo_all, wf1_all, wf2_all, cot_all,
    a0, a1, b0, b1, d0, d1, e0, e1, f0, f1, g0, g1, h0, h1, i0, i1, local,
):
    c, s, core, x, yl = place()
    sib = (sibling(c), s)
    mate = (c, s + 1 - 2 * yl)
    greet(
        [(lax.rem(c + k, 16), s) for k in range(1, 16)]
        + [(c, lax.rem(s + k, 8)) for k in range(1, 8)]
    )
    out = []
    for k in range(1, 16):
        peer = lax.rem(c + k, 16)
        cols = pl.ds(pl.multiple_of(lax.rem(peer, 2) * 384, 128), 384)
        out.append(send(qkv.at[peer // 2, :, cols], parts.at[c], (a0, a1), k - 1, (peer, s)))
    rows = half_rows(core, 64)
    rows2 = half_rows(core, 256)
    for k in range(1, 8):
        peer = lax.rem(s + k, 8)
        out.append(send(wo.at[rows], wo_all.at[s, rows], (b0, b1), k - 1, (c, peer)))
        cols = pl.ds(pl.multiple_of(peer // 2 * 1024, 128), 1024)
        out.append(send(wf1.at[rows, cols], wf1_all.at[s, rows], (d0, d1), k - 1, (c, peer)))
    out.append(send(wf2.at[rows2], wf2_all.at[yl, rows2], (e0, e1), 0, mate))
    for k in range(1, 4):
        peer = lax.rem(x + k, 4)
        out.append(send(cot, cot_all.at[x], (f0, f1), k - 1, (c, 2 * peer + yl)))
    mine = pl.ds(pl.multiple_of(core * 384, 128), 384)
    quarter = pl.ds(pl.multiple_of(x * 1024, 128), 1024)
    own = [
        pltpu.make_async_copy(qkv.at[c // 2, :, mine], parts.at[c], local.at[0]),
        pltpu.make_async_copy(wo, wo_all.at[s], local.at[1]),
        pltpu.make_async_copy(wf1.at[:, quarter], wf1_all.at[s], local.at[2]),
        pltpu.make_async_copy(wf2, wf2_all.at[yl], local.at[3]),
        pltpu.make_async_copy(cot, cot_all.at[x], local.at[4]),
    ]
    for copy in own:
        copy.start()
    for k in range(1, 8):
        origin = lax.rem(s - k + 8, 8)
        for whole, near, far in ((wo_all, (b0, b1), (g0, g1)), (wf1_all, (d0, d1), (h0, h1))):
            block = whole.at[origin, rows]
            arrived(block, near, k - 1, c, s)
            out.append(send(block, block, far, k - 1, sib))
    block = wf2_all.at[1 - yl, rows2]
    arrived(block, (e0, e1), 0, c, s)
    out.append(send(block, block, (i0, i1), 0, sib))
    other = half_rows(1 - core, 64)
    for k in range(1, 8):
        origin = lax.rem(s - k + 8, 8)
        arrived(wo_all.at[origin, other], (g0, g1), k - 1, c, s)
        arrived(wf1_all.at[origin, other], (h0, h1), k - 1, c, s)
    arrived(wf2_all.at[1 - yl, half_rows(1 - core, 256)], (i0, i1), 0, c, s)
    for k in range(1, 16):
        arrived(parts.at[lax.rem(c - k + 16, 16)], (a0, a1), k - 1, c, s)
    for k in range(1, 4):
        arrived(cot_all.at[lax.rem(x - k + 4, 4)], (f0, f1), k - 1, c, s)
    for copy in out:
        copy.wait_send()
    for copy in own:
        copy.wait()


def head_columns(x, core):
    return pl.ds(pl.multiple_of(x * 256 + core * 128, 128), 128)


def mix_back(mixed, rows_out, a0, a1, local):
    c, s, core, x, yl = place()
    z, yh = c // 4, lax.rem(c // 2, 2)
    barrier = pltpu.get_barrier_semaphore()
    at_home = z == x
    for k in range(16):
        xo = k // 4
        co = x * 4 + k % 4
        so = 2 * xo + yl

        @pl.when(jnp.logical_not((co == c) & (so == s)))
        def _():
            pl.semaphore_signal(barrier, inc=1, device_id=(co, so), device_id_type=MESH)

    pl.semaphore_wait(barrier, 16 - at_home.astype(jnp.int32))
    cols = head_columns(x, core)
    target = 2 * z + yl

    def copy_to(k):
        peer = lax.rem(c + k, 16)
        return pltpu.make_async_remote_copy(
            src_ref=mixed.at[peer],
            dst_ref=rows_out.at[yh, :, cols],
            send_sem=a0.at[k],
            recv_sem=a1.at[x * 4 + yh * 2 + core],
            device_id=(peer, target),
            device_id_type=MESH,
        )

    for k in range(1, 16):
        copy_to(k).start()

    @pl.when(at_home)
    def _():
        copy = pltpu.make_async_copy(mixed.at[c], rows_out.at[yh, :, cols], local.at[0])
        copy.start()
        copy.wait()

    @pl.when(jnp.logical_not(at_home))
    def _():
        copy_to(0).start()

    for k in range(16):
        xo, yo, ko = k // 4, (k // 2) % 2, k % 2
        mine = at_home & (xo == x) & (yo == yh) & (ko == core)

        @pl.when(jnp.logical_not(mine))
        def _():
            arrived(rows_out.at[yo, :, pl.ds(xo * 256 + ko * 128, 128)], (a0, a1), k, c, s)

    for k in range(1, 16):
        copy_to(k).wait_send()

    @pl.when(jnp.logical_not(at_home))
    def _():
        copy_to(0).wait_send()


def mix_forth(rows_in, parts, a0, a1, local):
    c, s, core, x, yl = place()
    z, yh = c // 4, lax.rem(c // 2, 2)
    barrier = pltpu.get_barrier_semaphore()
    at_home = z == x
    source = 2 * z + yl
    for k in range(1, 16):
        pl.semaphore_signal(
            barrier, inc=1, device_id=(lax.rem(c + k, 16), source), device_id_type=MESH
        )

    @pl.when(jnp.logical_not(at_home))
    def _():
        pl.semaphore_signal(barrier, inc=1, device_id=(c, source), device_id_type=MESH)

    pl.semaphore_wait(barrier, 16 - at_home.astype(jnp.int32))

    def copy_to(k):
        xo, yo, ko = k // 4, (k // 2) % 2, k % 2
        return pltpu.make_async_remote_copy(
            src_ref=rows_in.at[yo, :, pl.ds(xo * 256 + ko * 128, 128)],
            dst_ref=parts.at[c],
            send_sem=a0.at[k],
            recv_sem=a1.at[c],
            device_id=(x * 4 + yo * 2 + ko, 2 * xo + yl),
            device_id_type=MESH,
        )

    for k in range(16):
        xo, yo, ko = k // 4, (k // 2) % 2, k % 2
        mine = at_home & (xo == x) & (yo == yh) & (ko == core)

        @pl.when(jnp.logical_not(mine))
        def _():
            copy_to(k).start()

    @pl.when(at_home)
    def _():
        copy = pltpu.make_async_copy(
            rows_in.at[yh, :, head_columns(x, core)], parts.at[c], local.at[0]
        )
        copy.start()
        copy.wait()

    for k in range(1, 16):
        origin = lax.rem(c + k, 16)
        arrived(parts.at[origin], (a0, a1), origin, c, s)

    @pl.when(jnp.logical_not(at_home))
    def _():
        arrived(parts.at[c], (a0, a1), c, c, s)

    for k in range(16):
        xo, yo, ko = k // 4, (k // 2) % 2, k % 2
        mine = at_home & (xo == x) & (yo == yh) & (ko == core)

        @pl.when(jnp.logical_not(mine))
        def _():
            copy_to(k).wait_send()


def gather_x(mine, whole, a0, a1, local):
    c, s, core, x, yl = place()
    greet([(c, 2 * lax.rem(x + k, 4) + yl) for k in range(1, 4)])
    out = []
    for k in range(1, 4):
        peer = lax.rem(x + k, 4)
        out.append(send(mine, whole.at[x], (a0, a1), k - 1, (c, 2 * peer + yl)))
    own = pltpu.make_async_copy(mine, whole.at[x], local.at[0])
    own.start()
    for k in range(1, 4):
        arrived(whole.at[lax.rem(x - k + 4, 4)], (a0, a1), k - 1, c, s)
    for copy in out:
        copy.wait_send()
    own.wait()


def scatter_x(part_one, part_two, got_one, got_two, a0, a1, b0, b1, local):
    c, s, core, x, yl = place()
    greet([(c, 2 * lax.rem(x + k, 4) + yl) for k in range(1, 4)])
    out = []
    for part, got, sems in ((part_one, got_one, (a0, a1)), (part_two, got_two, (b0, b1))):
        for k in range(1, 4):
            peer = lax.rem(x + k, 4)
            out.append(send(part.at[peer], got.at[k - 1], sems, k - 1, (c, 2 * peer + yl)))
    for got, sems in ((got_one, (a0, a1)), (got_two, (b0, b1))):
        for k in range(1, 4):
            arrived(got.at[k - 1], sems, k - 1, c, s)
    for copy in out:
        copy.wait_send()


def heads_back(parts, whole, a0, a1, local):
    c, s, core, x, yl = place()
    greet([(lax.rem(c + k, 16), s) for k in range(1, 16)])
    cols = pl.ds(pl.multiple_of(core * 384, 128), 384)
    out = []
    for k in range(1, 16):
        peer = lax.rem(c + k, 16)
        out.append(send(parts.at[peer], whole.at[c // 2, :, cols], (a0, a1), k - 1, (peer, s)))
    own = pltpu.make_async_copy(parts.at[c], whole.at[c // 2, :, cols], local.at[0])
    own.start()
    for k in range(1, 16):
        origin = lax.rem(c - k + 16, 16)
        place_of = pl.ds(pl.multiple_of(lax.rem(origin, 2) * 384, 128), 384)
        arrived(whole.at[origin // 2, :, place_of], (a0, a1), k - 1, c, s)
    for copy in out:
        copy.wait_send()
    own.wait()


def sum_ctx(
    part, g_qkv, g_out, g_one, g_two, vec,
    got_part, s_qkv, s_out, s_one, s_two, s_vec,
    n_qkv, n_out, n_one, n_two, t_qkv, t_out, t_one, t_two, t_vec,
    p0, p1, a0, a1, b0, b1, v0, v1, local,
):
    c, s, core, x, yl = place()
    sib = (sibling(c), s)
    chip = c // 2
    greet(
        [(lax.rem(c + k, 16), s) for k in range(1, 16)]
        + [(c, 2 * lax.rem(x + k, 4) + yl) for k in range(1, 4)]
    )
    out = []
    for k in range(1, 4):
        peer = lax.rem(x + k, 4)
        out.append(send(part.at[peer], got_part.at[k - 1], (p0, p1), k - 1, (c, 2 * peer + yl)))
    for k in range(1, 16):
        peer = lax.rem(c + k, 16)
        out.append(send(vec.at[peer], t_vec.at[k - 1], (v0, v1), k - 1, (peer, s)))
    grads = (
        (g_two, n_two, t_two, s_two),
        (g_one, n_one, t_one, s_one),
        (g_out, n_out, t_out, s_out),
        (g_qkv, n_qkv, t_qkv, s_qkv),
    )
    for i, (g, near, far, total) in enumerate(grads):
        out.append(send(g.at[:, 1 - core], near, (a0, a1), i, sib))
    for i, (g, near, far, total) in enumerate(grads):
        arrived(near, (a0, a1), i, c, s)

        def add(j, _):
            near[j] = (near[j].astype(F32) + g[j, core].astype(F32)).astype(BF16)
            return 0

        lax.fori_loop(0, 8, add, 0)
        for k in range(1, 8):
            peer = lax.rem(chip + k, 8)
            out.append(
                send(near.at[peer], far.at[k - 1], (b0, b1), 7 * i + k - 1, (2 * peer + core, s))
            )
    for k in range(1, 16):
        arrived(t_vec.at[k - 1], (v0, v1), k - 1, c, s)
    s_vec[...] = vec[c] + jnp.sum(t_vec[...], axis=0)
    for i, (g, near, far, total) in enumerate(grads):
        for k in range(1, 8):
            arrived(far.at[k - 1], (b0, b1), 7 * i + k - 1, c, s)

        def add_rows(j, _):
            rows = pl.ds(pl.multiple_of(j * 16, 16), 16)
            acc = near[chip, rows].astype(F32)
            for k in range(7):
                acc = acc + far[k, rows].astype(F32)
            total[rows] = acc
            return 0

        lax.fori_loop(0, 4, add_rows, 0)
    for k in range(1, 4):
        arrived(got_part.at[k - 1], (p0, p1), k - 1, c, s)
    for copy in out:
        copy.wait_send()


def to_owners(
    s_qkv, s_out, s_one, s_two, s_vec,
    r_qkv, r_out, r_one, r_two, r_vec,
    a0, a1, b0, b1, d0, d1, e0, e1, f0, f1, local,
):
    c, s, core, x, yl = place()
    barrier = pltpu.get_barrier_semaphore()
    low = lax.rem(c, 4)
    to_c, to_x = 4 * x + c // 4, low
    from_c, from_x = 4 * low + x, c // 4
    stays = (to_c == c) & (to_x == x)
    for k in range(1, 8):
        pl.semaphore_signal(
            barrier, inc=1, device_id=(c, lax.rem(s + k, 8)), device_id_type=MESH
        )
    for y in range(2):

        @pl.when(jnp.logical_not(stays & (yl == y)))
        def _():
            pl.semaphore_signal(
                barrier, inc=1, device_id=(from_c, 2 * from_x + y), device_id_type=MESH
            )

    pl.semaphore_wait(barrier, 9 - stays.astype(jnp.int32))
    out = []

    def two_to(y):
        return pltpu.make_async_remote_copy(
            src_ref=s_two.at[y],
            dst_ref=r_two.at[yl],
            send_sem=e0.at[y],
            recv_sem=e1.at[yl],
            device_id=(to_c, 2 * to_x + y),
            device_id_type=MESH,
        )

    for y in range(2):

        @pl.when(jnp.logical_not(stays & (yl == y)))
        def _():
            two_to(y).start()

    @pl.when(stays)
    def _():
        copy = pltpu.make_async_copy(s_two.at[yl], r_two.at[yl], local.at[0])
        copy.start()
        copy.wait()

    triples = ((s_qkv, r_qkv, (a0, a1)), (s_out, r_out, (b0, b1)), (s_one, r_one, (d0, d1)))
    for k in range(1, 8):
        peer = lax.rem(s + k, 8)
        rows = pl.ds(pl.multiple_of(peer * 8, 8), 8)
        for src, dst, sems in triples:
            out.append(send(src.at[rows], dst.at[s], sems, k - 1, (c, peer)))
        out.append(send(s_vec, r_vec.at[s], (f0, f1), k - 1, (c, peer)))
    own_rows = pl.ds(pl.multiple_of(s * 8, 8), 8)
    own = [
        pltpu.make_async_copy(src.at[own_rows], dst.at[s], local.at[1 + i])
        for i, (src, dst, _) in enumerate(triples)
    ] + [pltpu.make_async_copy(s_vec, r_vec.at[s], local.at[4])]
    for copy in own:
        copy.start()
    for k in range(1, 8):
        origin = lax.rem(s - k + 8, 8)
        for _, dst, sems in triples:
            arrived(dst.at[origin], sems, k - 1, c, s)
        arrived(r_vec.at[origin], (f0, f1), k - 1, c, s)
    for y in range(2):

        @pl.when(jnp.logical_not(stays & (yl == y)))
        def _():
            arrived(r_two.at[y], (e0, e1), y, c, s)

    for copy in out:
        copy.wait_send()
    for y in range(2):

        @pl.when(jnp.logical_not(stays & (yl == y)))
        def _():
            two_to(y).wait_send()

    for copy in own:
        copy.wait()


def exact_gelu(inputs):
    return jax.nn.gelu(inputs, approximate=False)


def norm_parts(inputs):
    centre = inputs - jnp.mean(inputs, axis=-1, keepdims=True)
    spread = jnp.mean(centre * centre, axis=-1, keepdims=True)
    inverse = lax.rsqrt(spread + eps_norm)
    return (centre * inverse, inverse)


def norm_back(grad_normed, normed, inverse, gain):
    scaled = grad_normed * gain
    centred = scaled - jnp.mean(scaled, axis=-1, keepdims=True)
    return inverse * (centred - normed * jnp.mean(scaled * normed, axis=-1, keepdims=True))


def dot(left, right):
    return jnp.dot(left, right, preferred_element_type=F32)


def dot_rows(left, right):
    return jnp.einsum("rd,re->de", left, right, preferred_element_type=F32)


def dot_back(left, right):
    return jnp.einsum("re,de->rd", left, right, preferred_element_type=F32)


def shards(
    tokens,
    lengths,
    block_pairs,
    ln1_gain,
    ln1_bias,
    w_qkv,
    query_bias,
    value_bias,
    w_out,
    out_bias,
    ln2_gain,
    ln2_bias,
    w_fc1,
    fc1_bias,
    w_fc2,
    fc2_bias,
    out_cotangent,
):
    c, s = lax.axis_index("ctx"), lax.axis_index("shard")
    core, x, yl = c % 2, s // 2, s % 2
    scale = HEAD_DIM ** (-0.5)
    tok = tokens.reshape(128, 1024)
    cot = out_cotangent.reshape(128, 1024)

    row = jnp.arange(64)
    blocks = jnp.where(row[None, :] < 32, block_pairs[:, None], 31 - block_pairs[:, None])
    places = blocks * 32 + (row % 32)[None, :]
    my_places = lax.dynamic_index_in_dim(places, c, 0, keepdims=False)
    places = places.reshape(1024)

    vectors = [
        p.astype(F32).reshape(-1, 128)
        for p in (
            ln1_gain, ln1_bias, query_bias, value_bias, out_bias, ln2_gain, ln2_bias, fc2_bias, fc1_bias,
        )
    ]
    last = jnp.zeros((4, 128), F32).at[0, :2].set(lengths.astype(F32))
    small = jnp.concatenate(vectors + [last], axis=0)
    wq = w_qkv.reshape(128, 3, 4, 2, 128).transpose(2, 0, 3, 1, 4).reshape(4, 128, 768)
    tok_all, wq_all, small_all = comm_call(
        gather_first,
        "gather_first",
        0,
        [((4, 128, 1024), BF16), ((8, 128, 768), BF16), ((8, 16, 128), F32)],
        [7, 7, 3, 7],
        (tok, wq, small),
    )
    gain_one, bias_one, bias_q, bias_v, bias_out, gain_two, bias_two, bias_down = [
        small_all[:, i].reshape(1024) for i in range(8)
    ]
    bias_up = lax.dynamic_slice_in_dim(small_all[:, 8:12].reshape(4096), x * 1024, 1024)
    len_all = small_all[:, 12, :2].astype(jnp.int32)
    len_x = len_all.reshape(4, 2, 2)
    len_x = jnp.where(yl == 0, len_x[:, 0], len_x[:, 1]).reshape(8)
    my_len = lax.dynamic_index_in_dim(len_x, c // 2, 0, keepdims=False)
    w_q = wq_all.reshape(1024, 768)

    rows_all = tok_all.reshape(512, 1024).astype(F32)
    normed_all, _ = norm_parts(rows_all)
    attn_in = (normed_all * gain_one + bias_one).astype(BF16)
    bq = lax.dynamic_slice_in_dim(bias_q, x * 256, 256).reshape(2, 1, 128)
    bv = lax.dynamic_slice_in_dim(bias_v, x * 256, 256).reshape(2, 1, 128)
    bias768 = jnp.concatenate([bq, jnp.zeros_like(bq), bv], axis=1).reshape(768)
    qkv = (dot(attn_in, w_q) + bias768).astype(BF16).reshape(8, 64, 768)

    parts, wo_all, wf1_all, wf2_all, cot_all = comm_call(
        gather_rest,
        "gather_rest",
        1,
        [
            ((16, 64, 384), BF16),
            ((8, 128, 1024), BF16),
            ((8, 128, 1024), BF16),
            ((2, 512, 1024), BF16),
            ((4, 128, 1024), BF16),
        ],
        [15, 7, 7, 1, 3, 7, 7, 1],
        (qkv, w_out, w_fc1, w_fc2, cot),
    )
    w_o = wo_all.reshape(1024, 1024)
    w_up = wf1_all.reshape(1024, 1024)
    w_down = wf2_all.reshape(1024, 1024)

    parts = parts.reshape(1024, 3, 2, 64)
    q, k, v = parts[:, 0], parts[:, 1], parts[:, 2]
    allowed = (places[None, :] < my_len) & (places[None, :] <= places[:, None])

    def scores_of():
        raw = jnp.einsum("qhd,khd->hqk", q, k, preferred_element_type=F32) * scale
        return jnp.where(allowed[None], raw, negative)

    scores = scores_of()
    row_max = jnp.max(scores, axis=-1, keepdims=True)
    powers = jnp.exp(scores - row_max)
    total = jnp.sum(powers, axis=-1, keepdims=True)
    probs_first = (powers / total).astype(BF16)
    log_total = row_max + jnp.log(total)
    mixed = jnp.einsum("hqk,khd->qhd", probs_first, v, preferred_element_type=F32)
    mixed = mixed.reshape(16, 64, 128).astype(BF16)
    (mix_rows,) = comm_call(mix_back, "mix_back", 2, [((2, 64, 1024), BF16)], [16], (mixed,))
    mix_rows = mix_rows.reshape(128, 1024)

    residual = tok.astype(F32)
    hidden = residual + (dot(mix_rows, w_o) + bias_out)
    normed_two, inverse_two = norm_parts(hidden)
    mlp_in = (normed_two * gain_two + bias_two).astype(BF16)
    (mlp_all,) = comm_call(gather_x, "gather_x", 3, [((4, 128, 1024), BF16)], [3], (mlp_in,))
    mlp_all = mlp_all.reshape(512, 1024)

    pre_act = dot(mlp_all, w_up) + bias_up
    activated, gelu_pull = jax.vjp(exact_gelu, pre_act)
    act_low = activated.astype(BF16)
    mlp_part = dot(act_low, w_down)
    valid_all = (my_places[None, :] < len_x[:, None]).astype(F32).reshape(512, 1)
    g_all = cot_all.reshape(512, 1024).astype(F32) * valid_all
    g_low = g_all.astype(BF16)
    grad_act = dot_back(g_low, w_down)
    grad_pre = gelu_pull(grad_act)[0]
    grad_up_b = jnp.sum(grad_pre, axis=0)
    grad_pre_low = grad_pre.astype(BF16)
    gm_part = dot_back(grad_pre_low, w_up)
    g_two = dot_rows(act_low, g_low).astype(BF16)
    g_one = dot_rows(mlp_all, grad_pre_low).astype(BF16)
    gm_part = gm_part.reshape(4, 128, 1024)
    mlp_part = mlp_part.reshape(4, 128, 1024)
    got_gm, got_out = comm_call(
        scatter_x,
        "scatter_x",
        4,
        [((3, 128, 1024), BF16)] * 2,
        [3, 3],
        (gm_part.astype(BF16), mlp_part.astype(BF16)),
    )

    def own_block(blocks4):
        return lax.dynamic_index_in_dim(blocks4, x, 0, keepdims=False)

    grad_mlp_in = own_block(gm_part) + jnp.sum(got_gm.astype(F32), axis=0)
    mlp_out = own_block(mlp_part) + jnp.sum(got_out.astype(F32), axis=0) + bias_down
    row_valid = own_block(valid_all.reshape(4, 128, 1))
    layer_out = (row_valid * (hidden + mlp_out)).astype(BF16).reshape(tokens.shape)
    grad_out = cot.astype(F32) * row_valid
    grad_down_b = jnp.sum(grad_out, axis=0)
    grad_gain_two = jnp.sum(grad_mlp_in * normed_two, axis=0)
    grad_bias_two = jnp.sum(grad_mlp_in, axis=0)
    grad_hidden = grad_out + norm_back(grad_mlp_in, normed_two, inverse_two, gain_two)
    hidden_low = grad_hidden.astype(BF16)
    grad_out_b = jnp.sum(grad_hidden, axis=0)
    grad_mixed = dot_back(hidden_low, w_o).astype(BF16).reshape(2, 64, 1024)
    g_out = dot_rows(mix_rows, hidden_low).astype(BF16)
    (gm,) = comm_call(mix_forth, "mix_forth", 5, [((16, 64, 128), BF16)], [16], (grad_mixed,))

    gm = gm.reshape(1024, 2, 64)
    probs = jnp.exp(scores_of() - log_total)
    probs_low = probs.astype(BF16)
    grad_probs = jnp.einsum("qhd,khd->hqk", gm, v, preferred_element_type=F32)
    delta = jnp.sum(probs * grad_probs, axis=-1, keepdims=True)
    grad_scores = (probs * (grad_probs - delta)).astype(BF16)
    gq = jnp.einsum("hqk,khd->qhd", grad_scores, k, preferred_element_type=F32) * scale
    gk = jnp.einsum("hqk,qhd->khd", grad_scores, q, preferred_element_type=F32) * scale
    gv = jnp.einsum("hqk,qhd->khd", probs_low, gm, preferred_element_type=F32)
    gq, gk, gv = (g.reshape(1024, 128) for g in (gq, gk, gv))
    grad_bq, grad_bv = jnp.sum(gq, axis=0), jnp.sum(gv, axis=0)
    g_parts = jnp.concatenate([gq, gk, gv], axis=1).astype(BF16).reshape(16, 64, 384)
    (g_qkv,) = comm_call(heads_back, "heads_back", 6, [((8, 64, 768), BF16)], [15], (g_parts,))
    g_qkv = g_qkv.reshape(512, 768)
    ga_part = dot_back(g_qkv, w_q).reshape(4, 128, 1024)
    gw_qkv = dot_rows(attn_in, g_qkv).astype(BF16)

    zeros = jnp.zeros((1024,), F32)
    head_at = x * 256 + core * 128
    full = [
        grad_out_b,
        grad_gain_two,
        grad_bias_two,
        grad_down_b,
        lax.dynamic_update_slice(zeros, grad_bq, (head_at,)),
        lax.dynamic_update_slice(zeros, grad_bv, (head_at,)),
    ]
    up_full = lax.dynamic_update_slice(jnp.zeros((4096,), F32), grad_up_b, (x * 1024,))

    def chunks(vectors, tail):
        body = jnp.stack([v.reshape(16, 64) for v in vectors], axis=1).reshape(16, -1, 128)
        if tail is not None:
            body = jnp.concatenate([body, tail.reshape(16, 2, 128)], axis=1)
        return jnp.pad(body, ((0, 0), (0, 8 - body.shape[1]), (0, 0)))

    vec = chunks(full, up_full)
    sums = comm_call(
        sum_ctx,
        "sum_ctx",
        7,
        [
            ((3, 128, 1024), BF16),
            ((64, 768), F32),
            ((64, 1024), F32),
            ((64, 1024), F32),
            ((64, 1024), F32),
            ((8, 128), F32),
        ],
        [3, 4, 28, 15],
        (
            ga_part.astype(BF16),
            gw_qkv.reshape(8, 2, 64, 768),
            g_out.reshape(8, 2, 64, 1024),
            g_one.reshape(8, 2, 64, 1024),
            g_two.reshape(8, 2, 64, 1024),
            vec,
        ),
        spaces=[ANY, VMEM, VMEM, VMEM, VMEM, VMEM],
        out_spaces=[ANY, VMEM, VMEM, VMEM, VMEM, VMEM],
        scratch=[
            pltpu.VMEM((8, 64, 768), BF16),
            pltpu.VMEM((8, 64, 1024), BF16),
            pltpu.VMEM((8, 64, 1024), BF16),
            pltpu.VMEM((8, 64, 1024), BF16),
            pltpu.VMEM((7, 64, 768), BF16),
            pltpu.VMEM((7, 64, 1024), BF16),
            pltpu.VMEM((7, 64, 1024), BF16),
            pltpu.VMEM((7, 64, 1024), BF16),
            pltpu.VMEM((15, 8, 128), F32),
        ],
    )
    got_ga, s_qkv, s_out, s_one, s_two, s_vec = sums
    normed_one, inverse_one = norm_parts(residual)
    grad_attn_in = own_block(ga_part) + jnp.sum(got_ga.astype(F32), axis=0)
    input_grad = (
        (grad_hidden + norm_back(grad_attn_in, normed_one, inverse_one, gain_one))
        .astype(BF16)
        .reshape(tokens.shape)
    )
    vec_one = chunks([jnp.sum(grad_attn_in * normed_one, axis=0), jnp.sum(grad_attn_in, axis=0)], None)
    (s_vec_one,) = comm_call(
        sum_vec,
        "sum_vec",
        8,
        [((8, 128), F32)],
        [15],
        (vec_one,),
        spaces=[VMEM],
        out_spaces=[VMEM],
        scratch=[pltpu.VMEM((15, 8, 128), F32)],
    )
    s_vec = jnp.concatenate([s_vec, s_vec_one], axis=0)
    r_qkv, r_out, r_one, r_two, r_vec = comm_call(
        to_owners,
        "to_owners",
        9,
        [
            ((8, 8, 768), F32),
            ((8, 8, 1024), F32),
            ((8, 8, 1024), F32),
            ((2, 32, 1024), F32),
            ((8, 16, 128), F32),
        ],
        [7, 7, 7, 2, 7],
        (s_qkv, s_out, s_one, s_two.reshape(2, 32, 1024), s_vec),
    )
    by_x = jnp.sum(r_qkv.reshape(4, 2, 8, 2, 3, 128), axis=1)
    grad_w_qkv = by_x.transpose(1, 3, 0, 2, 4).reshape(8, 3072)
    grad_w_out = jnp.sum(r_out, axis=0)
    one_x = jnp.sum(r_one.reshape(4, 2, 8, 1024), axis=1)
    grad_w_fc1 = one_x.transpose(1, 0, 2).reshape(8, 4096)
    grad_w_fc2 = jnp.sum(r_two, axis=0)
    vec_sum = jnp.sum(r_vec, axis=0)
    small_sums = vec_sum[:3].reshape(6, 8, 8)
    small_sums = lax.dynamic_index_in_dim(small_sums, s, 1, keepdims=False)
    up_sum = lax.dynamic_index_in_dim(vec_sum[3:5].reshape(8, 32), s, 0, keepdims=False)
    one_sums = vec_sum[8:9].reshape(2, 8, 8)
    one_sums = lax.dynamic_index_in_dim(one_sums, s, 1, keepdims=False)
    return (
        layer_out,
        input_grad,
        one_sums[0],
        one_sums[1],
        grad_w_qkv,
        small_sums[4],
        small_sums[5],
        grad_w_out,
        small_sums[0],
        small_sums[1],
        small_sums[2],
        grad_w_fc1,
        up_sum,
        grad_w_fc2,
        small_sums[3],
    )


def sum_vec(vec, total, got, a0, a1, local):
    c, s, core, x, yl = place()
    greet([(lax.rem(c + k, 16), s) for k in range(1, 16)])
    out = []
    for k in range(1, 16):
        peer = lax.rem(c + k, 16)
        out.append(send(vec.at[peer], got.at[k - 1], (a0, a1), k - 1, (peer, s)))
    for k in range(1, 16):
        arrived(got.at[k - 1], (a0, a1), k - 1, c, s)
    total[...] = vec[c] + jnp.sum(got[...], axis=0)
    for copy in out:
        copy.wait_send()


def solution(mesh):
    one, both = P("shard"), P(("ctx", "shard"))
    rows, both_rows = P("shard", None), P(("ctx", "shard"), None)
    whole = P("ctx", "shard", None, None)
    return jax.shard_map(
        shards,
        mesh=mesh,
        in_specs=(
            whole, one, P(), one, one, rows, one, one, rows, one, one, one, rows, one, rows, one, whole,
        ),
        out_specs=(
            whole, whole, both, both, both_rows, both, both, both_rows, both, both, both,
            both_rows, both, both_rows, both,
        ),
        check_vma=False,
    )
```

time: 3440 us -> 407 us (0.12)
  waiting for transfers between devices: 3020 us -> 0 us
  Pallas kernels: 0 us -> 270 us
  blocking collectives: 241 us -> 0 us
    reduce_scatter x5 -> x0, waiting for transfers between devices: 2620 us -> none  [the longest x1 671 us: shards(): lax.psum_scatter(grad_down_w, ('ctx', 'shard'), scatter_dimension=0, tile...]
    all_gather x5 -> x0, waiting for transfers between devices: 399 us -> none  [the longest x1 170 us: shards(): lax.all_gather(w_fc2, 'shard', axis=0, tiled=True)]
    pallas_call x0 -> x10, Pallas kernels: none -> 270 us  [comm_call(): pl.pallas_call(kernel, name=name, out_shape=[jax.ShapeDtypeStruct(shape,...]
    all_gather x9 -> x0, blocking collectives: 178 us -> none  [the longest x1 24 us: shards(): lax.all_gather(value_bias, 'shard', axis=0, tiled=True)]
    unnamed x1 -> x0, blocking collectives: 63.6 us -> none
  transfers between devices with their start and end apart: 10 -> 0, of which waited for: 9 -> 0; matrix products, arithmetic and copies ran while one was open for 3% -> 0% of each run, Pallas kernels for 0% -> 0%
where the time goes in v1:
time: 407 us; the launch traced here: 402 us
  Pallas kernels  270 us (66%)
  matrix products  58.4 us (14%)
  other arithmetic  41.2 us (10%)
  local copies, waits for them, and re-layouts  30.8 us (8%)
    pallas_call x10, Pallas kernels, comm_call(): pl.pallas_call(kernel, name=name, out_shape=[jax.ShapeDtypeStruct(shape,...  270 us
    dot_general x4, matrix products, dot_back(): return jnp.einsum('re,de->rd', left, right, preferred_element_type=F32)  15.9 us
    dot_general x4, matrix products, dot_rows(): return jnp.einsum('rd,re->de', left, right, preferred_element_type=F32)  10.9 us
    dot_general x4, matrix products, dot(): return jnp.dot(left, right, preferred_element_type=F32)  10.1 us
    unnamed x68, local copies, waits for them, and re-layouts  9.43 us

profile of v1, /device:TPU:0, one launch (start us, length us, event | category | flops | bytes accessed | tf_op | source)
XLA Modules:
  0.0 402.0 jit_solution(14104752082918883092)
XLA Ops:
  4.7 1.2 concatenate.25.small
  5.9 1.5 copy.112
  7.5 1.2 copy.114.wq
  8.7 27.0 %gather_first.1 = (bf16[4,128,1024]{2,1,0:T(8,128)(2,1)}, bf16[8,128,768]{2,1,0:T(8,128)(2,1)}, f32[8,16,128]{2,1,0:T(8,128)}) custom-call(bf16[128,1024]{1,0:T(8,128)(2,1)} %bitcast.203, bf16[4,128,768]{2,1,0:T(8,128)(2,1)} %copy.114.wq, f32[16,128]{1,0:T(8,128)} %concatenate.25.small), custom_call_target="tpu_custom_call" | custom-call | tf_op jit(solution)/shard_map/gather_first/pallas_call | solution.py:68
  35.8 1.3 fusion.71
  37.4 1.6 convert_reduce_fusion
  38.9 1.6 fusion.8
  41.1 1.9 add_convert_fusion
  42.9 65.6 %gather_rest.1 = (bf16[16,64,384]{2,1,0:T(8,128)(2,1)}, bf16[8,128,1024]{2,1,0:T(8,128)(2,1)}, bf16[8,128,1024]{2,1,0:T(8,128)(2,1)}, bf16[2,512,1024]{2,1,0:T(8,128)(2,1)}, bf16[4,128,1024]{2,1,0:T(8,128)(2,1)}) custom-call(bf16[8,64,768]{2,1,0:T(8,128)(2,1)} %bitcast.227, bf16[128,1024]{1,0:T(8,128)(2,1)} %wo.1, bf16[128,4096]{1,0:T(8,128)(2,1)} %wf1.1, ...), custom_call_target="tpu_custom_call" | custom-call | tf_op jit(solution)/shard_map/gather_rest/pallas_call | solution.py:68
  108.6 3.5 reshape.728
  112.1 1.1 fusion.68
  114.0 0.8 slice_convert_fusion
  116.6 1.0 compare_and_fusion
  117.6 1.9 fusion.73
  119.6 1.2 fusion
  120.7 2.1 copy-done
  123.2 0.7 copy-done.14
  123.9 5.0 %fusion.27 = bf16[1024,2,64]{0,2,1:T(8,128)(2,1)S(1)} fusion(f32[2,1024,1024]{1,2,0:T(8,128)} %copy-done, f32[2,1024]{1,0:T(2,128)S(1)} %fusion, f32[2,1024]{1,0:T(2,128)S(1)} %get-tuple-element.110, bf16[1024,1,2,64]{0,3,2,1:T(8,128)(2,1)S(1)} %copy.139), kind=kOutput, calls=%fused_computation.58 | convolution fusion | flops 274857984 | bytes 8929280 | tf_op jit(solution)/shard_map/hqk,khd->qhd/dot_general | solution.py:641
  129.3 1.1 copy.120.mixed
  130.5 19.1 %mix_back.1 = bf16[2,64,1024]{2,1,0:T(8,128)(2,1)} custom-call(bf16[16,64,128]{2,1,0:T(8,128)(2,1)} %copy.120.mixed), custom_call_target="tpu_custom_call" | custom-call | tf_op jit(solution)/shard_map/mix_back/pallas_call | solution.py:68
  149.6 1.5 fusion.74
  151.3 0.9 add_convert_fusion.1.mine
  152.2 15.9 %gather_x.1 = bf16[4,128,1024]{2,1,0:T(8,128)(2,1)} custom-call(bf16[128,1024]{1,0:T(8,128)(2,1)} %add_convert_fusion.1.mine), custom_call_target="tpu_custom_call" | custom-call | tf_op jit(solution)/shard_map/gather_x/pallas_call | solution.py:68
  168.1 3.8 fusion.78
  172.2 2.5 multiply_convert_fusion.1
  174.7 0.8 slice.115
  175.4 8.6 %fusion.66 = (f32[1024]{0:T(1024)S(1)}, bf16[512,1024]{1,0:T(8,128)(2,1)S(1)}, f32[512,1024]{1,0:T(8,128)S(1)}) fusion(f32[512,1024]{1,0:T(8,128)} %fusion.78, f32[1024]{0:T(1024)S(1)} %dynamic_slice.48, bf16[512,1024]{1,0:T(8,128)(2,1)} %bitcast.222, bf16[1024,1024]{1,0:T(8,128)(2,1)} %bitcast.258), kind=kOutput, calls=%fused_computation.162 | convolution fusion | flops 1112538112 | bytes 8396800 | tf_op jit(solution)/shard_map/re,de->rd/dot_general | solution.py:540
  184.6 1.8 copy-done.28
  186.4 2.9 fusion.76
  189.3 3.1 fusion.75
  192.4 26.4 %scatter_x.1 = (bf16[3,128,1024]{2,1,0:T(8,128)(2,1)}, bf16[3,128,1024]{2,1,0:T(8,128)(2,1)}) custom-call(bf16[4,128,1024]{2,1,0:T(8,128)(2,1)} %get-tuple-element.114.part_one, bf16[4,128,1024]{2,1,0:T(8,128)(2,1)} %get-tuple-element.116.part_two), custom_call_target="tpu_custom_call" | custom-call | tf_op jit(solution)/shard_map/scatter_x/pallas_call | solution.py:68
  218.8 1.3 convert_reduce_fusion.2
  220.1 2.1 multiply_reduce_fusion.2
  222.3 0.9 convert_reduce_fusion.3
  223.3 2.5 fusion.65
  225.7 1.5 convolution_convert_fusion.4
  227.3 11.4 %mix_forth.1 = bf16[16,64,128]{2,1,0:T(8,128)(2,1)} custom-call(bf16[2,64,1024]{2,1,0:T(8,128)(2,1)} %bitcast.226), custom_call_target="tpu_custom_call" | custom-call | tf_op jit(solution)/shard_map/mix_forth/pallas_call | solution.py:68
  238.7 1.2 reshape.729
  240.3 5.2 %multiply_reduce_fusion = (f32[2,1024]{1,0:T(2,128)S(1)}, f32[2,1024,1024]{1,2,0:T(8,128)S(1)}) fusion(f32[2,1024,1024]{1,2,0:T(8,128)} %copy-done, f32[2,1024]{1,0:T(2,128)S(1)} %log_add_fusion, bf16[1024,2,64]{0,2,1:T(8,128)(2,1)S(1)} %copy.136, bf16[1024,1,2,64]{0,3,2,1:T(8,128)(2,1)S(1)} %copy-done.15), kind=kOutput, calls=%fused_computation.1 | convolution fusion | flops 274724864 | bytes 17317888 | tf_op jit(solution)/shard_map/qhd,khd->hqk/dot_general | solution.py:699
  245.5 4.7 %multiply_convert_fusion = bf16[2,1024,1024]{1,2,0:T(8,128)(2,1)S(1)} fusion(f32[2,1024,1024]{1,2,0:T(8,128)S(1)} %get-tuple-element.120, f32[2,1024,1024]{1,2,0:T(8,128)} %copy-done, f32[2,1024]{1,0:T(2,128)S(1)} %get-tuple-element.119, f32[2,1024]{1,0:T(2,128)S(1)} %log_add_fusion), kind=kLoop, calls=%fused_computation | loop fusion | flops 8388608 | bytes 20987904 | tf_op jit(solution)/shard_map/convert_element_type | solution.py:701
  250.2 0.9 fusion.70
  251.1 1.0 copy-done.1
  252.5 4.9 %fusion.69 = (f32[2,64]{1,0:T(2,128)S(1)}, bf16[1024,2,64]{0,2,1:T(8,128)(2,1)S(1)}) fusion(bf16[1024,2,64]{0,2,1:T(8,128)(2,1)S(1)} %copy.136, f32[2,1024,1024]{1,2,0:T(8,128)} %copy-done, f32[2,1024]{1,0:T(2,128)S(1)} %log_add_fusion), kind=kOutput, calls=%fused_computation.164 | convolution fusion | flops 272891776 | bytes 8921600 | tf_op jit(solution)/shard_map/hqk,qhd->khd/dot_general | solution.py:704
  259.6 2.1 convolution_convert_fusion.2
  262.5 3.6 fusion.26
  267.8 1.0 pad_maximum_fusion.parts
  268.8 15.6 %heads_back.1 = bf16[8,64,768]{2,1,0:T(8,128)(2,1)} custom-call(bf16[16,64,384]{2,1,0:T(8,128)(2,1)} %pad_maximum_fusion.parts), custom_call_target="tpu_custom_call" | custom-call | tf_op jit(solution)/shard_map/heads_back/pallas_call | solution.py:68
  284.4 3.5 convolution_convert_fusion.3
  287.9 2.6 convolution_convert_fusion.1
  290.6 2.7 fusion.77
  293.7 0.8 copy-done.22
  294.5 2.6 convolution_convert_fusion
  297.1 57.9 %sum_ctx.1 = (bf16[3,128,1024]{2,1,0:T(8,128)(2,1)}, f32[64,768]{1,0:T(8,128)}, f32[64,1024]{1,0:T(8,128)}, f32[64,1024]{1,0:T(8,128)}, f32[64,1024]{1,0:T(8,128)}, /*index=5*/f32[8,128]{1,0:T(8,128)}) custom-call(bf16[4,128,1024]{2,1,0:T(8,128)(2,1)} %get-tuple-element.122.part, bf16[8,2,64,768]{3,2,1,0:T(8,128)(2,1)} %bitcast.219, ...), custom_call_target="tpu_custom_call" | custom-call | tf_op jit(solution)/shard_map/sum_ctx/pallas_call | solution.py:68
  355.0 1.3 convert_reduce_fusion.1
  356.9 1.4 fusion.37
  359.2 10.9 %sum_vec.1 = f32[8,128]{1,0:T(8,128)} custom-call(f32[16,8,128]{2,1,0:T(8,128)} %pad.14.vec), custom_call_target="tpu_custom_call" | custom-call | tf_op jit(solution)/shard_map/sum_vec/pallas_call | solution.py:68
  370.1 1.3 pad_maximum_fusion.2.s_vec
  371.4 20.3 %to_owners.1 = (f32[8,8,768]{2,1,0:T(8,128)}, f32[8,8,1024]{2,1,0:T(8,128)}, f32[8,8,1024]{2,1,0:T(8,128)}, f32[2,32,1024]{2,1,0:T(8,128)}, f32[8,16,128]{2,1,0:T(8,128)}) custom-call(f32[64,768]{1,0:T(8,128)} %get-tuple-element.59.s_qkv, f32[64,1024]{1,0:T(8,128)} %get-tuple-element.60.s_out, f32[64,1024]{1,0:T(8,128)} %get-tuple-element.61.s_one, ...), custom_call_target="tpu_custom_call" | custom-call | tf_op jit(solution)/shard_map/to_owners/pallas_call | solution.py:68
  391.6 1.0 reduce_sum.292
  393.2 1.6 reduce_sum.295
  394.9 1.6 bitcast_reduce_fusion
  396.5 0.9 reduce_sum.291
  398.0 1.6 reduce_sum.293
  400.8 1.0 fusion.36
  (159 shorter events, 19.1 us)
Async XLA Ops:
  35.8 4.8 %copy-start.2 = (bf16[4,128,1024]{2,1,0:T(8,128)(2,1)S(1)}, bf16[4,128,1024]{2,1,0:T(8,128)(2,1)}, u32[]{:S(2)}) copy-start(bf16[4,128,1024]{2,1,0:T(8,128)(2,1)} %get-tuple-element.49) | copy-start | bytes 3145732
  37.4 3.7 copy-start.12
  41.0 1.9 copy-start.19
  112.0 3.8 copy-start.25
  113.5 6.0 %copy-start.16 = (bf16[1024,1,2,64]{0,3,2,1:T(8,128)(2,1)}, bf16[1024,1,2,64]{0,3,2,1:T(8,128)(2,1)S(1)}, u32[]{:S(2)}) copy-start(bf16[1024,1,2,64]{0,3,2,1:T(8,128)(2,1)S(1)} %copy.140) | copy-start | bytes 786436
  114.0 5.6 %copy-start.8 = (bf16[1024,1,2,64]{0,3,2,1:T(8,128)(2,1)}, bf16[1024,1,2,64]{0,3,2,1:T(8,128)(2,1)S(1)}, u32[]{:S(2)}) copy-start(bf16[1024,1,2,64]{0,3,2,1:T(8,128)(2,1)S(1)} %copy.141) | copy-start | bytes 786436
  119.6 3.2 copy-start
  123.2 0.7 copy-start.14
  123.9 25.7 %copy-start.4 = (bf16[8,128,1024]{2,1,0:T(8,128)(2,1)S(1)}, bf16[8,128,1024]{2,1,0:T(8,128)(2,1)}, u32[]{:S(2)}) copy-start(bf16[8,128,1024]{2,1,0:T(8,128)(2,1)} %get-tuple-element.52) | copy-start | bytes 6291460
  129.0 20.6 %copy-start.3 = (bf16[1,2,64,1024]{3,2,1,0:T(8,128)(2,1)S(1)}, bf16[1,2,64,1024]{3,2,1,0:T(8,128)(2,1)}, u32[]{:S(2)}) copy-start(bf16[1,2,64,1024]{3,2,1,0:T(8,128)(2,1)} %param.19) | copy-start | bytes 786436
  151.1 17.0 %copy-start.26 = (bf16[8,128,1024]{2,1,0:T(8,128)(2,1)S(1)}, bf16[8,128,1024]{2,1,0:T(8,128)(2,1)}, u32[]{:S(2)}) copy-start(bf16[8,128,1024]{2,1,0:T(8,128)(2,1)} %get-tuple-element.53) | copy-start | bytes 6291460
  175.4 8.6 %copy-start.11 = (f32[512,1024]{1,0:T(8,128)S(1)}, f32[512,1024]{1,0:T(8,128)}, u32[]{:S(2)}) copy-start(f32[512,1024]{1,0:T(8,128)} %fusion.78) | copy-start | bytes 6291460
  184.1 5.3 %copy-start.29 = (bf16[512,1024]{1,0:T(8,128)(2,1)}, bf16[512,1024]{1,0:T(8,128)(2,1)S(1)}, u32[]{:S(2)}) copy-start(bf16[512,1024]{1,0:T(8,128)(2,1)S(1)} %get-tuple-element.81) | copy-start | bytes 3145732
  184.1 2.3 copy-start.28
  184.6 4.7 %copy-start.21 = (bf16[512,1024]{1,0:T(8,128)(2,1)}, bf16[512,1024]{1,0:T(8,128)(2,1)S(1)}, u32[]{:S(2)}) copy-start(bf16[512,1024]{1,0:T(8,128)(2,1)S(1)} %multiply_convert_fusion.2) | copy-start | bytes 3145732
  186.4 2.9 copy-start.27
  220.1 2.1 copy-start.23
  225.7 14.5 %copy-start.15 = (bf16[1024,1,2,64]{0,3,2,1:T(8,128)(2,1)S(1)}, bf16[1024,1,2,64]{0,3,2,1:T(8,128)(2,1)}, u32[]{:S(2)}) copy-start(bf16[1024,1,2,64]{0,3,2,1:T(8,128)(2,1)} %copy-done.14) | copy-start | bytes 786436
  245.5 4.7 %copy-start.9 = (bf16[1024,1,2,64]{0,3,2,1:T(8,128)(2,1)S(1)}, bf16[1024,1,2,64]{0,3,2,1:T(8,128)(2,1)}, u32[]{:S(2)}) copy-start(bf16[1024,1,2,64]{0,3,2,1:T(8,128)(2,1)} %copy-done.8) | copy-start | bytes 786436
  250.2 2.0 copy-start.1
  252.5 5.6 %copy-start.7 = (bf16[1,2,64,1024]{3,2,1,0:T(8,128)(2,1)S(1)}, bf16[1,2,64,1024]{3,2,1,0:T(8,128)(2,1)}, u32[]{:S(2)}) copy-start(bf16[1,2,64,1024]{3,2,1,0:T(8,128)(2,1)} %param.35) | copy-start | bytes 786436
  252.5 7.1 %copy-start.10 = (bf16[2,64,1024]{2,1,0:T(8,128)(2,1)S(1)}, bf16[2,64,1024]{2,1,0:T(8,128)(2,1)}, u32[]{:S(2)}) copy-start(bf16[2,64,1024]{2,1,0:T(8,128)(2,1)} %mix_back.1) | copy-start | bytes 786436
  259.6 2.9 copy-start.17
  267.3 17.1 %copy-start.20 = (bf16[4,128,1024]{2,1,0:T(8,128)(2,1)S(1)}, bf16[4,128,1024]{2,1,0:T(8,128)(2,1)}, u32[]{:S(2)}) copy-start(bf16[4,128,1024]{2,1,0:T(8,128)(2,1)} %copy-done.19) | copy-start | bytes 3145732
  284.4 3.6 copy-start.18
  284.4 3.5 copy-start.30
  287.9 2.6 copy-start.6
  287.9 2.6 copy-start.13
  290.6 2.8 copy-start.5
  293.3 1.2 copy-start.22
  355.0 15.0 %copy-start.24 = (f32[8,128]{1,0:T(8,128)S(1)}, f32[8,128]{1,0:T(8,128)}, u32[]{:S(2)}) copy-start(f32[8,128]{1,0:T(8,128)} %get-tuple-element.63) | copy-start | bytes 12292

commit v2 on v1

--- a/solution.py
+++ b/solution.py
@@ -1,3 +1,5 @@
+from types import SimpleNamespace
+
 import jax
 import jax.numpy as jnp
 from jax import lax
@@ -84,172 +86,432 @@
     return pl.ds(pl.multiple_of(core * rows, rows), rows)
 
 
-def gather_first(tok, wq, small, tok_all, wq_all, small_all, a0, a1, b0, b1, d0, d1, e0, e1, local):
+def head_columns(x, core):
+    return pl.ds(pl.multiple_of(x * 256 + core * 128, 128), 128)
+
+
+def pick(value, unit):
+    return pl.multiple_of(value * unit, unit)
+
+
+def loop(count, body, first=0):
+    def step(k, carry):
+        body(k)
+        return carry
+
+    lax.fori_loop(first, count, step, 0)
+
+
+def remote(src, dst, send_sem, recv_sem, device):
+    return pltpu.make_async_remote_copy(
+        src_ref=src,
+        dst_ref=dst,
+        send_sem=send_sem,
+        recv_sem=recv_sem,
+        device_id=device,
+        device_id_type=MESH,
+    )
+
+
+def not_when(condition, body):
+    pl.when(jnp.logical_not(condition))(body)
+
+
+def norm_rows(rows):
+    centre = rows - jnp.mean(rows, axis=-1, keepdims=True)
+    inverse = lax.rsqrt(jnp.mean(centre * centre, axis=-1, keepdims=True) + eps_norm)
+    return centre * inverse, inverse
+
+
+def dot_nt(left, right):
+    return lax.dot_general(left, right, (((1,), (1,)), ((), ())), preferred_element_type=F32)
+
+
+VECTORS = (
+    "ln1_gain", "ln1_bias", "query_bias", "value_bias", "out_bias", "ln2_gain", "ln2_bias", "fc2_bias",
+)
+
+FORWARD_IN = (
+    ("lengths", pltpu.SMEM),
+    ("block_pairs", pltpu.SMEM),
+    ("tok", VMEM),
+    *[(name, VMEM) for name in VECTORS],
+    ("fc1_bias", VMEM),
+    ("w_qkv", ANY),
+    ("w_out", ANY),
+    ("w_fc1", ANY),
+    ("w_fc2", ANY),
+    ("cot", ANY),
+)
+
+FORWARD_OUT = (
+    ("attn_all", VMEM, (4, 128, 1024), BF16),
+    ("wq_all", VMEM, (8, 128, 768), BF16),
+    ("wo_all", VMEM, (8, 128, 1024), BF16),
+    ("w1_all", ANY, (8, 128, 1024), BF16),
+    ("w2_all", ANY, (2, 512, 1024), BF16),
+    ("cot_all", ANY, (4, 128, 1024), BF16),
+    ("parts", VMEM, (16, 64, 384), BF16),
+    ("probs", VMEM, (2, 1024, 1024), BF16),
+    ("mix_t", VMEM, (128, 1024), F32),
+    ("mix_rows", VMEM, (2, 64, 1024), BF16),
+    ("hidden", VMEM, (128, 1024), F32),
+    ("mlp_in", VMEM, (128, 1024), BF16),
+    ("small_all", VMEM, (16, 1024), F32),
+    ("places", VMEM, (1024, 128), F32),
+)
+
+FORWARD_SCRATCH = (
+    ("small", pltpu.VMEM((16, 128), F32)),
+    ("tok_all", pltpu.VMEM((4, 128, 1024), BF16)),
+    ("qkv", pltpu.VMEM((16, 64, 384), BF16)),
+    ("mixed", pltpu.VMEM((16, 64, 128), BF16)),
+    *[
+        (name, pltpu.SemaphoreType.DMA((count,)))
+        for name, count in (
+            ("local", 16), ("sm_s", 8), ("sm_r", 8), ("wq_s", 24), ("wq_r", 24), ("tk_s", 4), ("tk_r", 4),
+            ("wz_s", 4), ("wz_r", 4), ("wc_s", 4), ("wc_r", 4), ("qa_s", 16), ("qa_r", 16),
+            ("mx_s", 16), ("mx_r", 16), ("wo_s", 8), ("wo_r", 8), ("woc_s", 8), ("woc_r", 8),
+            ("w1_s", 8), ("w1_r", 8), ("w1c_s", 8), ("w1c_r", 8), ("w2_s", 2), ("w2_r", 2), ("w2c_s", 2),
+            ("w2c_r", 2), ("ct_s", 4), ("ct_r", 4),
+        )
+    ],
+)
+
+
+def forward_kernel(*refs):
+    names = [n[0] for n in FORWARD_IN] + [n[0] for n in FORWARD_OUT] + [n[0] for n in FORWARD_SCRATCH]
+    r = SimpleNamespace(**dict(zip(names, refs, strict=True)))
     c, s, core, x, yl = place()
+    z, yh = c // 4, lax.rem(c // 2, 2)
     sib = (sibling(c), s)
-    greet([(c, lax.rem(s + k, 8)) for k in range(1, 8)] + [sib])
-    rows = half_rows(core, 64)
-    out = []
-    for k in range(1, 8):
+    at_home = z == x
+
+    barrier = pltpu.get_barrier_semaphore()
+
+    def hail(device):
+        pl.semaphore_signal(barrier, inc=1, device_id=device, device_id_type=MESH)
+
+    loop(8, lambda k: hail((c, lax.rem(s + k, 8))), 1)
+    loop(16, lambda k: hail((lax.rem(c + k, 16), s)), 1)
+
+    def hail_source(k):
+        co, so = x * 4 + lax.rem(k, 4), 2 * (k // 4) + yl
+        not_when((co == c) & (so == s), lambda: hail((co, so)))
+
+    loop(16, hail_source)
+
+    for i, name in enumerate(VECTORS):
+        r.small[i : i + 1, :] = getattr(r, name)[...].astype(F32)
+    r.small[8:12, :] = r.fc1_bias[...].astype(F32)
+    lane = lax.broadcasted_iota(jnp.int32, (4, 128), 1)
+    r.small[12:16, :] = jnp.where(
+        lane == 0, r.lengths[0].astype(F32), jnp.where(lane == 1, r.lengths[1].astype(F32), 0.0)
+    )
+    pl.semaphore_wait(barrier, 38 - at_home.astype(jnp.int32))
+
+    def await_block(dst, recv_sem):
+        remote(dst, dst, r.local.at[15], recv_sem, sib).wait_recv()
+
+    slice_rows = pl.ds(pick(z * 2 + core, 16), 16)
+    columns_of = lambda peer: pl.ds(pick(peer, 128), 128)
+
+    def small_to(k):
+        return remote(
+            r.small, r.small_all.at[:, columns_of(s)], r.sm_s.at[k], r.sm_r.at[k], (c, lax.rem(s + k, 8))
+        )
+
+    def wq_to(k, t):
         peer = lax.rem(s + k, 8)
-        out.append(send(small, small_all.at[s], (a0, a1), k - 1, (c, peer)))
-    for k in range(1, 8):
-        peer = lax.rem(s + k, 8)
-        out.append(
-            send(wq.at[peer // 2, rows], wq_all.at[s, rows], (b0, b1), k - 1, (c, peer))
-        )
-    for k in range(1, 4):
-        peer = lax.rem(x + k, 4)
-        out.append(send(tok, tok_all.at[x], (d0, d1), k - 1, (c, 2 * peer + yl)))
+        cols = pl.ds(pick(t * 4 + peer // 2, 256), 256)
+        return remote(
+            r.w_qkv.at[slice_rows, cols],
+            r.wq_all.at[s, slice_rows, t * 256 : t * 256 + 256],
+            r.wq_s.at[3 * k + t],
+            r.wq_r.at[3 * k + t],
+            (c, peer),
+        )
+
+    def tok_to(k):
+        peer = 2 * lax.rem(x + k, 4) + yl
+        return remote(r.tok, r.tok_all.at[x], r.tk_s.at[k], r.tk_r.at[k], (c, peer))
+
+    loop(8, lambda k: small_to(k).start(), 1)
+
+    def wq_start(k):
+        for t in range(3):
+            wq_to(k, t).start()
+
+    loop(8, wq_start, 1)
+    tok_to(1).start()
+    tok_to(3).start()
+    tok_to(2).start()
     own = [
-        pltpu.make_async_copy(tok, tok_all.at[x], local.at[0]),
-        pltpu.make_async_copy(wq.at[x], wq_all.at[s], local.at[1]),
-        pltpu.make_async_copy(small, small_all.at[s], local.at[2]),
+        pltpu.make_async_copy(
+            r.w_qkv.at[slice_rows, pl.ds(pick(t * 4 + x, 256), 256)],
+            r.wq_all.at[s, slice_rows, t * 256 : t * 256 + 256],
+            r.local.at[t],
+        )
+        for t in range(3)
     ]
     for copy in own:
         copy.start()
-    for k in range(1, 8):
-        origin = lax.rem(s - k + 8, 8)
-        block = wq_all.at[origin, rows]
-        arrived(block, (b0, b1), k - 1, c, s)
-        out.append(send(block, block, (e0, e1), k - 1, sib))
-    other = half_rows(1 - core, 64)
-    for k in range(1, 8):
-        origin = lax.rem(s - k + 8, 8)
-        arrived(wq_all.at[origin, other], (e0, e1), k - 1, c, s)
-        arrived(small_all.at[origin], (a0, a1), k - 1, c, s)
-    for k in range(1, 4):
-        arrived(tok_all.at[lax.rem(x - k + 4, 4)], (d0, d1), k - 1, c, s)
-    for copy in out:
-        copy.wait_send()
+    r.small_all[:, columns_of(s)] = r.small[...]
+    r.tok_all[x] = r.tok[...]
+
+    sub = lax.broadcasted_iota(jnp.int32, (64, 128), 0)
+
+    def set_places(k):
+        pair = r.block_pairs[k]
+        block = jnp.where(sub < 32, pair, 31 - pair)
+        r.places[pl.ds(pick(k, 64), 64), :] = (block * 32 + lax.rem(sub, 32)).astype(F32)
+
+    loop(16, set_places)
+
     for copy in own:
         copy.wait()
 
-
-def gather_rest(
-    qkv, wo, wf1, wf2, cot,
-    parts, wo_all, wf1_all, wf2_all, cot_all,
-    a0, a1, b0, b1, d0, d1, e0, e1, f0, f1, g0, g1, h0, h1, i0, i1, local,
-):
-    c, s, core, x, yl = place()
-    sib = (sibling(c), s)
-    mate = (c, s + 1 - 2 * yl)
-    greet(
-        [(lax.rem(c + k, 16), s) for k in range(1, 16)]
-        + [(c, lax.rem(s + k, 8)) for k in range(1, 8)]
-    )
-    out = []
-    for k in range(1, 16):
-        peer = lax.rem(c + k, 16)
-        cols = pl.ds(pl.multiple_of(lax.rem(peer, 2) * 384, 128), 384)
-        out.append(send(qkv.at[peer // 2, :, cols], parts.at[c], (a0, a1), k - 1, (peer, s)))
-    rows = half_rows(core, 64)
-    rows2 = half_rows(core, 256)
-    for k in range(1, 8):
+    def wq_arrived(k):
+        origin = lax.rem(s - k + 8, 8)
+        for t in range(3):
+            await_block(r.wq_all.at[origin, slice_rows, t * 256 : t * 256 + 256], r.wq_r.at[3 * k + t])
+
+    loop(8, wq_arrived, 1)
+
+    def slice_of(zp, core_of):
+        return r.wq_all.at[:, pl.ds(pick(zp * 2 + core_of, 16), 16)]
+
+    def wq_along(k):
+        block = slice_of(z, core)
+        return remote(block, block, r.wz_s.at[k], r.wz_r.at[k], (lax.rem(c + 4 * k, 16), s))
+
+    def wq_across(k):
+        block = slice_of(lax.rem(z - k + 4, 4), core)
+        return remote(block, block, r.wc_s.at[k], r.wc_r.at[k], sib)
+
+    wq_along(1).start()
+    wq_along(3).start()
+    wq_along(2).start()
+    wq_across(0).start()
+    loop(
+        8,
+        lambda k: await_block(r.small_all.at[:, columns_of(lax.rem(s - k + 8, 8))], r.sm_r.at[k]),
+        1,
+    )
+    for k in (1, 3, 2):
+        await_block(slice_of(lax.rem(z - k + 4, 4), core), r.wz_r.at[k])
+        wq_across(k).start()
+
+    half = lambda which, rows: pl.ds(pick(which, rows), rows)
+
+    def wo_to(k):
         peer = lax.rem(s + k, 8)
-        out.append(send(wo.at[rows], wo_all.at[s, rows], (b0, b1), k - 1, (c, peer)))
-        cols = pl.ds(pl.multiple_of(peer // 2 * 1024, 128), 1024)
-        out.append(send(wf1.at[rows, cols], wf1_all.at[s, rows], (d0, d1), k - 1, (c, peer)))
-    out.append(send(wf2.at[rows2], wf2_all.at[yl, rows2], (e0, e1), 0, mate))
-    for k in range(1, 4):
-        peer = lax.rem(x + k, 4)
-        out.append(send(cot, cot_all.at[x], (f0, f1), k - 1, (c, 2 * peer + yl)))
-    mine = pl.ds(pl.multiple_of(core * 384, 128), 384)
-    quarter = pl.ds(pl.multiple_of(x * 1024, 128), 1024)
+        return remote(
+            r.w_out.at[half(core, 64)], r.wo_all.at[s, half(core, 64)], r.wo_s.at[k], r.wo_r.at[k], (c, peer)
+        )
+
+    def cot_to(k):
+        peer = 2 * lax.rem(x + k, 4) + yl
+        return remote(r.cot, r.cot_all.at[x], r.ct_s.at[k], r.ct_r.at[k], (c, peer))
+
+    def w1_to(k):
+        peer = lax.rem(s + k, 8)
+        return remote(
+            r.w_fc1.at[half(core, 64), pl.ds(pick(peer // 2, 1024), 1024)],
+            r.w1_all.at[s, half(core, 64)],
+            r.w1_s.at[k],
+            r.w1_r.at[k],
+            (c, peer),
+        )
+
+    def w2_to():
+        mate = (c, s + 1 - 2 * yl)
+        rows = half(core, 256)
+        return remote(r.w_fc2.at[rows], r.w2_all.at[yl, rows], r.w2_s.at[0], r.w2_r.at[0], mate)
+
     own = [
-        pltpu.make_async_copy(qkv.at[c // 2, :, mine], parts.at[c], local.at[0]),
-        pltpu.make_async_copy(wo, wo_all.at[s], local.at[1]),
-        pltpu.make_async_copy(wf1.at[:, quarter], wf1_all.at[s], local.at[2]),
-        pltpu.make_async_copy(wf2, wf2_all.at[yl], local.at[3]),
-        pltpu.make_async_copy(cot, cot_all.at[x], local.at[4]),
+        pltpu.make_async_copy(r.w_out, r.wo_all.at[s], r.local.at[4]),
+        pltpu.make_async_copy(r.w_fc1.at[:, pl.ds(pick(x, 1024), 1024)], r.w1_all.at[s], r.local.at[5]),
+        pltpu.make_async_copy(r.w_fc2, r.w2_all.at[yl], r.local.at[6]),
+        pltpu.make_async_copy(r.cot, r.cot_all.at[x], r.local.at[7]),
     ]
+
+    gain_one, bias_one = r.small_all[0:1, :], r.small_all[1:2, :]
+    head_cols = pl.ds(pick(x, 256), 256)
+    bias_qkv = (r.small_all[2:3, head_cols], None, r.small_all[3:4, head_cols])
+
+    def parts_to(target):
+        return remote(
+            r.qkv.at[target], r.parts.at[c], r.qa_s.at[target], r.qa_r.at[c], (target, s)
+        )
+
+    def qkv_block(k):
+        hop = k + (k // 2) * (1 - 2 * lax.rem(k, 2))
+        origin = lax.rem(x - hop + 4, 4)
+
+        @pl.when(k > 0)
+        def _():
+            await_block(r.tok_all.at[origin], r.tk_r.at[hop])
+
+        normed, _ = norm_rows(r.tok_all[origin].astype(F32))
+        r.attn_all[origin] = (normed * gain_one + bias_one).astype(BF16)
+
+        @pl.when(k == 0)
+        def _():
+            for j in range(4):
+                await_block(slice_of(lax.rem(z - j + 4, 4), 1 - core), r.wc_r.at[j])
+
+        for t in range(3):
+            cols = slice(t * 256, t * 256 + 256)
+            acc = dot(r.attn_all[origin], r.wq_all[:, :, cols].reshape(1024, 256))
+            if bias_qkv[t] is not None:
+                acc = acc + bias_qkv[t]
+            acc = acc.astype(BF16)
+            for j in range(2):
+                for p in range(2):
+                    r.qkv[origin * 4 + j * 2 + p, :, t * 128 : t * 128 + 128] = acc[
+                        j * 64 : j * 64 + 64, p * 128 : p * 128 + 128
+                    ]
+
+        for j in range(4):
+            target = origin * 4 + j
+            not_when(target == c, lambda: parts_to(target).start())
+
+    loop(4, qkv_block)
+    loop(8, lambda k: wo_to(k).start(), 1)
+    for k in (1, 3, 2):
+        cot_to(k).start()
     for copy in own:
         copy.start()
-    for k in range(1, 8):
-        origin = lax.rem(s - k + 8, 8)
-        for whole, near, far in ((wo_all, (b0, b1), (g0, g1)), (wf1_all, (d0, d1), (h0, h1))):
-            block = whole.at[origin, rows]
-            arrived(block, near, k - 1, c, s)
-            out.append(send(block, block, far, k - 1, sib))
-    block = wf2_all.at[1 - yl, rows2]
-    arrived(block, (e0, e1), 0, c, s)
-    out.append(send(block, block, (i0, i1), 0, sib))
-    other = half_rows(1 - core, 64)
-    for k in range(1, 8):
-        origin = lax.rem(s - k + 8, 8)
-        arrived(wo_all.at[origin, other], (g0, g1), k - 1, c, s)
-        arrived(wf1_all.at[origin, other], (h0, h1), k - 1, c, s)
-    arrived(wf2_all.at[1 - yl, half_rows(1 - core, 256)], (i0, i1), 0, c, s)
-    for k in range(1, 16):
-        arrived(parts.at[lax.rem(c - k + 16, 16)], (a0, a1), k - 1, c, s)
-    for k in range(1, 4):
-        arrived(cot_all.at[lax.rem(x - k + 4, 4)], (f0, f1), k - 1, c, s)
-    for copy in out:
-        copy.wait_send()
-    for copy in own:
-        copy.wait()
-
-
-def head_columns(x, core):
-    return pl.ds(pl.multiple_of(x * 256 + core * 128, 128), 128)
-
-
-def mix_back(mixed, rows_out, a0, a1, local):
-    c, s, core, x, yl = place()
-    z, yh = c // 4, lax.rem(c // 2, 2)
-    barrier = pltpu.get_barrier_semaphore()
-    at_home = z == x
-    for k in range(16):
-        xo = k // 4
-        co = x * 4 + k % 4
-        so = 2 * xo + yl
-
-        @pl.when(jnp.logical_not((co == c) & (so == s)))
-        def _():
-            pl.semaphore_signal(barrier, inc=1, device_id=(co, so), device_id_type=MESH)
-
-    pl.semaphore_wait(barrier, 16 - at_home.astype(jnp.int32))
-    cols = head_columns(x, core)
-    target = 2 * z + yl
-
-    def copy_to(k):
+    r.parts[c] = r.qkv[c]
+    loop(16, lambda k: await_block(r.parts.at[lax.rem(c + k, 16)], r.qa_r.at[lax.rem(c + k, 16)]), 1)
+    w2_to().start()
+    loop(8, lambda k: w1_to(k).start(), 1)
+
+    slot_lane = lax.rem(c // 2, 2)
+    row = r.small_all[12:13, columns_of(2 * (c // 4) + yl)]
+    lane = lax.broadcasted_iota(jnp.int32, (1, 128), 1)
+    length = jnp.sum(jnp.where(lane == slot_lane, row, 0.0), axis=1, keepdims=True)
+    head_lane = lax.broadcasted_iota(jnp.int32, (1, 128), 1) // 64
+    value_t = r.parts[:, :, 256:384].reshape(1024, 128).T
+
+    def attend(i):
+        keys = r.parts[:, :, 128:256].reshape(1024, 128)
+        key_place = r.places[:, 0:1]
+        query_place = r.places[pl.ds(pick(i, 256), 256), :].T[0:1, :]
+        allowed = (key_place < length) & (key_place <= query_place)
+        queries = r.parts[pl.ds(i * 4, 4), :, 0:128].reshape(256, 128) * jnp.asarray(0.125, BF16)
+        cols = pl.ds(pick(i, 256), 256)
+        for h in range(2):
+            mine = jnp.where(head_lane == h, queries, jnp.zeros_like(queries))
+            scores = jnp.where(allowed, dot_nt(keys, mine), negative)
+            powers = jnp.exp(scores - jnp.max(scores, axis=0, keepdims=True))
+            low = (powers * (1.0 / jnp.sum(powers, axis=0, keepdims=True))).astype(BF16)
+            r.probs[h, :, cols] = low
+            r.mix_t[h * 64 : h * 64 + 64, cols] = dot(value_t[h * 64 : h * 64 + 64], low)
+
+    loop(4, attend)
+    r.mixed[...] = r.mix_t[...].T.astype(BF16).reshape(16, 64, 128)
+
+    def mix_to(k):
         peer = lax.rem(c + k, 16)
-        return pltpu.make_async_remote_copy(
-            src_ref=mixed.at[peer],
-            dst_ref=rows_out.at[yh, :, cols],
-            send_sem=a0.at[k],
-            recv_sem=a1.at[x * 4 + yh * 2 + core],
-            device_id=(peer, target),
-            device_id_type=MESH,
-        )
-
-    for k in range(1, 16):
-        copy_to(k).start()
+        return remote(
+            r.mixed.at[peer],
+            r.mix_rows.at[yh, :, head_columns(x, core)],
+            r.mx_s.at[k],
+            r.mx_r.at[x * 4 + yh * 2 + core],
+            (peer, 2 * z + yl),
+        )
+
+    loop(16, lambda k: mix_to(k).start(), 1)
+    not_when(at_home, lambda: mix_to(0).start())
 
     @pl.when(at_home)
     def _():
-        copy = pltpu.make_async_copy(mixed.at[c], rows_out.at[yh, :, cols], local.at[0])
-        copy.start()
+        r.mix_rows[yh, :, head_columns(x, core)] = r.mixed[c]
+
+    def across(whole, recv, send_next, recv_next, rows):
+        def body(k):
+            block = whole.at[lax.rem(s - k + 8, 8), half(core, rows)]
+            await_block(block, recv.at[k])
+            remote(block, block, send_next.at[k], recv_next.at[k], sib).start()
+
+        return body
+
+    loop(8, across(r.wo_all, r.wo_r, r.woc_s, r.woc_r, 64), 1)
+    loop(
+        8,
+        lambda k: await_block(r.wo_all.at[lax.rem(s - k + 8, 8), half(1 - core, 64)], r.woc_r.at[k]),
+        1,
+    )
+    own[0].wait()
+
+    def mix_arrived(k):
+        xo, yo, ko = k // 4, lax.rem(k // 2, 2), lax.rem(k, 2)
+        here = at_home & (xo == x) & (yo == yh) & (ko == core)
+        not_when(here, lambda: await_block(r.mix_rows.at[yo, :, head_columns(xo, ko)], r.mx_r.at[k]))
+
+    loop(16, mix_arrived)
+
+    mix = r.mix_rows[...].reshape(128, 1024)
+    hidden = r.tok[...].astype(F32) + (dot(mix, r.wo_all[...].reshape(1024, 1024)) + r.small_all[4:5, :])
+    r.hidden[...] = hidden
+    normed, _ = norm_rows(hidden)
+    r.mlp_in[...] = (normed * r.small_all[5:6, :] + r.small_all[6:7, :]).astype(BF16)
+
+    loop(8, across(r.w1_all, r.w1_r, r.w1c_s, r.w1c_r, 64), 1)
+    block = r.w2_all.at[1 - yl, half(core, 256)]
+    await_block(block, r.w2_r.at[0])
+    w2_across = remote(block, block, r.w2c_s.at[0], r.w2c_r.at[0], sib)
+    w2_across.start()
+    for k in range(1, 4):
+        await_block(r.cot_all.at[lax.rem(x - k + 4, 4)], r.ct_r.at[k])
+    loop(
+        8,
+        lambda k: await_block(r.w1_all.at[lax.rem(s - k + 8, 8), half(1 - core, 64)], r.w1c_r.at[k]),
+        1,
+    )
+    await_block(r.w2_all.at[1 - yl, half(1 - core, 256)], r.w2c_r.at[0])
+    for copy in own[1:]:
         copy.wait()
 
-    @pl.when(jnp.logical_not(at_home))
-    def _():
-        copy_to(0).start()
-
-    for k in range(16):
-        xo, yo, ko = k // 4, (k // 2) % 2, k % 2
-        mine = at_home & (xo == x) & (yo == yh) & (ko == core)
-
-        @pl.when(jnp.logical_not(mine))
-        def _():
-            arrived(rows_out.at[yo, :, pl.ds(xo * 256 + ko * 128, 128)], (a0, a1), k, c, s)
-
-    for k in range(1, 16):
-        copy_to(k).wait_send()
-
-    @pl.when(jnp.logical_not(at_home))
-    def _():
-        copy_to(0).wait_send()
+    def sent(k):
+        small_to(k).wait_send()
+        for t in range(3):
+            wq_to(k, t).wait_send()
+        wo_to(k).wait_send()
+        w1_to(k).wait_send()
+        for whole, sem in ((r.wo_all, r.woc_s), (r.w1_all, r.w1c_s)):
+            block = whole.at[lax.rem(s - k + 8, 8), half(core, 64)]
+            remote(block, block, sem.at[k], sem.at[k], sib).wait_send()
+
+    loop(8, sent, 1)
+    for k in range(1, 4):
+        tok_to(k).wait_send()
+        wq_along(k).wait_send()
+        cot_to(k).wait_send()
+    for k in range(4):
+        wq_across(k).wait_send()
+    w2_to().wait_send()
+    w2_across.wait_send()
+    loop(16, lambda k: not_when(k == c, lambda: parts_to(k).wait_send()))
+    loop(16, lambda k: mix_to(k).wait_send(), 1)
+    not_when(at_home, lambda: mix_to(0).wait_send())
+
+
+def named_call(kernel, name, cid, ins, outs, scratch, operands):
+    results = pl.pallas_call(
+        kernel,
+        name=name,
+        out_shape=[jax.ShapeDtypeStruct(shape, dtype) for _, _, shape, dtype in outs],
+        in_specs=[pl.BlockSpec(memory_space=space) for _, space in ins],
+        out_specs=[pl.BlockSpec(memory_space=space) for _, space, _, _ in outs],
+        scratch_shapes=[kind for _, kind in scratch],
+        compiler_params=pltpu.CompilerParams(
+            collective_id=cid, has_side_effects=True, vmem_limit_bytes=60 << 20
+        ),
+    )(*[operands[name] for name, _ in ins])
+    return SimpleNamespace(**dict(zip([o[0] for o in outs], results, strict=True)))
 
 
 def mix_forth(rows_in, parts, a0, a1, local):
@@ -565,88 +827,54 @@
     tok = tokens.reshape(128, 1024)
     cot = out_cotangent.reshape(128, 1024)
 
-    row = jnp.arange(64)
-    blocks = jnp.where(row[None, :] < 32, block_pairs[:, None], 31 - block_pairs[:, None])
-    places = blocks * 32 + (row % 32)[None, :]
-    my_places = lax.dynamic_index_in_dim(places, c, 0, keepdims=False)
-    places = places.reshape(1024)
-
-    vectors = [
-        p.astype(F32).reshape(-1, 128)
-        for p in (
-            ln1_gain, ln1_bias, query_bias, value_bias, out_bias, ln2_gain, ln2_bias, fc2_bias, fc1_bias,
-        )
-    ]
-    last = jnp.zeros((4, 128), F32).at[0, :2].set(lengths.astype(F32))
-    small = jnp.concatenate(vectors + [last], axis=0)
-    wq = w_qkv.reshape(128, 3, 4, 2, 128).transpose(2, 0, 3, 1, 4).reshape(4, 128, 768)
-    tok_all, wq_all, small_all = comm_call(
-        gather_first,
-        "gather_first",
+    f = named_call(
+        forward_kernel,
+        "forward",
         0,
-        [((4, 128, 1024), BF16), ((8, 128, 768), BF16), ((8, 16, 128), F32)],
-        [7, 7, 3, 7],
-        (tok, wq, small),
-    )
-    gain_one, bias_one, bias_q, bias_v, bias_out, gain_two, bias_two, bias_down = [
-        small_all[:, i].reshape(1024) for i in range(8)
-    ]
-    bias_up = lax.dynamic_slice_in_dim(small_all[:, 8:12].reshape(4096), x * 1024, 1024)
-    len_all = small_all[:, 12, :2].astype(jnp.int32)
-    len_x = len_all.reshape(4, 2, 2)
+        FORWARD_IN,
+        FORWARD_OUT,
+        FORWARD_SCRATCH,
+        dict(
+            lengths=lengths,
+            block_pairs=block_pairs,
+            tok=tok,
+            ln1_gain=ln1_gain.reshape(1, 128),
+            ln1_bias=ln1_bias.reshape(1, 128),
+            query_bias=query_bias.reshape(1, 128),
+            value_bias=value_bias.reshape(1, 128),
+            out_bias=out_bias.reshape(1, 128),
+            ln2_gain=ln2_gain.reshape(1, 128),
+            ln2_bias=ln2_bias.reshape(1, 128),
+            fc2_bias=fc2_bias.reshape(1, 128),
+            fc1_bias=fc1_bias.reshape(4, 128),
+            w_qkv=w_qkv,
+            w_out=w_out,
+            w_fc1=w_fc1,
+            w_fc2=w_fc2,
+            cot=cot,
+        ),
+    )
+    gain_one, gain_two, bias_down = f.small_all[0], f.small_all[5], f.small_all[7]
+    bias_up = lax.dynamic_slice_in_dim(
+        f.small_all[8:12].reshape(4, 8, 128).transpose(1, 0, 2).reshape(4096), x * 1024, 1024
+    )
+    len_x = f.small_all[12].reshape(4, 2, 128)[:, :, :2]
     len_x = jnp.where(yl == 0, len_x[:, 0], len_x[:, 1]).reshape(8)
-    my_len = lax.dynamic_index_in_dim(len_x, c // 2, 0, keepdims=False)
-    w_q = wq_all.reshape(1024, 768)
-
-    rows_all = tok_all.reshape(512, 1024).astype(F32)
-    normed_all, _ = norm_parts(rows_all)
-    attn_in = (normed_all * gain_one + bias_one).astype(BF16)
-    bq = lax.dynamic_slice_in_dim(bias_q, x * 256, 256).reshape(2, 1, 128)
-    bv = lax.dynamic_slice_in_dim(bias_v, x * 256, 256).reshape(2, 1, 128)
-    bias768 = jnp.concatenate([bq, jnp.zeros_like(bq), bv], axis=1).reshape(768)
-    qkv = (dot(attn_in, w_q) + bias768).astype(BF16).reshape(8, 64, 768)
-
-    parts, wo_all, wf1_all, wf2_all, cot_all = comm_call(
-        gather_rest,
-        "gather_rest",
-        1,
-        [
-            ((16, 64, 384), BF16),
-            ((8, 128, 1024), BF16),
-            ((8, 128, 1024), BF16),
-            ((2, 512, 1024), BF16),
-            ((4, 128, 1024), BF16),
-        ],
-        [15, 7, 7, 1, 3, 7, 7, 1],
-        (qkv, w_out, w_fc1, w_fc2, cot),
-    )
-    w_o = wo_all.reshape(1024, 1024)
-    w_up = wf1_all.reshape(1024, 1024)
-    w_down = wf2_all.reshape(1024, 1024)
-
-    parts = parts.reshape(1024, 3, 2, 64)
+    my_places = lax.dynamic_slice_in_dim(f.places[:, 0], c * 64, 64)
+    w_q = f.wq_all.reshape(1024, 768)
+    w_o = f.wo_all.reshape(1024, 1024)
+    w_up = f.w1_all.reshape(1024, 1024)
+    w_down = f.w2_all.reshape(1024, 1024)
+    attn_in = f.attn_all.reshape(512, 1024)
+    mix_rows = f.mix_rows.reshape(128, 1024)
+    cot_all = f.cot_all
+    parts = f.parts.reshape(1024, 3, 2, 64)
     q, k, v = parts[:, 0], parts[:, 1], parts[:, 2]
-    allowed = (places[None, :] < my_len) & (places[None, :] <= places[:, None])
-
-    def scores_of():
-        raw = jnp.einsum("qhd,khd->hqk", q, k, preferred_element_type=F32) * scale
-        return jnp.where(allowed[None], raw, negative)
-
-    scores = scores_of()
-    row_max = jnp.max(scores, axis=-1, keepdims=True)
-    powers = jnp.exp(scores - row_max)
-    total = jnp.sum(powers, axis=-1, keepdims=True)
-    probs_first = (powers / total).astype(BF16)
-    log_total = row_max + jnp.log(total)
-    mixed = jnp.einsum("hqk,khd->qhd", probs_first, v, preferred_element_type=F32)
-    mixed = mixed.reshape(16, 64, 128).astype(BF16)
-    (mix_rows,) = comm_call(mix_back, "mix_back", 2, [((2, 64, 1024), BF16)], [16], (mixed,))
-    mix_rows = mix_rows.reshape(128, 1024)
 
     residual = tok.astype(F32)
-    hidden = residual + (dot(mix_rows, w_o) + bias_out)
+    hidden = f.hidden
     normed_two, inverse_two = norm_parts(hidden)
-    mlp_in = (normed_two * gain_two + bias_two).astype(BF16)
+    mlp_in = f.mlp_in
     (mlp_all,) = comm_call(gather_x, "gather_x", 3, [((4, 128, 1024), BF16)], [3], (mlp_in,))
     mlp_all = mlp_all.reshape(512, 1024)
 
@@ -694,8 +922,8 @@
     (gm,) = comm_call(mix_forth, "mix_forth", 5, [((16, 64, 128), BF16)], [16], (grad_mixed,))
 
     gm = gm.reshape(1024, 2, 64)
-    probs = jnp.exp(scores_of() - log_total)
-    probs_low = probs.astype(BF16)
+    probs_low = jnp.swapaxes(f.probs, 1, 2)
+    probs = probs_low.astype(F32)
     grad_probs = jnp.einsum("qhd,khd->hqk", gm, v, preferred_element_type=F32)
     delta = jnp.sum(probs * grad_probs, axis=-1, keepdims=True)
     grad_scores = (probs * (grad_probs - delta)).astype(BF16)
@@ -706,7 +934,7 @@
     grad_bq, grad_bv = jnp.sum(gq, axis=0), jnp.sum(gv, axis=0)
     g_parts = jnp.concatenate([gq, gk, gv], axis=1).astype(BF16).reshape(16, 64, 384)
     (g_qkv,) = comm_call(heads_back, "heads_back", 6, [((8, 64, 768), BF16)], [15], (g_parts,))
-    g_qkv = g_qkv.reshape(512, 768)
+    g_qkv = g_qkv.reshape(512, 2, 3, 128).swapaxes(1, 2).reshape(512, 768)
     ga_part = dot_back(g_qkv, w_q).reshape(4, 128, 1024)
     gw_qkv = dot_rows(attn_in, g_qkv).astype(BF16)
 
@@ -799,8 +1027,8 @@
         [7, 7, 7, 2, 7],
         (s_qkv, s_out, s_one, s_two.reshape(2, 32, 1024), s_vec),
     )
-    by_x = jnp.sum(r_qkv.reshape(4, 2, 8, 2, 3, 128), axis=1)
-    grad_w_qkv = by_x.transpose(1, 3, 0, 2, 4).reshape(8, 3072)
+    by_x = jnp.sum(r_qkv.reshape(4, 2, 8, 3, 256), axis=1)
+    grad_w_qkv = by_x.transpose(1, 2, 0, 3).reshape(8, 3072)
     grad_w_out = jnp.sum(r_out, axis=0)
     one_x = jnp.sum(r_one.reshape(4, 2, 8, 1024), axis=1)
     grad_w_fc1 = one_x.transpose(1, 0, 2).reshape(8, 4096)

time: 407 us -> 354 us (0.87)
  Pallas kernels: 270 us -> 254 us
  other arithmetic: 41.2 us -> 25.5 us
  matrix products: 58.4 us -> 45.5 us
  local copies, waits for them, and re-layouts: 30.8 us -> 25.2 us
    pallas_call x10 -> x7, Pallas kernels: 270 us -> 160 us  [comm_call(): pl.pallas_call(kernel, name=name, out_shape=[jax.ShapeDtypeStruct(shape,...]
    pallas_call x0 -> x1, Pallas kernels: none -> 94 us  [named_call(): pl.pallas_call(kernel, name=name, out_shape=[jax.ShapeDtypeStruct(shape,...]
    dot_general x2 -> x0, matrix products: 6.95 us -> none  [the longest x1 5.04 us: shards(): jnp.einsum('hqk,khd->qhd', probs_first, v, preferred_element_type=F32)]
    unnamed x68 -> x35, local copies, waits for them, and re-layouts: 9.43 us -> 3.33 us
    dot_general x4 -> x2, matrix products: 10.1 us -> 5.58 us  [dot(): return jnp.dot(left, right, preferred_element_type=F32)]
where the time goes in v2:
time: 354 us; the launch traced here: 351 us
  Pallas kernels  254 us (72%)
  matrix products  45.5 us (13%)
  other arithmetic  25.5 us (7%)
  local copies, waits for them, and re-layouts  25.2 us (7%)
    pallas_call x7, Pallas kernels, comm_call(): pl.pallas_call(kernel, name=name, out_shape=[jax.ShapeDtypeStruct(shape,...  160 us
    pallas_call x1, Pallas kernels, named_call(): pl.pallas_call(kernel, name=name, out_shape=[jax.ShapeDtypeStruct(shape,...  94 us
    dot_general x4, matrix products, dot_back(): return jnp.einsum('re,de->rd', left, right, preferred_element_type=F32)  14.9 us
    dot_general x4, matrix products, dot_rows(): return jnp.einsum('rd,re->de', left, right, preferred_element_type=F32)  10.8 us

profile of v2, /device:TPU:0, one launch (start us, length us, event | category | flops | bytes accessed | tf_op | source)
XLA Modules:
  0.0 351.4 jit_solution(7283458053959754965)
XLA Ops:
  0.7 94.0 %forward.1 = (bf16[4,128,1024]{2,1,0:T(8,128)(2,1)}, bf16[8,128,768]{2,1,0:T(8,128)(2,1)}, bf16[8,128,1024]{2,1,0:T(8,128)(2,1)}, bf16[8,128,1024]{2,1,0:T(8,128...) custom-call(s32[2]{0:T(128)} %refs_0_.1, ...), custom_call_target="tpu_custom_call" | custom-call | tf_op jit(solution)/shard_map/forward/pallas_call | solution.py:503
  94.6 0.9 fusion.41
  95.7 0.9 dynamic-slice_reduce_fusion
  96.7 0.8 slice.81
  97.5 1.6 multiply_convert_fusion
  99.2 16.3 %gather_x.1 = bf16[4,128,1024]{2,1,0:T(8,128)(2,1)} custom-call(bf16[128,1024]{1,0:T(8,128)(2,1)} %get-tuple-element.44.mine), custom_call_target="tpu_custom_call" | custom-call | tf_op jit(solution)/shard_map/gather_x/pallas_call | solution.py:70
  115.5 2.6 fusion.46
  118.1 6.3 %fusion.36 = (f32[1024]{0:T(1024)S(1)}, bf16[512,1024]{1,0:T(8,128)(2,1)S(1)}, f32[512,1024]{1,0:T(8,128)S(1)}) fusion(f32[512,1024]{1,0:T(8,128)S(1)} %fusion.46, f32[1024]{0:T(1024)S(1)} %dynamic_slice.37, bf16[512,1024]{1,0:T(8,128)(2,1)S(1)} %bitcast.172, bf16[1024,1024]{1,0:T(8,128)(2,1)S(1)} %bitcast.206), kind=kOutput, calls=%fused_computation.109 | convolution fusion | flops 1112538112 | bytes 8396800 | tf_op jit(solution)/shard_map/re,de->rd/dot_general | solution.py:802
  124.4 0.5 multiply_convert_fusion.1
  124.9 3.0 fusion.44
  127.9 3.0 fusion.43
  130.9 26.7 %scatter_x.1 = (bf16[3,128,1024]{2,1,0:T(8,128)(2,1)}, bf16[3,128,1024]{2,1,0:T(8,128)(2,1)}) custom-call(bf16[4,128,1024]{2,1,0:T(8,128)(2,1)} %get-tuple-element.104.part_one, bf16[4,128,1024]{2,1,0:T(8,128)(2,1)} %get-tuple-element.106.part_two), custom_call_target="tpu_custom_call" | custom-call | tf_op jit(solution)/shard_map/scatter_x/pallas_call | solution.py:70
  157.6 1.8 convert_reduce_fusion.1
  159.8 1.4 multiply_reduce_fusion.3
  161.1 2.3 fusion.35
  163.4 1.5 convolution_convert_fusion.4
  164.9 10.9 %mix_forth.1 = bf16[16,64,128]{2,1,0:T(8,128)(2,1)} custom-call(bf16[2,64,1024]{2,1,0:T(8,128)(2,1)} %bitcast.174), custom_call_target="tpu_custom_call" | custom-call | tf_op jit(solution)/shard_map/mix_forth/pallas_call | solution.py:70
  175.9 1.2 reshape.411
  177.1 0.4 copy.107
  177.5 1.7 reshape.410
  179.2 3.3 fusion.38
  182.5 0.4 copy.111
  182.9 3.6 %fusion = (f32[2,1024]{1,0:T(2,128)S(1)}, f32[2,1024,1024]{1,2,0:T(8,128)S(1)}) fusion(bf16[2,1024,1024]{2,1,0:T(8,128)(2,1)} %get-tuple-element.51, bf16[1024,2,64]{0,2,1:T(8,128)(2,1)S(1)} %copy.107, bf16[1024,1,2,64]{0,3,2,1:T(8,128)(2,1)S(1)} %copy.111), kind=kOutput, calls=%fused_computation.2 | convolution fusion | flops 274724864 | bytes 13115392 | tf_op jit(solution)/shard_map/qhd,khd->hqk/dot_general | solution.py:927
  186.5 3.6 %fusion.1 = bf16[2,1024,1024]{1,2,0:T(8,128)(2,1)} fusion(bf16[2,1024,1024]{2,1,0:T(8,128)(2,1)S(1)} %copy-done, f32[2,1024,1024]{1,2,0:T(8,128)S(1)} %get-tuple-element.110, f32[2,1024]{1,0:T(2,128)S(1)} %get-tuple-element.109), kind=kLoop, calls=%fused_computation.3 | loop fusion | flops 8388608 | bytes 16785408 | tf_op jit(solution)/shard_map/convert_element_type | solution.py:929
  190.1 1.3 copy.110
  191.4 3.1 fusion.40
  194.8 3.8 %fusion.39 = (f32[2,64]{1,0:T(2,128)S(1)}, bf16[1024,2,64]{0,2,1:T(8,128)(2,1)S(1)}) fusion(bf16[1024,2,64]{0,2,1:T(8,128)(2,1)S(1)} %copy.107, bf16[2,1024,1024]{2,1,0:T(8,128)(2,1)} %get-tuple-element.51), kind=kOutput, calls=%fused_computation.111 | convolution fusion | flops 268697472 | bytes 4719104 | tf_op jit(solution)/shard_map/hqk,qhd->khd/dot_general | solution.py:932
  200.0 0.7 select_maximum_fusion.vec
  201.1 1.0 copy-done.8
  202.1 2.6 convolution_convert_fusion
  205.1 0.5 copy.97
  205.6 0.6 copy.112
  206.2 3.6 %fusion.11 = bf16[1024,2,64]{0,2,1:T(8,128)(2,1)S(1)} fusion(bf16[2,1024,1024]{1,2,0:T(8,128)(2,1)} %fusion.1, bf16[1024,1,2,64]{0,3,2,1:T(8,128)(2,1)S(1)} %copy.112), kind=kOutput, calls=%fused_computation.37 | convolution fusion | flops 268697600 | bytes 4718592 | tf_op jit(solution)/shard_map/hqk,qhd->khd/dot_general | solution.py:931
  209.8 0.3 concatenate.18
  210.2 0.5 copy.98
  210.6 0.3 concatenate.19
  211.0 0.5 copy.99
  211.4 1.0 pad_maximum_fusion.parts
  212.5 16.6 %heads_back.1 = bf16[8,64,768]{2,1,0:T(8,128)(2,1)} custom-call(bf16[16,64,384]{2,1,0:T(8,128)(2,1)} %pad_maximum_fusion.parts), custom_call_target="tpu_custom_call" | custom-call | tf_op jit(solution)/shard_map/heads_back/pallas_call | solution.py:70
  229.1 2.5 reshape.384
  231.6 0.9 copy.101
  232.5 3.5 convolution_convert_fusion.3
  236.0 0.8 copy.100
  236.8 0.4 dot_general.59
  237.2 4.1 %fusion.45 = (bf16[4,128,1024]{2,1,0:T(8,128)(2,1)}, f32[4,128,1024]{2,1,0:T(8,128)}) fusion(bf16[4,128,768]{2,1,0:T(8,128)(2,1)S(1)} %dot_general.59, bf16[1024,768,1]{1,0,2:T(8,128)(2,1)} %bitcast.168), kind=kOutput, calls=%fused_computation.117 | convolution fusion | flops 805830656 | bytes 5505024 | tf_op jit(solution)/shard_map/re,de->rd/dot_general | solution.py:802
  241.3 2.1 convolution_convert_fusion.2
  243.4 2.6 convolution_convert_fusion.1
  246.1 58.2 %sum_ctx.1 = (bf16[3,128,1024]{2,1,0:T(8,128)(2,1)}, f32[64,768]{1,0:T(8,128)}, f32[64,1024]{1,0:T(8,128)}, f32[64,1024]{1,0:T(8,128)}, f32[64,1024]{1,0:T(8,128)}, /*index=5*/f32[8,128]{1,0:T(8,128)}) custom-call(bf16[4,128,1024]{2,1,0:T(8,128)(2,1)} %get-tuple-element.112.part, bf16[8,2,64,768]{3,2,1,0:T(8,128)(2,1)} %bitcast.169, ...), custom_call_target="tpu_custom_call" | custom-call | tf_op jit(solution)/shard_map/sum_ctx/pallas_call | solution.py:70
  304.3 1.3 convert_reduce_fusion
  306.2 1.4 multiply_reduce_fusion
  307.8 0.6 pad.9.vec
  308.4 10.9 %sum_vec.1 = f32[8,128]{1,0:T(8,128)} custom-call(f32[16,8,128]{2,1,0:T(8,128)} %pad.9.vec), custom_call_target="tpu_custom_call" | custom-call | tf_op jit(solution)/shard_map/sum_vec/pallas_call | solution.py:70
  319.3 1.3 pad_maximum_fusion.2.s_vec
  320.6 20.6 %to_owners.1 = (f32[8,8,768]{2,1,0:T(8,128)}, f32[8,8,1024]{2,1,0:T(8,128)}, f32[8,8,1024]{2,1,0:T(8,128)}, f32[2,32,1024]{2,1,0:T(8,128)}, f32[8,16,128]{2,1,0:T(8,128)}) custom-call(f32[64,768]{1,0:T(8,128)} %get-tuple-element.57.s_qkv, f32[64,1024]{1,0:T(8,128)} %get-tuple-element.58.s_out, f32[64,1024]{1,0:T(8,128)} %get-tuple-element.59.s_one, ...), custom_call_target="tpu_custom_call" | custom-call | tf_op jit(solution)/shard_map/to_owners/pallas_call | solution.py:70
  341.2 1.0 reduce_sum.262
  342.2 0.7 reshape.400
  342.9 1.6 reduce_sum.265
  344.5 1.6 bitcast_reduce_fusion
  346.1 0.9 reduce_sum.261
  347.1 0.5 fusion.25
  347.6 1.6 reduce_sum.263
  349.3 0.5 fusion.26
  349.9 0.5 fusion.24
  350.5 1.0 add_convert_fusion
  (90 shorter events, 4.4 us)
Async XLA Ops:
  97.5 17.9 %copy-start.12 = (bf16[8,128,1024]{2,1,0:T(8,128)(2,1)S(1)}, bf16[8,128,1024]{2,1,0:T(8,128)(2,1)}, u32[]{:S(2)}) copy-start(bf16[8,128,1024]{2,1,0:T(8,128)(2,1)} %get-tuple-element.45) | copy-start | bytes 6291460
  115.5 2.6 copy-start.13
  124.4 3.5 %copy-start.14 = (bf16[512,1024]{1,0:T(8,128)(2,1)}, bf16[512,1024]{1,0:T(8,128)(2,1)S(1)}, u32[]{:S(2)}) copy-start(bf16[512,1024]{1,0:T(8,128)(2,1)S(1)} %get-tuple-element.79) | copy-start | bytes 3145732
  124.9 3.0 copy-start.7
  130.9 28.5 %copy-start.1 = (f32[128,1024]{1,0:T(8,128)S(1)}, f32[128,1024]{1,0:T(8,128)}, u32[]{:S(2)}) copy-start(f32[128,1024]{1,0:T(8,128)} %get-tuple-element.43) | copy-start | bytes 1572868
  159.4 1.7 copy-start.4
  161.1 2.3 copy-start.5
  163.4 14.1 %copy-start.9 = (bf16[16,64,384]{2,1,0:T(8,128)(2,1)S(1)}, bf16[16,64,384]{2,1,0:T(8,128)(2,1)}, u32[]{:S(2)}) copy-start(bf16[16,64,384]{2,1,0:T(8,128)(2,1)} %get-tuple-element.50) | copy-start | bytes 2359300
  182.8 3.7 %copy-start = (bf16[2,1024,1024]{2,1,0:T(8,128)(2,1)S(1)}, bf16[2,1024,1024]{2,1,0:T(8,128)(2,1)}, u32[]{:S(2)}) copy-start(bf16[2,1024,1024]{2,1,0:T(8,128)(2,1)} %get-tuple-element.51) | copy-start | bytes 12582916
  194.8 6.0 %copy-start.3 = (bf16[4,128,1024]{2,1,0:T(8,128)(2,1)S(1)}, bf16[4,128,1024]{2,1,0:T(8,128)(2,1)}, u32[]{:S(2)}) copy-start(bf16[4,128,1024]{2,1,0:T(8,128)(2,1)} %get-tuple-element.47) | copy-start | bytes 3145732
  200.9 1.2 copy-start.8
  237.2 4.1 %copy-start.10 = (bf16[2,64,1024]{2,1,0:T(8,128)(2,1)S(1)}, bf16[2,64,1024]{2,1,0:T(8,128)(2,1)}, u32[]{:S(2)}) copy-start(bf16[2,64,1024]{2,1,0:T(8,128)(2,1)} %get-tuple-element.55) | copy-start | bytes 786436
  241.3 2.1 copy-start.6
  241.3 2.1 copy-start.15
  246.0 59.6 %copy-start.2 = (bf16[1,2,64,1024]{3,2,1,0:T(8,128)(2,1)S(1)}, bf16[1,2,64,1024]{3,2,1,0:T(8,128)(2,1)}, u32[]{:S(2)}) copy-start(bf16[1,2,64,1024]{3,2,1,0:T(8,128)(2,1)} %param.17) | copy-start | bytes 786436
  304.3 15.0 %copy-start.11 = (f32[8,128]{1,0:T(8,128)S(1)}, f32[8,128]{1,0:T(8,128)}, u32[]{:S(2)}) copy-start(f32[8,128]{1,0:T(8,128)} %get-tuple-element.61) | copy-start | bytes 12292

commit v3 on v2

v3 whole, which is shorter than its diff:
```python
from types import SimpleNamespace

import jax
import jax.numpy as jnp
from jax import lax
from jax.experimental import pallas as pl
from jax.experimental.pallas import tpu as pltpu
from jax.sharding import PartitionSpec as P

HEADS = 16
HEAD_DIM = 64
MESH = pl.DeviceIdType.MESH
ANY = pl.ANY
VMEM = pltpu.VMEM
F32 = jnp.float32
BF16 = jnp.bfloat16

eps_norm = 1e-05
negative = -1e30


def place():
    c, s = lax.axis_index("ctx"), lax.axis_index("shard")
    return c, s, lax.rem(c, 2), s // 2, lax.rem(s, 2)


def sibling(c):
    return c + 1 - 2 * lax.rem(c, 2)


def norm_back(grad_normed, normed, inverse, gain):
    scaled = grad_normed * gain
    centred = scaled - jnp.mean(scaled, axis=-1, keepdims=True)
    return inverse * (centred - normed * jnp.mean(scaled * normed, axis=-1, keepdims=True))


def dot(left, right):
    return jnp.dot(left, right, preferred_element_type=F32)


def dot_tn(left, right):
    return lax.dot_general(left, right, (((0,), (0,)), ((), ())), preferred_element_type=F32)


def head_columns(x, core):
    return pl.ds(pl.multiple_of(x * 256 + core * 128, 128), 128)


def pick(value, unit):
    return pl.multiple_of(value * unit, unit)


def loop(count, body, first=0):
    def step(k, carry):
        body(k)
        return carry

    lax.fori_loop(first, count, step, 0)


def remote(src, dst, send_sem, recv_sem, device):
    return pltpu.make_async_remote_copy(
        src_ref=src,
        dst_ref=dst,
        send_sem=send_sem,
        recv_sem=recv_sem,
        device_id=device,
        device_id_type=MESH,
    )


def not_when(condition, body):
    pl.when(jnp.logical_not(condition))(body)


def norm_rows(rows):
    centre = rows - jnp.mean(rows, axis=-1, keepdims=True)
    inverse = lax.rsqrt(jnp.mean(centre * centre, axis=-1, keepdims=True) + eps_norm)
    return centre * inverse, inverse


def dot_nt(left, right):
    return lax.dot_general(left, right, (((1,), (1,)), ((), ())), preferred_element_type=F32)


VECTORS = (
    "ln1_gain", "ln1_bias", "query_bias", "value_bias", "out_bias", "ln2_gain", "ln2_bias", "fc2_bias",
)

LAYER_IN = (
    ("lengths", pltpu.SMEM),
    ("block_pairs", pltpu.SMEM),
    ("tok", VMEM),
    *[(name, VMEM) for name in VECTORS],
    ("fc1_bias", VMEM),
    ("w_qkv", ANY),
    ("w_out", ANY),
    ("w_fc1", ANY),
    ("w_fc2", ANY),
    ("cot", ANY),
)

LAYER_OUT = (
    ("layer_out", VMEM, (128, 1024), BF16),
    ("input_grad", VMEM, (128, 1024), BF16),
    ("o_qkv", VMEM, (8, 3072), F32),
    ("o_out", VMEM, (8, 1024), F32),
    ("o_one", VMEM, (8, 4096), F32),
    ("o_two", VMEM, (32, 1024), F32),
    ("o_vec", VMEM, (8, 128), F32),
    ("o_up", VMEM, (1, 128), F32),
)

LAYER_SCRATCH = (
    *[
        (name, pltpu.VMEM(shape, BF16))
        for name, shape in (
            ("tok_all", (4, 128, 1024)), ("attn_all", (4, 128, 1024)), ("cot_all", (4, 128, 1024)),
            ("wq_all", (8, 128, 768)), ("wo_all", (8, 128, 1024)), ("w1_all", (8, 128, 1024)),
            ("w2_all", (2, 512, 1024)), ("qkv", (16, 64, 384)), ("parts", (16, 64, 384)),
            ("probs", (2, 1024, 1024)), ("mixed", (16, 64, 128)), ("mix_rows", (2, 64, 1024)),
            ("mlp_all", (4, 128, 1024)), ("act_all", (4, 128, 1024)), ("gp_all", (4, 128, 1024)),
            ("gm_out", (4, 128, 1024)), ("mo_out", (4, 128, 1024)), ("gm_in", (4, 128, 1024)),
            ("mo_in", (4, 128, 1024)), ("hidden_low", (128, 1024)), ("gmix", (2, 64, 1024)),
            ("gmixed", (16, 64, 128)), ("gparts", (16, 64, 384)), ("gback", (16, 64, 384)),
            ("gqkv", (4, 128, 768)), ("ga_out", (4, 128, 1024)), ("ga_in", (4, 128, 1024)),
            ("g_two", (8, 2, 64, 1024)), ("g_one", (8, 2, 64, 1024)), ("g_out", (8, 2, 64, 1024)),
            ("g_qkv", (8, 2, 64, 768)), ("n_two", (8, 64, 1024)), ("n_one", (8, 64, 1024)),
            ("n_out", (8, 64, 1024)), ("n_qkv", (8, 64, 768)), ("f_two", (8, 64, 1024)),
            ("f_one", (8, 64, 1024)), ("f_out", (8, 64, 1024)), ("f_qkv", (8, 64, 768)),
        )
    ],
    *[
        (name, pltpu.VMEM(shape, F32))
        for name, shape in (
            ("small", (16, 128)), ("small_all", (16, 1024)), ("places", (1024, 128)), ("mix_t", (128, 1024)),
            ("hidden", (128, 1024)), ("gm_own", (128, 1024)), ("mo_own", (128, 1024)),
            ("grad_hidden", (128, 1024)), ("ga_own", (128, 1024)), ("gq_t", (128, 1024)), ("delta", (2, 1024)),
            ("s_two", (64, 1024)), ("s_one", (64, 1024)), ("s_out", (64, 1024)), ("s_qkv", (64, 768)),
            ("r_two", (2, 32, 1024)), ("r_one", (8, 8, 1024)), ("r_out", (8, 8, 1024)), ("r_qkv", (8, 8, 768)),
            ("vec", (8, 1024)), ("vec_sib", (8, 1024)), ("vec_in", (8, 8, 128)), ("vec_sum", (8, 128)),
            ("vec_all", (8, 8, 128)), ("up", (1, 1024)), ("up_sib", (1, 1024)), ("up_in", (8, 1, 1024)),
            ("up_sum", (1, 1024)), ("up_sum_own", (1, 1024)), ("up_all", (8, 1, 1024)),
        )
    ],
    *[
        (name, pltpu.SemaphoreType.DMA((count,)))
        for name, count in (
            ("local", 16), ("sm_s", 8), ("sm_r", 8), ("wq_s", 24), ("wq_r", 24), ("tk_s", 4), ("tk_r", 4),
            ("wz_s", 4), ("wz_r", 4), ("wc_s", 4), ("wc_r", 4), ("qa_s", 16), ("qa_r", 16),
            ("mx_s", 16), ("mx_r", 16), ("wo_s", 8), ("wo_r", 8), ("woc_s", 8), ("woc_r", 8),
            ("w1_s", 8), ("w1_r", 8), ("w1c_s", 8), ("w1c_r", 8), ("w2_s", 2), ("w2_r", 2), ("w2c_s", 2),
            ("w2c_r", 2), ("ct_s", 4), ("ct_r", 4), ("ml_s", 4), ("ml_r", 4), ("gm_s", 4), ("gm_r", 4),
            ("mo_s", 4), ("mo_r", 4), ("mf_s", 16), ("mf_r", 16), ("hb_s", 16), ("hb_r", 16), ("ga_s", 4),
            ("ga_r", 4), ("ns_s", 8), ("ns_r", 8), ("two_s", 8), ("two_r", 8), ("one_s", 8), ("one_r", 8),
            ("out_s", 8), ("out_r", 8), ("qk_s", 8), ("qk_r", 8), ("v1_s", 8), ("v1_r", 8), ("u1_s", 8),
            ("u1_r", 8), ("v2_s", 8), ("v2_r", 8), ("u2_s", 8), ("u2_r", 8), ("t_two_s", 2), ("t_two_r", 2),
            ("t_one_s", 8), ("t_one_r", 8), ("t_out_s", 8), ("t_out_r", 8), ("t_qk_s", 8), ("t_qk_r", 8),
        )
    ],
)


def layer_kernel(*refs):
    names = [n[0] for n in LAYER_IN + LAYER_OUT + LAYER_SCRATCH]
    r = SimpleNamespace(**dict(zip(names, refs, strict=True)))
    c, s, core, x, yl = place()
    z, yh = c // 4, lax.rem(c // 2, 2)
    sib = (sibling(c), s)
    at_home = z == x

    barrier = pltpu.get_barrier_semaphore()

    def hail(device):
        pl.semaphore_signal(barrier, inc=1, device_id=device, device_id_type=MESH)

    loop(8, lambda k: hail((c, lax.rem(s + k, 8))), 1)
    loop(16, lambda k: hail((lax.rem(c + k, 16), s)), 1)

    def hail_source(k):
        co, so = x * 4 + lax.rem(k, 4), 2 * (k // 4) + yl
        not_when((co == c) & (so == s), lambda: hail((co, so)))

    loop(16, hail_source)
    loop(16, lambda k: hail((lax.rem(c + k, 16), 2 * z + yl)), 1)
    not_when(at_home, lambda: hail((c, 2 * z + yl)))

    low = lax.rem(c, 4)
    to_c, to_x, from_c, from_x = 4 * x + z, low, 4 * low + x, z
    stays = (to_c == c) & (to_x == x)
    for y in range(2):
        not_when(stays & (yl == y), lambda: hail((from_c, 2 * from_x + y)))

    for i, name in enumerate(VECTORS):
        r.small[i : i + 1, :] = getattr(r, name)[...].astype(F32)
    r.small[8:12, :] = r.fc1_bias[...].astype(F32)
    lane = lax.broadcasted_iota(jnp.int32, (4, 128), 1)
    r.small[12:16, :] = jnp.where(
        lane == 0, r.lengths[0].astype(F32), jnp.where(lane == 1, r.lengths[1].astype(F32), 0.0)
    )
    pl.semaphore_wait(barrier, 56 - 2 * at_home.astype(jnp.int32) - stays.astype(jnp.int32))

    def await_block(dst, recv_sem):
        remote(dst, dst, r.local.at[15], recv_sem, sib).wait_recv()

    slice_rows = pl.ds(pick(z * 2 + core, 16), 16)
    columns_of = lambda peer: pl.ds(pick(peer, 128), 128)

    def small_to(k):
        return remote(
            r.small, r.small_all.at[:, columns_of(s)], r.sm_s.at[k], r.sm_r.at[k], (c, lax.rem(s + k, 8))
        )

    def wq_to(k, t):
        peer = lax.rem(s + k, 8)
        cols = pl.ds(pick(t * 4 + peer // 2, 256), 256)
        return remote(
            r.w_qkv.at[slice_rows, cols],
            r.wq_all.at[s, slice_rows, t * 256 : t * 256 + 256],
            r.wq_s.at[3 * k + t],
            r.wq_r.at[3 * k + t],
            (c, peer),
        )

    def tok_to(k):
        peer = 2 * lax.rem(x + k, 4) + yl
        return remote(r.tok, r.tok_all.at[x], r.tk_s.at[k], r.tk_r.at[k], (c, peer))

    loop(8, lambda k: small_to(k).start(), 1)

    def wq_start(k):
        for t in range(3):
            wq_to(k, t).start()

    loop(8, wq_start, 1)
    tok_to(1).start()
    tok_to(3).start()
    tok_to(2).start()
    own = [
        pltpu.make_async_copy(
            r.w_qkv.at[slice_rows, pl.ds(pick(t * 4 + x, 256), 256)],
            r.wq_all.at[s, slice_rows, t * 256 : t * 256 + 256],
            r.local.at[t],
        )
        for t in range(3)
    ]
    for copy in own:
        copy.start()
    r.small_all[:, columns_of(s)] = r.small[...]
    r.tok_all[x] = r.tok[...]

    sub = lax.broadcasted_iota(jnp.int32, (64, 128), 0)

    def set_places(k):
        pair = r.block_pairs[k]
        block = jnp.where(sub < 32, pair, 31 - pair)
        r.places[pl.ds(pick(k, 64), 64), :] = (block * 32 + lax.rem(sub, 32)).astype(F32)

    loop(16, set_places)

    for copy in own:
        copy.wait()

    def wq_arrived(k):
        origin = lax.rem(s - k + 8, 8)
        for t in range(3):
            await_block(r.wq_all.at[origin, slice_rows, t * 256 : t * 256 + 256], r.wq_r.at[3 * k + t])

    loop(8, wq_arrived, 1)

    def slice_of(zp, core_of):
        return r.wq_all.at[:, pl.ds(pick(zp * 2 + core_of, 16), 16)]

    def wq_along(k):
        block = slice_of(z, core)
        return remote(block, block, r.wz_s.at[k], r.wz_r.at[k], (lax.rem(c + 4 * k, 16), s))

    def wq_across(k):
        block = slice_of(lax.rem(z - k + 4, 4), core)
        return remote(block, block, r.wc_s.at[k], r.wc_r.at[k], sib)

    wq_along(1).start()
    wq_along(3).start()
    wq_along(2).start()
    wq_across(0).start()
    loop(
        8,
        lambda k: await_block(r.small_all.at[:, columns_of(lax.rem(s - k + 8, 8))], r.sm_r.at[k]),
        1,
    )
    for k in (1, 3, 2):
        await_block(slice_of(lax.rem(z - k + 4, 4), core), r.wz_r.at[k])
        wq_across(k).start()

    half = lambda which, rows: pl.ds(pick(which, rows), rows)

    def wo_to(k):
        peer = lax.rem(s + k, 8)
        return remote(
            r.w_out.at[half(core, 64)], r.wo_all.at[s, half(core, 64)], r.wo_s.at[k], r.wo_r.at[k], (c, peer)
        )

    def cot_to(k):
        peer = 2 * lax.rem(x + k, 4) + yl
        return remote(r.cot, r.cot_all.at[x], r.ct_s.at[k], r.ct_r.at[k], (c, peer))

    def w1_to(k):
        peer = lax.rem(s + k, 8)
        return remote(
            r.w_fc1.at[half(core, 64), pl.ds(pick(peer // 2, 1024), 1024)],
            r.w1_all.at[s, half(core, 64)],
            r.w1_s.at[k],
            r.w1_r.at[k],
            (c, peer),
        )

    def w2_to():
        mate = (c, s + 1 - 2 * yl)
        rows = half(core, 256)
        return remote(r.w_fc2.at[rows], r.w2_all.at[yl, rows], r.w2_s.at[0], r.w2_r.at[0], mate)

    own = [
        pltpu.make_async_copy(r.w_out, r.wo_all.at[s], r.local.at[4]),
        pltpu.make_async_copy(r.w_fc1.at[:, pl.ds(pick(x, 1024), 1024)], r.w1_all.at[s], r.local.at[5]),
        pltpu.make_async_copy(r.w_fc2, r.w2_all.at[yl], r.local.at[6]),
        pltpu.make_async_copy(r.cot, r.cot_all.at[x], r.local.at[7]),
    ]

    gain_one, bias_one = r.small_all[0:1, :], r.small_all[1:2, :]
    head_cols = pl.ds(pick(x, 256), 256)
    bias_qkv = (r.small_all[2:3, head_cols], None, r.small_all[3:4, head_cols])

    def parts_to(target):
        return remote(
            r.qkv.at[target], r.parts.at[c], r.qa_s.at[target], r.qa_r.at[c], (target, s)
        )

    def qkv_block(k):
        hop = k + (k // 2) * (1 - 2 * lax.rem(k, 2))
        origin = lax.rem(x - hop + 4, 4)

        @pl.when(k > 0)
        def _():
            await_block(r.tok_all.at[origin], r.tk_r.at[hop])

        normed, _ = norm_rows(r.tok_all[origin].astype(F32))
        r.attn_all[origin] = (normed * gain_one + bias_one).astype(BF16)

        @pl.when(k == 0)
        def _():
            for j in range(4):
                await_block(slice_of(lax.rem(z - j + 4, 4), 1 - core), r.wc_r.at[j])

        for t in range(3):
            cols = slice(t * 256, t * 256 + 256)
            acc = dot(r.attn_all[origin], r.wq_all[:, :, cols].reshape(1024, 256))
            if bias_qkv[t] is not None:
                acc = acc + bias_qkv[t]
            acc = acc.astype(BF16)
            for j in range(2):
                for p in range(2):
                    r.qkv[origin * 4 + j * 2 + p, :, t * 128 : t * 128 + 128] = acc[
                        j * 64 : j * 64 + 64, p * 128 : p * 128 + 128
                    ]

        for j in range(4):
            target = origin * 4 + j
            not_when(target == c, lambda: parts_to(target).start())

    loop(4, qkv_block)
    loop(8, lambda k: wo_to(k).start(), 1)
    for k in (1, 3, 2):
        cot_to(k).start()
    for copy in own:
        copy.start()
    r.parts[c] = r.qkv[c]
    loop(16, lambda k: await_block(r.parts.at[lax.rem(c + k, 16)], r.qa_r.at[lax.rem(c + k, 16)]), 1)
    w2_to().start()
    loop(8, lambda k: w1_to(k).start(), 1)

    slot_lane = lax.rem(c // 2, 2)
    row = r.small_all[12:13, columns_of(2 * (c // 4) + yl)]
    lane = lax.broadcasted_iota(jnp.int32, (1, 128), 1)
    length = jnp.sum(jnp.where(lane == slot_lane, row, 0.0), axis=1, keepdims=True)
    head_lane = lax.broadcasted_iota(jnp.int32, (1, 128), 1) // 64
    value_t = r.parts[:, :, 256:384].reshape(1024, 128).T

    def attend(i):
        keys = r.parts[:, :, 128:256].reshape(1024, 128)
        key_place = r.places[:, 0:1]
        query_place = r.places[pl.ds(pick(i, 256), 256), :].T[0:1, :]
        allowed = (key_place < length) & (key_place <= query_place)
        queries = r.parts[pl.ds(i * 4, 4), :, 0:128].reshape(256, 128) * jnp.asarray(0.125, BF16)
        cols = pl.ds(pick(i, 256), 256)
        for h in range(2):
            mine = jnp.where(head_lane == h, queries, jnp.zeros_like(queries))
            scores = jnp.where(allowed, dot_nt(keys, mine), negative)
            powers = jnp.exp(scores - jnp.max(scores, axis=0, keepdims=True))
            low = (powers * (1.0 / jnp.sum(powers, axis=0, keepdims=True))).astype(BF16)
            r.probs[h, :, cols] = low
            r.mix_t[h * 64 : h * 64 + 64, cols] = dot(value_t[h * 64 : h * 64 + 64], low)

    loop(4, attend)
    r.mixed[...] = r.mix_t[...].T.astype(BF16).reshape(16, 64, 128)

    def mix_to(k):
        peer = lax.rem(c + k, 16)
        return remote(
            r.mixed.at[peer],
            r.mix_rows.at[yh, :, head_columns(x, core)],
            r.mx_s.at[k],
            r.mx_r.at[x * 4 + yh * 2 + core],
            (peer, 2 * z + yl),
        )

    loop(16, lambda k: mix_to(k).start(), 1)
    not_when(at_home, lambda: mix_to(0).start())

    @pl.when(at_home)
    def _():
        r.mix_rows[yh, :, head_columns(x, core)] = r.mixed[c]

    def across(whole, recv, send_next, recv_next, rows):
        def body(k):
            block = whole.at[lax.rem(s - k + 8, 8), half(core, rows)]
            await_block(block, recv.at[k])
            remote(block, block, send_next.at[k], recv_next.at[k], sib).start()

        return body

    loop(8, across(r.wo_all, r.wo_r, r.woc_s, r.woc_r, 64), 1)
    loop(
        8,
        lambda k: await_block(r.wo_all.at[lax.rem(s - k + 8, 8), half(1 - core, 64)], r.woc_r.at[k]),
        1,
    )
    own[0].wait()

    def mix_arrived(k):
        xo, yo, ko = k // 4, lax.rem(k // 2, 2), lax.rem(k, 2)
        here = at_home & (xo == x) & (yo == yh) & (ko == core)
        not_when(here, lambda: await_block(r.mix_rows.at[yo, :, head_columns(xo, ko)], r.mx_r.at[k]))

    loop(16, mix_arrived)

    mix = r.mix_rows[...].reshape(128, 1024)
    hidden = r.tok[...].astype(F32) + (dot(mix, r.wo_all[...].reshape(1024, 1024)) + r.small_all[4:5, :])
    r.hidden[...] = hidden
    normed, _ = norm_rows(hidden)
    r.mlp_all[x] = (normed * r.small_all[5:6, :] + r.small_all[6:7, :]).astype(BF16)

    def mlp_to(k):
        peer = 2 * lax.rem(x + k, 4) + yl
        return remote(r.mlp_all.at[x], r.mlp_all.at[x], r.ml_s.at[k], r.ml_r.at[k], (c, peer))

    for k in (1, 3, 2):
        mlp_to(k).start()
    loop(8, across(r.w1_all, r.w1_r, r.w1c_s, r.w1c_r, 64), 1)
    block = r.w2_all.at[1 - yl, half(core, 256)]
    await_block(block, r.w2_r.at[0])
    w2_across = remote(block, block, r.w2c_s.at[0], r.w2c_r.at[0], sib)
    w2_across.start()
    for copy in own[1:]:
        copy.wait()
    loop(
        8,
        lambda k: await_block(r.w1_all.at[lax.rem(s - k + 8, 8), half(1 - core, 64)], r.w1c_r.at[k]),
        1,
    )
    await_block(r.w2_all.at[1 - yl, half(1 - core, 256)], r.w2c_r.at[0])

    r.up[...] = jnp.zeros_like(r.up)
    row_lane = lax.broadcasted_iota(jnp.int32, (1, 128), 1)
    upper = lax.broadcasted_iota(jnp.int32, (128, 1), 0) < 64

    def valid_of(origin):
        row = r.small_all[12:13, columns_of(2 * origin + yl)]
        lens = [jnp.sum(jnp.where(row_lane == j, row, 0.0), axis=1, keepdims=True) for j in range(2)]
        mine = r.places[pl.ds(pick(c, 64), 64), 0:1]
        return (jnp.concatenate([mine, mine], axis=0) < jnp.where(upper, lens[0], lens[1])).astype(F32)

    def part_to(out, into, sems, k):
        peer = lax.rem(x + k, 4)
        return remote(out.at[peer], into.at[k], sems[0].at[k], sems[1].at[k], (c, 2 * peer + yl))

    gm_sems, mo_sems, ga_sems = (r.gm_s, r.gm_r), (r.mo_s, r.mo_r), (r.ga_s, r.ga_r)

    def mlp_block(k):
        hop = k + (k // 2) * (1 - 2 * lax.rem(k, 2))
        origin = lax.rem(x - hop + 4, 4)

        @pl.when(k > 0)
        def _():
            await_block(r.mlp_all.at[origin], r.ml_r.at[hop])
            await_block(r.cot_all.at[origin], r.ct_r.at[hop])

        r.cot_all[origin] = (r.cot_all[origin].astype(F32) * valid_of(origin)).astype(BF16)
        for i in range(4):
            cols = slice(i * 256, i * 256 + 256)
            bias = jnp.concatenate(
                [
                    r.small_all[8 + (2 * i + a) % 4 : 9 + (2 * i + a) % 4, columns_of(2 * x + i // 2)]
                    for a in range(2)
                ],
                axis=1,
            )
            pre = dot(r.mlp_all[origin], r.w1_all[:, :, cols].reshape(1024, 256)) + bias
            spread = 0.5 * (1.0 + lax.erf(pre * 0.7071067811865476))
            r.act_all[origin, :, cols] = (pre * spread).astype(BF16)
            slope = spread + pre * (0.3989422804014327 * jnp.exp(-0.5 * pre * pre))
            grad = dot_nt(r.cot_all[origin], r.w2_all[i // 2, (i % 2) * 256 : (i % 2) * 256 + 256]) * slope
            r.up[:, cols] += jnp.sum(grad, axis=0, keepdims=True)
            r.gp_all[origin, :, cols] = grad.astype(BF16)
        for i in range(4):
            cols = slice(i * 256, i * 256 + 256)
            part = dot_nt(r.gp_all[origin], r.w1_all[2 * i : 2 * i + 2].reshape(256, 1024))
            r.gm_out[origin, :, cols] = part.astype(BF16)

            @pl.when(k == 0)
            def _():
                r.gm_own[:, cols] = part

        @pl.when(k > 0)
        def _():
            part_to(r.gm_out, r.gm_in, gm_sems, 4 - hop).start()

        for i in range(4):
            cols = slice(i * 256, i * 256 + 256)
            part = dot(r.act_all[origin], r.w2_all[:, :, cols].reshape(1024, 256))
            r.mo_out[origin, :, cols] = part.astype(BF16)

            @pl.when(k == 0)
            def _():
                r.mo_own[:, cols] = part

    loop(4, mlp_block)
    for k in (1, 3, 2):
        part_to(r.mo_out, r.mo_in, mo_sems, k).start()

    def outer(left, right, into, width):
        def body(i):
            rows = pl.ds(pick(i, 256), 256)
            part = dot_tn(left[:, :, rows].reshape(512, 256), right[...].reshape(512, width))
            into[pl.ds(2 * i, 2)] = part.astype(BF16).reshape(2, 2, 64, width)

        loop(4, body)

    def near_to(which, grad, near):
        return remote(grad.at[:, 1 - core], near, r.ns_s.at[which], r.ns_r.at[which], sib)

    def far_to(k, near, far, sems):
        peer = lax.rem(c // 2 + k, 8)
        return remote(near.at[peer], far.at[k], sems[0].at[k], sems[1].at[k], (2 * peer + core, s))

    def pair_sum(which, grad, near, far, sems):
        await_block(near, r.ns_r.at[which])

        def add(j):
            near[j] = (near[j].astype(F32) + grad[j, core].astype(F32)).astype(BF16)

        loop(8, add)
        loop(8, lambda k: far_to(k, near, far, sems).start(), 1)

    def far_sum(near, far, sems, total):
        loop(8, lambda k: await_block(far.at[k], sems[1].at[k]), 1)

        def add(j):
            rows = pl.ds(pick(j, 16), 16)
            acc = near[c // 2, rows].astype(F32)
            for k in range(1, 8):
                acc = acc + far[k, rows].astype(F32)
            total[rows] = acc

        loop(4, add)

    two = (r.n_two, r.f_two, (r.two_s, r.two_r))
    one = (r.n_one, r.f_one, (r.one_s, r.one_r))
    out = (r.n_out, r.f_out, (r.out_s, r.out_r))
    qk = (r.n_qkv, r.f_qkv, (r.qk_s, r.qk_r))

    outer(r.act_all, r.cot_all, r.g_two, 1024)
    near_to(0, r.g_two, r.n_two).start()
    outer(r.mlp_all, r.gp_all, r.g_one, 1024)
    near_to(1, r.g_one, r.n_one).start()

    total = r.gm_own[...]
    for k in (1, 3, 2):
        await_block(r.gm_in.at[k], r.gm_r.at[k])
        total = total + r.gm_in[k].astype(F32)
    normed, inverse = norm_rows(r.hidden[...])
    grad_out = r.cot_all[x].astype(F32)
    grad_hidden = grad_out + norm_back(total, normed, inverse, r.small_all[5:6, :])
    r.grad_hidden[...] = grad_hidden
    r.hidden_low[...] = grad_hidden.astype(BF16)
    for i, rows in enumerate((grad_hidden, total * normed, total, grad_out)):
        r.vec[i : i + 1, :] = jnp.sum(rows, axis=0, keepdims=True)
    for i in range(4):
        part = dot_nt(r.hidden_low[...], r.wo_all[2 * i : 2 * i + 2].reshape(256, 1024))
        r.gmix[:, :, i * 256 : i * 256 + 256] = part.astype(BF16).reshape(2, 64, 256)

    def gmix_to(k):
        xo, yo, ko = k // 4, lax.rem(k // 2, 2), lax.rem(k, 2)
        return remote(
            r.gmix.at[yo, :, head_columns(xo, ko)],
            r.gmixed.at[c],
            r.mf_s.at[k],
            r.mf_r.at[c],
            (x * 4 + yo * 2 + ko, 2 * xo + yl),
        )

    def gmix_away(k):
        return at_home & (k // 4 == x) & (lax.rem(k // 2, 2) == yh) & (lax.rem(k, 2) == core)

    loop(16, lambda k: not_when(gmix_away(k), lambda: gmix_to(k).start()))

    @pl.when(at_home)
    def _():
        r.gmixed[c] = r.gmix[yh, :, head_columns(x, core)]

    def out_rows(i):
        rows = pl.ds(pick(i, 256), 256)
        part = dot_tn(r.mix_rows[:, :, rows].reshape(128, 256), r.hidden_low[...])
        r.g_out[pl.ds(2 * i, 2)] = part.astype(BF16).reshape(2, 2, 64, 1024)

    loop(4, out_rows)
    near_to(2, r.g_out, r.n_out).start()
    pair_sum(0, r.g_two, *two)
    pair_sum(1, r.g_one, *one)
    pair_sum(2, r.g_out, *out)

    loop(16, lambda k: await_block(r.gmixed.at[lax.rem(c + k, 16)], r.mf_r.at[lax.rem(c + k, 16)]), 1)
    not_when(at_home, lambda: await_block(r.gmixed.at[c], r.mf_r.at[c]))

    def masked(rows, h):
        return jnp.where(head_lane == h, rows, jnp.zeros_like(rows))

    def values_back(i):
        gm = r.gmixed[...].reshape(1024, 128)
        rows = pl.ds(pick(i, 256), 256)
        acc = dot(r.probs[0, rows], masked(gm, 0)) + dot(r.probs[1, rows], masked(gm, 1))
        r.gparts[pl.ds(i * 4, 4), :, 256:384] = acc.astype(BF16).reshape(4, 64, 128)
        return jnp.sum(acc, axis=0, keepdims=True)

    bias_v = lax.fori_loop(0, 4, lambda i, acc: acc + values_back(i), jnp.zeros((1, 128), F32))
    products = r.gmixed[...].reshape(1024, 128).astype(F32).T * r.mix_t[...]
    for h in range(2):
        r.delta[h : h + 1, :] = jnp.sum(products[h * 64 : h * 64 + 64], axis=0, keepdims=True)
    keys_t = r.parts[:, :, 128:256].reshape(1024, 128).T

    def scores_back(i):
        cols = pl.ds(pick(i, 256), 256)
        values = r.parts[:, :, 256:384].reshape(1024, 128)
        gm = r.gmixed[pl.ds(i * 4, 4)].reshape(256, 128)
        for h in range(2):
            grad = dot_nt(values, masked(gm, h)) - r.delta[h : h + 1, cols]
            low = (r.probs[h, :, cols].astype(F32) * grad).astype(BF16)
            r.probs[h, :, cols] = low
            r.gq_t[h * 64 : h * 64 + 64, cols] = dot(keys_t[h * 64 : h * 64 + 64], low)

    loop(4, scores_back)

    def keys_back(i):
        queries = r.parts[:, :, 0:128].reshape(1024, 128) * jnp.asarray(0.125, BF16)
        rows = pl.ds(pick(i, 256), 256)
        acc = dot(r.probs[0, rows], masked(queries, 0)) + dot(r.probs[1, rows], masked(queries, 1))
        r.gparts[pl.ds(i * 4, 4), :, 128:256] = acc.astype(BF16).reshape(4, 64, 128)

    loop(4, keys_back)
    gq = r.gq_t[...].T * 0.125
    r.gparts[:, :, 0:128] = gq.astype(BF16).reshape(16, 64, 128)

    def back_to(k):
        peer = lax.rem(c + k, 16)
        return remote(r.gparts.at[peer], r.gback.at[c], r.hb_s.at[k], r.hb_r.at[c], (peer, s))

    loop(16, lambda k: back_to(k).start(), 1)
    r.gback[c] = r.gparts[c]
    wide = lax.broadcasted_iota(jnp.int32, (1, 1024), 1) // 128 == 2 * x + core
    for i, sums in ((4, jnp.sum(gq, axis=0, keepdims=True)), (5, bias_v)):
        r.vec[i : i + 1, :] = jnp.where(wide, jnp.concatenate([sums] * 8, axis=1), 0.0)

    total = r.mo_own[...] + r.small_all[7:8, :]
    for k in (1, 3, 2):
        await_block(r.mo_in.at[k], r.mo_r.at[k])
        total = total + r.mo_in[k].astype(F32)
    r.layer_out[...] = (valid_of(x) * (r.hidden[...] + total)).astype(BF16)
    loop(16, lambda k: await_block(r.gback.at[lax.rem(c + k, 16)], r.hb_r.at[lax.rem(c + k, 16)]), 1)

    r.vec[6:8, :] = jnp.zeros((2, 1024), F32)

    def attn_back(k):
        hop = jnp.where(k == 0, 2, jnp.where(k == 1, 3, jnp.where(k == 2, 1, 0)))
        origin = lax.rem(x + hop, 4)
        for t in range(3):
            for j in range(2):
                for p in range(2):
                    r.gqkv[origin, j * 64 : j * 64 + 64, t * 256 + p * 128 : t * 256 + p * 128 + 128] = r.gback[
                        origin * 4 + j * 2 + p, :, t * 128 : t * 128 + 128
                    ]
        normed, _ = norm_rows(r.tok_all[origin].astype(F32))
        for i in range(4):
            cols = slice(i * 256, i * 256 + 256)
            part = dot_nt(r.gqkv[origin], r.wq_all[2 * i : 2 * i + 2].reshape(256, 768))
            r.ga_out[origin, :, cols] = part.astype(BF16)
            r.vec[6:7, cols] += jnp.sum(part * normed[:, cols], axis=0, keepdims=True)
            r.vec[7:8, cols] += jnp.sum(part, axis=0, keepdims=True)

            @pl.when(k == 3)
            def _():
                r.ga_own[:, cols] = part

        @pl.when(k < 3)
        def _():
            part_to(r.ga_out, r.ga_in, ga_sems, hop).start()

    loop(4, attn_back)
    vec_across = remote(r.vec, r.vec_sib, r.ns_s.at[4], r.ns_r.at[4], sib)
    up_across = remote(r.up, r.up_sib, r.ns_s.at[5], r.ns_r.at[5], sib)
    vec_across.start()
    up_across.start()
    outer(r.attn_all, r.gqkv, r.g_qkv, 768)
    near_to(3, r.g_qkv, r.n_qkv).start()
    await_block(r.vec_sib, r.ns_r.at[4])
    await_block(r.up_sib, r.ns_r.at[5])
    vec_across.wait_send()
    up_across.wait_send()
    r.vec[...] += r.vec_sib[...]
    r.up[...] += r.up_sib[...]
    chip = c // 2

    def vec_to(k):
        peer = lax.rem(chip + k, 8)
        return remote(r.vec.at[:, columns_of(peer)], r.vec_in.at[k], r.v1_s.at[k], r.v1_r.at[k], (2 * peer + core, s))

    def up_to(k):
        peer = lax.rem(chip + k, 8)
        return remote(r.up, r.up_in.at[k], r.u1_s.at[k], r.u1_r.at[k], (2 * peer + core, s))

    loop(8, lambda k: vec_to(k).start(), 1)
    loop(8, lambda k: up_to(k).start(), 1)
    pair_sum(3, r.g_qkv, *qk)

    def rows_to(k, total, into, sems):
        peer = lax.rem(s + k, 8)
        rows = pl.ds(pick(peer, 8), 8)
        return remote(total.at[rows], into.at[s], sems[0].at[k], sems[1].at[k], (c, peer))

    def two_to(y):
        return remote(
            r.s_two.at[32 * y : 32 * y + 32],
            r.r_two.at[yl],
            r.t_two_s.at[y],
            r.t_two_r.at[yl],
            (to_c, 2 * to_x + y),
        )

    my_rows = pl.ds(pick(s, 8), 8)
    one_set = (r.s_one, r.r_one, (r.t_one_s, r.t_one_r))
    out_set = (r.s_out, r.r_out, (r.t_out_s, r.t_out_r))
    qk_set = (r.s_qkv, r.r_qkv, (r.t_qk_s, r.t_qk_r))

    def spread_rows(total, into, sems):
        loop(8, lambda k: rows_to(k, total, into, sems).start(), 1)
        into[s] = total[my_rows]

    far_sum(*two, r.s_two)
    for y in range(2):
        not_when(stays & (yl == y), lambda: two_to(y).start())

    @pl.when(stays)
    def _():
        r.r_two[yl] = r.s_two[pl.ds(pick(yl, 32), 32)]

    far_sum(*one, r.s_one)
    spread_rows(*one_set)
    far_sum(*out, r.s_out)
    spread_rows(*out_set)

    loop(8, lambda k: await_block(r.vec_in.at[k], r.v1_r.at[k]), 1)
    loop(8, lambda k: await_block(r.up_in.at[k], r.u1_r.at[k]), 1)
    sums = r.vec[:, columns_of(chip)]
    up_sums = r.up[...]
    for k in range(1, 8):
        sums = sums + r.vec_in[k]
        up_sums = up_sums + r.up_in[k]
    r.vec_sum[...] = sums
    r.up_sum[...] = up_sums

    def vec_rows_to(k):
        return remote(r.vec_sum, r.vec_all.at[s], r.v2_s.at[k], r.v2_r.at[k], (c, lax.rem(s + k, 8)))

    def up_rows_to(k):
        return remote(r.up_sum, r.up_all.at[s], r.u2_s.at[k], r.u2_r.at[k], (c, lax.rem(s + k, 8)))

    loop(8, lambda k: vec_rows_to(k).start(), 1)
    loop(8, lambda k: up_rows_to(k).start(), 1)
    r.vec_all[s] = sums
    r.up_all[s] = up_sums

    total = r.ga_own[...]
    for k in (1, 3, 2):
        await_block(r.ga_in.at[k], r.ga_r.at[k])
        total = total + r.ga_in[k].astype(F32)
    normed, inverse = norm_rows(r.tok[...].astype(F32))
    r.input_grad[...] = (
        r.grad_hidden[...] + norm_back(total, normed, inverse, r.small_all[0:1, :])
    ).astype(BF16)

    far_sum(*qk, r.s_qkv)
    spread_rows(*qk_set)

    def rows_arrived(into, sems):
        loop(8, lambda k: await_block(into.at[lax.rem(s - k + 8, 8)], sems[1].at[k]), 1)

    for y in range(2):
        not_when(stays & (yl == y), lambda: await_block(r.r_two.at[y], r.t_two_r.at[y]))
    r.o_two[...] = r.r_two[0] + r.r_two[1]
    rows_arrived(r.r_one, one_set[2])
    for i in range(4):
        r.o_one[:, i * 1024 : i * 1024 + 1024] = r.r_one[2 * i] + r.r_one[2 * i + 1]
    rows_arrived(r.r_out, out_set[2])
    total = r.r_out[0]
    for i in range(1, 8):
        total = total + r.r_out[i]
    r.o_out[...] = total
    rows_arrived(r.vec_all, (r.v2_s, r.v2_r))
    rows_arrived(r.up_all, (r.u2_s, r.u2_r))
    total = r.vec_all[0]
    for i in range(1, 8):
        total = total + r.vec_all[i]
    r.o_vec[...] = total
    up_sums = r.up_all[2 * z] + r.up_all[2 * z + 1]
    r.up_sum_own[...] = up_sums
    r.o_up[...] = r.up_sum_own[:, columns_of(2 * low + s // 4)]
    rows_arrived(r.r_qkv, qk_set[2])
    for i in range(4):
        total = r.r_qkv[2 * i] + r.r_qkv[2 * i + 1]
        for t in range(3):
            r.o_qkv[:, t * 1024 + i * 256 : t * 1024 + i * 256 + 256] = total[:, t * 256 : t * 256 + 256]

    def sent(k):
        small_to(k).wait_send()
        for t in range(3):
            wq_to(k, t).wait_send()
        wo_to(k).wait_send()
        w1_to(k).wait_send()
        for whole, sem in ((r.wo_all, r.woc_s), (r.w1_all, r.w1c_s)):
            block = whole.at[lax.rem(s - k + 8, 8), half(core, 64)]
            remote(block, block, sem.at[k], sem.at[k], sib).wait_send()
        for group in (two, one, out, qk):
            far_to(k, *group).wait_send()
        for group in (one_set, out_set, qk_set):
            rows_to(k, *group).wait_send()
        vec_to(k).wait_send()
        up_to(k).wait_send()
        vec_rows_to(k).wait_send()
        up_rows_to(k).wait_send()

    loop(8, sent, 1)
    for k in range(1, 4):
        tok_to(k).wait_send()
        wq_along(k).wait_send()
        cot_to(k).wait_send()
        mlp_to(k).wait_send()
        part_to(r.gm_out, r.gm_in, gm_sems, k).wait_send()
        part_to(r.mo_out, r.mo_in, mo_sems, k).wait_send()
        part_to(r.ga_out, r.ga_in, ga_sems, k).wait_send()
    for k in range(4):
        wq_across(k).wait_send()
    near_to(0, r.g_two, r.n_two).wait_send()
    near_to(1, r.g_one, r.n_one).wait_send()
    near_to(2, r.g_out, r.n_out).wait_send()
    near_to(3, r.g_qkv, r.n_qkv).wait_send()
    w2_to().wait_send()
    w2_across.wait_send()
    loop(16, lambda k: not_when(k == c, lambda: parts_to(k).wait_send()))
    loop(16, lambda k: mix_to(k).wait_send(), 1)
    loop(16, lambda k: back_to(k).wait_send(), 1)
    loop(16, lambda k: not_when(gmix_away(k), lambda: gmix_to(k).wait_send()))
    not_when(at_home, lambda: mix_to(0).wait_send())
    for y in range(2):
        not_when(stays & (yl == y), lambda: two_to(y).wait_send())


def named_call(kernel, name, cid, ins, outs, scratch, operands):
    results = pl.pallas_call(
        kernel,
        name=name,
        out_shape=[jax.ShapeDtypeStruct(shape, dtype) for _, _, shape, dtype in outs],
        in_specs=[pl.BlockSpec(memory_space=space) for _, space in ins],
        out_specs=[pl.BlockSpec(memory_space=space) for _, space, _, _ in outs],
        scratch_shapes=[kind for _, kind in scratch],
        compiler_params=pltpu.CompilerParams(
            collective_id=cid, has_side_effects=True, vmem_limit_bytes=60 << 20
        ),
    )(*[operands[name] for name, _ in ins])
    return SimpleNamespace(**dict(zip([o[0] for o in outs], results, strict=True)))


def shards(
    tokens,
    lengths,
    block_pairs,
    ln1_gain,
    ln1_bias,
    w_qkv,
    query_bias,
    value_bias,
    w_out,
    out_bias,
    ln2_gain,
    ln2_bias,
    w_fc1,
    fc1_bias,
    w_fc2,
    fc2_bias,
    out_cotangent,
):
    c, s = lax.axis_index("ctx"), lax.axis_index("shard")
    f = named_call(
        layer_kernel,
        "layer",
        0,
        LAYER_IN,
        LAYER_OUT,
        LAYER_SCRATCH,
        dict(
            lengths=lengths,
            block_pairs=block_pairs,
            tok=tokens.reshape(128, 1024),
            ln1_gain=ln1_gain.reshape(1, 128),
            ln1_bias=ln1_bias.reshape(1, 128),
            query_bias=query_bias.reshape(1, 128),
            value_bias=value_bias.reshape(1, 128),
            out_bias=out_bias.reshape(1, 128),
            ln2_gain=ln2_gain.reshape(1, 128),
            ln2_bias=ln2_bias.reshape(1, 128),
            fc2_bias=fc2_bias.reshape(1, 128),
            fc1_bias=fc1_bias.reshape(4, 128),
            w_qkv=w_qkv,
            w_out=w_out,
            w_fc1=w_fc1,
            w_fc2=w_fc2,
            cot=out_cotangent.reshape(128, 1024),
        ),
    )
    mine = lax.dynamic_slice(f.o_vec, (0, (c % 2) * 64 + s * 8), (8, 8))
    up = lax.dynamic_slice_in_dim(f.o_up[0], (s % 4) * 32, 32)
    return (
        f.layer_out.reshape(tokens.shape),
        f.input_grad.reshape(tokens.shape),
        mine[6],
        mine[7],
        f.o_qkv,
        mine[4],
        mine[5],
        f.o_out,
        mine[0],
        mine[1],
        mine[2],
        f.o_one,
        up,
        f.o_two,
        mine[3],
    )


def solution(mesh):
    one, both = P("shard"), P(("ctx", "shard"))
    rows, both_rows = P("shard", None), P(("ctx", "shard"), None)
    whole = P("ctx", "shard", None, None)
    return jax.shard_map(
        shards,
        mesh=mesh,
        in_specs=(
            whole, one, P(), one, one, rows, one, one, rows, one, one, one, rows, one, rows, one, whole,
        ),
        out_specs=(
            whole, whole, both, both, both_rows, both, both, both_rows, both, both, both,
            both_rows, both, both_rows, both,
        ),
        check_vma=False,
    )
```

time: 354 us -> 219 us (0.62)
  matrix products: 45.5 us -> 0 us
  Pallas kernels: 254 us -> 210 us
  other arithmetic: 25.5 us -> 0 us
  local copies, waits for them, and re-layouts: 25.2 us -> 8.13 us
    pallas_call x7 -> x0, Pallas kernels: 160 us -> none  [comm_call(): pl.pallas_call(kernel, name=name, out_shape=[jax.ShapeDtypeStruct(shape,...]
    pallas_call x1, Pallas kernels: 94 us -> 210 us  [named_call(): pl.pallas_call(kernel, name=name, out_shape=[jax.ShapeDtypeStruct(shape,...]
    dot_general x14 -> x0, matrix products: 45.5 us -> none  [the longest x4 14.9 us: dot_back(): return jnp.einsum('re,de->rd', left, right, preferred_element_type=F32)]
    reduce_sum x15 -> x0, other arithmetic: 15.5 us -> none  [the longest x1 2.25 us: shards(): grad_out_b = jnp.sum(grad_hidden, axis=0)]
    convert_element_type x8 -> x0, other arithmetic: 7.01 us -> none  [the longest x1 3.57 us: shards(): grad_scores = (probs * (grad_probs - delta)).astype(BF16)]
    reshape x10 -> x0, local copies, waits for them, and re-layouts: 6.94 us -> none  [the longest x1 2.53 us: shards(): g_qkv = g_qkv.reshape(512, 2, 3, 128).swapaxes(1, 2).reshape(512, 768)]
    slice x7 -> x0, local copies, waits for them, and re-layouts: 4.97 us -> none  [the longest x1 3.28 us: shards(): q, k, v = (parts[:, 0], parts[:, 1], parts[:, 2])]
where the time goes in v3:
time: 219 us
  Pallas kernels  210 us (96%)
  local copies, waits for them, and re-layouts  8.13 us (4%)
    pallas_call x1, Pallas kernels, named_call(): pl.pallas_call(kernel, name=name, out_shape=[jax.ShapeDtypeStruct(shape,...  210 us
    unnamed x18, local copies, waits for them, and re-layouts  6.26 us

profile of v3, /device:TPU:0, one launch (start us, length us, event | category | flops | bytes accessed | tf_op | source)
XLA Modules:
  0.0 218.9 jit_solution(17838868381166586282)
XLA Ops:
  0.7 210.1 %layer.1 = (bf16[128,1024]{1,0:T(8,128)(2,1)}, bf16[128,1024]{1,0:T(8,128)(2,1)}, f32[8,3072]{1,0:T(8,128)}, f32[8,1024]{1,0:T(8,128)}, f32[8,4096]{1,0:T(8,128)...) custom-call(s32[2]{0:T(128)} %refs_0_.1, s32[16]{0:T(128)} %refs_1_.1, bf16[128,1024]{1,0:T(8,128)(2,1)} %bitcast.33, ...), custom_call_target="tpu_custom_call" | custom-call | tf_op jit(solution)/shard_map/layer/pallas_call | solution.py:886
  210.8 0.8 constant_dynamic-slice_fusion
  211.5 0.5 slice_bitcast_fusion
  212.0 0.0 copy-start.5
  212.1 0.6 copy-done.5
  212.7 0.6 dynamic-slice_bitcast_fusion
  213.2 0.0 copy-start
  213.2 1.7 copy.38
  214.9 0.0 copy-done
  214.9 0.0 copy-start.3
  215.0 0.7 copy.39
  215.7 0.3 copy-done.3
  215.9 0.0 copy-start.4
  215.9 0.0 copy-start.2
  215.9 0.6 copy.40
  216.6 0.1 copy-done.4
  216.7 0.6 copy.41
  217.3 0.0 copy-done.2
  217.3 0.0 copy-start.1
  217.3 0.7 copy.42
  217.9 0.3 copy-done.1
  218.2 0.7 copy.43
Async XLA Ops:
  212.0 0.6 copy-start.5
  213.2 1.7 copy-start
  214.9 1.0 copy-start.3
  215.9 0.8 copy-start.4
  215.9 1.4 copy-start.2
  217.3 1.0 copy-start.1

commit v4 on v3

v4 whole, which is shorter than its diff:
```python
from types import SimpleNamespace

import jax
import jax.numpy as jnp
from jax import lax
from jax.experimental import pallas as pl
from jax.experimental.pallas import tpu as pltpu
from jax.sharding import PartitionSpec as P

HEADS = 16
HEAD_DIM = 64
MESH = pl.DeviceIdType.MESH
ANY = pl.ANY
VMEM = pltpu.VMEM
F32 = jnp.float32
BF16 = jnp.bfloat16

eps_norm = 1e-05
negative = -1e30


def place():
    c, s = lax.axis_index("ctx"), lax.axis_index("shard")
    return c, s, lax.rem(c, 2), s // 2, lax.rem(s, 2)


def sibling(c):
    return c + 1 - 2 * lax.rem(c, 2)


def norm_back(grad_normed, normed, inverse, gain):
    scaled = grad_normed * gain
    centred = scaled - jnp.mean(scaled, axis=-1, keepdims=True)
    return inverse * (centred - normed * jnp.mean(scaled * normed, axis=-1, keepdims=True))


def dot(left, right):
    return jnp.dot(left, right, preferred_element_type=F32)


def dot_tn(left, right):
    return lax.dot_general(left, right, (((0,), (0,)), ((), ())), preferred_element_type=F32)


def pick(value, unit):
    return pl.multiple_of(value * unit, unit)


def loop(count, body, first=0):
    def step(k, carry):
        body(k)
        return carry

    lax.fori_loop(first, count, step, 0)


def remote(src, dst, send_sem, recv_sem, device):
    return pltpu.make_async_remote_copy(
        src_ref=src,
        dst_ref=dst,
        send_sem=send_sem,
        recv_sem=recv_sem,
        device_id=device,
        device_id_type=MESH,
    )


def not_when(condition, body):
    pl.when(jnp.logical_not(condition))(body)


def norm_rows(rows):
    centre = rows - jnp.mean(rows, axis=-1, keepdims=True)
    inverse = lax.rsqrt(jnp.mean(centre * centre, axis=-1, keepdims=True) + eps_norm)
    return centre * inverse, inverse


def dot_nt(left, right):
    return lax.dot_general(left, right, (((1,), (1,)), ((), ())), preferred_element_type=F32)


VECTORS = (
    "ln1_gain", "ln1_bias", "query_bias", "value_bias", "out_bias", "ln2_gain", "ln2_bias", "fc2_bias",
)

LAYER_IN = (
    ("lengths", pltpu.SMEM),
    ("block_pairs", pltpu.SMEM),
    ("tok", VMEM),
    *[(name, VMEM) for name in VECTORS],
    ("fc1_bias", VMEM),
    ("w_qkv", ANY),
    ("w_out", ANY),
    ("w_fc1", ANY),
    ("w_fc2", ANY),
    ("cot", ANY),
)

LAYER_OUT = (
    ("layer_out", VMEM, (128, 1024), BF16),
    ("input_grad", VMEM, (128, 1024), BF16),
    ("o_qkv", VMEM, (8, 3072), F32),
    ("o_out", VMEM, (8, 1024), F32),
    ("o_one", VMEM, (8, 4096), F32),
    ("o_two", VMEM, (32, 1024), F32),
    ("o_vec", VMEM, (16, 128), F32),
)

WEIGHTS = (("wq", 768), ("wo", 1024), ("w1", 1024), ("w2", 1024))
GRADS = (("two", 1024), ("one", 1024), ("out", 1024), ("qkv", 768))

LAYER_SCRATCH = (
    *[(name + "_all", pltpu.VMEM((8, 128, width), BF16)) for name, width in WEIGHTS],
    *[
        (prefix + name, pltpu.VMEM((*shape, width), BF16))
        for name, width in GRADS
        for prefix, shape in (
            ("g_", (8, 2, 64)), ("n_", (8, 64)), ("a_", (4, 4, 32)), ("b_", (4, 4, 32)), ("m_", (4, 32)), ("h_", (4, 32)),
        )
    ],
    *[("s_" + name, pltpu.VMEM((32, width), F32)) for name, width in GRADS],
    *[
        (name, pltpu.VMEM(shape, BF16))
        for name, shape in (
            ("tok_all", (4, 128, 1024)), ("attn_all", (4, 128, 1024)), ("cot_all", (4, 128, 1024)),
            ("qkv", (4, 4, 64, 384)), ("parts", (4, 4, 64, 384)),
            ("probs", (2, 1024, 1024)), ("mixed", (16, 64, 128)), ("mix_rows", (2, 64, 1024)),
            ("mlp_all", (4, 128, 1024)), ("act_all", (4, 128, 1024)), ("gp_all", (4, 128, 1024)),
            ("gm_out", (4, 128, 1024)), ("mo_out", (4, 128, 1024)), ("gm_in", (4, 128, 1024)),
            ("mo_in", (4, 128, 1024)), ("hidden_low", (128, 1024)), ("gmix", (2, 64, 1024)),
            ("gmixed", (16, 64, 128)), ("gparts", (4, 4, 64, 384)), ("gback", (4, 4, 64, 384)),
            ("gqkv", (4, 128, 768)), ("ga_out", (4, 128, 1024)), ("ga_in", (4, 128, 1024)),
        )
    ],
    *[
        (name, pltpu.VMEM(shape, F32))
        for name, shape in (
            ("small", (16, 128)), ("small_all", (16, 1024)), ("places", (1024, 128)), ("mix_t", (128, 1024)),
            ("hidden", (128, 1024)), ("gm_own", (128, 1024)), ("mo_own", (128, 1024)),
            ("grad_hidden", (128, 1024)), ("ga_own", (128, 1024)), ("gq_t", (128, 1024)), ("delta", (2, 1024)),
            ("r_two", (32, 1024)), ("r_one", (4, 8, 1024)), ("r_out", (4, 8, 1024)), ("r_qkv", (4, 8, 768)),
            ("vec", (16, 1024)), ("vec_sib", (16, 1024)), ("vec_in", (8, 16, 128)), ("vec_sum", (16, 128)),
            ("vec_all", (8, 16, 128)),
        )
    ],
    *[
        (prefix + name + end, pltpu.SemaphoreType.DMA((4,)))
        for name, _ in WEIGHTS
        for prefix in ("own_", "far_", "mate_")
        for end in ("_s", "_r")
    ],
    *[
        (prefix + name + end, pltpu.SemaphoreType.DMA((4,)))
        for name, _ in GRADS
        for prefix in ("first_", "second_", "last_")
        for end in ("_s", "_r")
    ],
    *[
        (name + end, pltpu.SemaphoreType.DMA((count,)))
        for name, count in (
            ("local", 16), ("sm", 8), ("tk", 4), ("qa", 16), ("mx", 16), ("ct", 4), ("ml", 4), ("gm", 4), ("mo", 4),
            ("mf", 16), ("hb", 16), ("ga", 4), ("ns", 8), ("v1", 8), ("v2", 8),
        )
        for end in ("_s", "_r")
    ],
)


def layer_kernel(*refs):
    names = [n[0] for n in LAYER_IN + LAYER_OUT + LAYER_SCRATCH]
    r = SimpleNamespace(**dict(zip(names, refs, strict=True)))
    ref = lambda *name: getattr(r, "".join(name))
    c, s, core, x, yl = place()
    z, yh, q4 = c // 4, lax.rem(c // 2, 2), lax.rem(c, 4)
    sib = (sibling(c), s)
    mate_s = s + 1 - 2 * yl
    half = lambda which: pl.ds(pick(which, 64), 64)

    pieces = [(r.w_qkv, r.wq_all, t * 1024 + z * 256, t * 256, 256) for t in range(3)]
    pieces += [(r.w_fc1, r.w1_all, t * 512 + z * 128, t * 128, 128) for t in range(8)]
    own = [
        pltpu.make_async_copy(
            weight.at[half(core), pl.ds(pl.multiple_of(source, 128), width)],
            whole.at[s, half(core), target : target + width],
            r.local_s.at[i],
        )
        for i, (weight, whole, source, target, width) in enumerate(pieces)
    ]
    own.append(pltpu.make_async_copy(r.w_out.at[half(core)], r.wo_all.at[s, half(core)], r.local_s.at[11]))
    own.append(
        pltpu.make_async_copy(r.w_fc2.at[half(2 * z + core)], r.w2_all.at[s, half(core)], r.local_s.at[12])
    )
    own.append(pltpu.make_async_copy(r.cot, r.cot_all.at[z], r.local_s.at[13]))
    for copy in own:
        copy.start()

    barrier = pltpu.get_barrier_semaphore()

    def hail(device):
        pl.semaphore_signal(barrier, inc=1, device_id=device, device_id_type=MESH)

    to_z, from_x, from_yl = 2 * yl + lax.rem(x, 2), x // 2 * 2 + lax.rem(z, 2), z // 2
    at_home = to_z == z
    two_to = (to_z * 4 + yh * 2 + z // 2, (lax.rem(z, 2) * 2 + core) * 2 + x // 2)
    two_from = (
        (core * 2 + x // 2) * 4 + yh * 2 + lax.rem(x, 2),
        (yl * 2 + lax.rem(z, 2)) * 2 + z // 2,
    )
    two_stays = (two_to[0] == c) & (two_to[1] == s)
    loop(8, lambda k: hail((c, lax.rem(s + k, 8))), 1)
    loop(16, lambda k: hail((lax.rem(c + k, 16), s)), 1)
    hail((c + 2 - 4 * yh, mate_s))
    loop(4, lambda k: not_when(at_home & (k == z), lambda: hail((k * 4 + q4, 2 * from_x + from_yl))))
    not_when(two_stays, lambda: hail(two_from))

    for i, name in enumerate(VECTORS):
        r.small[i : i + 1, :] = ref(name)[...].astype(F32)
    r.small[8:12, :] = r.fc1_bias[...].astype(F32)
    r.small[12:16, :] = jnp.zeros((4, 128), F32)
    for copy in own[:3]:
        copy.wait()
    pl.semaphore_wait(barrier, 28 - at_home.astype(jnp.int32) - two_stays.astype(jnp.int32))

    def await_block(dst, recv_sem):
        remote(dst, dst, r.local_s.at[15], recv_sem, sib).wait_recv()

    columns_of = lambda which: pl.ds(pick(which, 128), 128)
    z_peer = lambda k: (lax.rem(c + 4 * k, 16), s)
    x_peer = lambda k: (c, 2 * lax.rem(x + k, 4) + yl)

    def small_to(k):
        return remote(
            r.small, r.small_all.at[:, columns_of(s)], r.sm_s.at[k], r.sm_r.at[k], (c, lax.rem(s + k, 8))
        )

    def tok_to(k):
        return remote(r.tok, r.tok_all.at[z], r.tk_s.at[k], r.tk_r.at[k], z_peer(k))

    def cot_to(k):
        return remote(r.cot, r.cot_all.at[z], r.ct_s.at[k], r.ct_r.at[k], z_peer(k))

    def weight_copy(name, kind, k):
        whole = ref(name, "_all")
        device = (c, mate_s) if kind == "mate_" else x_peer(k)
        block = whole.at[mate_s if kind == "far_" else s, half(core)]
        if kind == "mate_" and k == 0:
            device, block = sib, whole.at[:, half(core)]
        return remote(block, block, ref(kind, name, "_s").at[k], ref(kind, name, "_r").at[k], device)

    def weight_own(name):
        weight_copy(name, "mate_", 1).start()
        for k in (1, 3, 2):
            weight_copy(name, "own_", k).start()

    def weight_far(name):
        await_block(ref(name, "_all").at[mate_s, half(core)], ref("mate_", name, "_r").at[1])
        for k in (1, 3, 2):
            weight_copy(name, "far_", k).start()

    def weight_across(name):
        for k in (1, 3, 2):
            origin = 2 * lax.rem(x - k + 4, 4)
            await_block(ref(name, "_all").at[origin + yl, half(core)], ref("own_", name, "_r").at[k])
            await_block(ref(name, "_all").at[origin + 1 - yl, half(core)], ref("far_", name, "_r").at[k])
        weight_copy(name, "mate_", 0).start()

    def weight_ready(name):
        await_block(ref(name, "_all").at[:, half(1 - core)], ref("mate_", name, "_r").at[0])

    weight_own("wq")
    loop(8, lambda k: small_to(k).start(), 1)
    for k in (1, 3, 2):
        tok_to(k).start()
    r.small_all[:, columns_of(s)] = r.small[...]
    r.tok_all[z] = r.tok[...]
    weight_far("wq")

    sub = lax.broadcasted_iota(jnp.int32, (64, 128), 0)

    def set_places(k):
        pair = r.block_pairs[k]
        block = jnp.where(sub < 32, pair, 31 - pair)
        r.places[pl.ds(pick(k, 64), 64), :] = (block * 32 + lax.rem(sub, 32)).astype(F32)

    loop(16, set_places)
    loop(
        8,
        lambda k: await_block(r.small_all.at[:, columns_of(lax.rem(s - k + 8, 8))], r.sm_r.at[k]),
        1,
    )
    weight_across("wq")
    for copy in own[3:]:
        copy.wait()
    weight_own("wo")

    gain_one, bias_one = r.small_all[0:1, :], r.small_all[1:2, :]
    head_cols = pl.ds(pick(z, 256), 256)
    bias_qkv = (r.small_all[2:3, head_cols], None, r.small_all[3:4, head_cols])

    def parts_to(m, origin):
        peer = lax.rem(q4 + m, 4)
        return remote(
            r.qkv.at[peer, origin],
            r.parts.at[origin, q4],
            r.qa_s.at[4 * m + origin],
            r.qa_r.at[4 * m + origin],
            (4 * z + peer, s),
        )

    def norm_block(origin):
        normed, _ = norm_rows(r.tok_all[origin].astype(F32))
        r.attn_all[origin] = (normed * gain_one + bias_one).astype(BF16)

    norm_block(z)
    weight_ready("wq")

    def hop_of(k):
        return k + (k // 2) * (1 - 2 * lax.rem(k, 2))

    def qkv_block(k):
        hop = hop_of(k)
        origin = lax.rem(z - hop + 4, 4)

        @pl.when(k > 0)
        def _():
            await_block(r.tok_all.at[origin], r.tk_r.at[hop])
            norm_block(origin)

        for t in range(3):
            cols = slice(t * 256, t * 256 + 256)
            acc = dot(r.attn_all[origin], r.wq_all[:, :, cols].reshape(1024, 256))
            if bias_qkv[t] is not None:
                acc = acc + bias_qkv[t]
            acc = acc.astype(BF16)
            for j in range(2):
                for p in range(2):
                    r.qkv[j * 2 + p, origin, :, t * 128 : t * 128 + 128] = acc[
                        j * 64 : j * 64 + 64, p * 128 : p * 128 + 128
                    ]
        for m in (1, 2, 3):
            parts_to(m, origin).start()
        r.parts[origin, q4] = r.qkv[q4, origin]

    loop(4, qkv_block)
    weight_far("wo")
    for k in (1, 3, 2):
        cot_to(k).start()
    weight_own("w1")

    def parts_arrived(k):
        m = 1 + k // 4
        origin = lax.rem(k, 4)
        await_block(r.parts.at[origin, lax.rem(q4 - m + 4, 4)], r.qa_r.at[4 * m + origin])

    loop(12, parts_arrived)
    weight_far("w1")
    weight_own("w2")

    length = jnp.where(yh == 0, r.lengths[0], r.lengths[1]).astype(F32)
    head_lane = lax.broadcasted_iota(jnp.int32, (1, 128), 1) // 64
    value_t = r.parts[:, :, :, 256:384].reshape(1024, 128).T

    def masked(rows, h):
        return jnp.where(head_lane == h, rows, jnp.zeros_like(rows))

    def attend(i):
        keys = r.parts[:, :, :, 128:256].reshape(1024, 128)
        key_place = r.places[:, 0:1]
        query_place = r.places[pl.ds(pick(i, 256), 256), :].T[0:1, :]
        allowed = (key_place < length) & (key_place <= query_place)
        queries = r.parts[i, :, :, 0:128].reshape(256, 128) * jnp.asarray(0.125, BF16)
        cols = pl.ds(pick(i, 256), 256)
        for h in range(2):
            scores = jnp.where(allowed, dot_nt(keys, masked(queries, h)), negative)
            powers = jnp.exp(scores - jnp.max(scores, axis=0, keepdims=True))
            low = (powers * (1.0 / jnp.sum(powers, axis=0, keepdims=True))).astype(BF16)
            r.probs[h, :, cols] = low
            r.mix_t[h * 64 : h * 64 + 64, cols] = dot(value_t[h * 64 : h * 64 + 64], low)

    loop(4, attend)
    r.mixed[...] = r.mix_t[...].T.astype(BF16).reshape(16, 64, 128)

    def pair_columns(which):
        return columns_of(which // 4 * 2 + lax.rem(which, 2))

    def slot_of(which):
        return lax.rem(which // 2, 2)

    def mix_to(k):
        peer = lax.rem(c + k, 16)
        return remote(
            r.mixed.at[peer], r.mix_rows.at[yh, :, pair_columns(c)], r.mx_s.at[k], r.mx_r.at[k], (peer, s)
        )

    loop(16, lambda k: mix_to(k).start(), 1)
    r.mix_rows[yh, :, pair_columns(c)] = r.mixed[c]
    weight_far("w2")
    weight_across("wo")
    weight_across("w1")
    weight_ready("wo")

    def mix_arrived(k):
        origin = lax.rem(c - k + 16, 16)
        await_block(r.mix_rows.at[slot_of(origin), :, pair_columns(origin)], r.mx_r.at[k])

    loop(16, mix_arrived, 1)

    mix = r.mix_rows[...].reshape(128, 1024)
    hidden = r.tok[...].astype(F32) + (dot(mix, r.wo_all[...].reshape(1024, 1024)) + r.small_all[4:5, :])
    r.hidden[...] = hidden
    normed, _ = norm_rows(hidden)
    r.mlp_all[z] = (normed * r.small_all[5:6, :] + r.small_all[6:7, :]).astype(BF16)

    def mlp_to(k):
        return remote(r.mlp_all.at[z], r.mlp_all.at[z], r.ml_s.at[k], r.ml_r.at[k], z_peer(k))

    for k in (1, 3, 2):
        mlp_to(k).start()
    weight_across("w2")
    weight_ready("w1")
    weight_ready("w2")

    r.vec[...] = jnp.zeros_like(r.vec)
    up_row = pl.ds(8 + z, 1)
    upper = lax.broadcasted_iota(jnp.int32, (128, 1), 0) < 64
    row_length = jnp.where(upper, r.lengths[0], r.lengths[1]).astype(F32)

    def valid_of(origin):
        mine = r.places[half(origin * 4 + q4), 0:1]
        return (jnp.concatenate([mine, mine], axis=0) < row_length).astype(F32)

    def part_to(out, into, sems, k):
        return remote(out.at[lax.rem(z + k, 4)], into.at[k], sems[0].at[k], sems[1].at[k], z_peer(k))

    gm_sems, mo_sems, ga_sems = (r.gm_s, r.gm_r), (r.mo_s, r.mo_r), (r.ga_s, r.ga_r)

    def mlp_block(k):
        hop = hop_of(k)
        origin = lax.rem(z - hop + 4, 4)

        @pl.when(k > 0)
        def _():
            await_block(r.mlp_all.at[origin], r.ml_r.at[hop])
            await_block(r.cot_all.at[origin], r.ct_r.at[hop])

        r.cot_all[origin] = (r.cot_all[origin].astype(F32) * valid_of(origin)).astype(BF16)
        for i in range(4):
            cols = slice(i * 256, i * 256 + 256)
            pre = dot(r.mlp_all[origin], r.w1_all[:, :, cols].reshape(1024, 256)) + r.small_all[up_row, cols]
            spread = 0.5 * (1.0 + lax.erf(pre * 0.7071067811865476))
            r.act_all[origin, :, cols] = (pre * spread).astype(BF16)
            slope = spread + pre * (0.3989422804014327 * jnp.exp(-0.5 * pre * pre))
            grad = dot_nt(r.cot_all[origin], r.w2_all[2 * i : 2 * i + 2].reshape(256, 1024)) * slope
            r.vec[up_row, cols] += jnp.sum(grad, axis=0, keepdims=True)
            r.gp_all[origin, :, cols] = grad.astype(BF16)
        for i in range(4):
            cols = slice(i * 256, i * 256 + 256)
            part = dot_nt(r.gp_all[origin], r.w1_all[2 * i : 2 * i + 2].reshape(256, 1024))
            r.gm_out[origin, :, cols] = part.astype(BF16)

            @pl.when(k == 0)
            def _():
                r.gm_own[:, cols] = part

        @pl.when(k > 0)
        def _():
            part_to(r.gm_out, r.gm_in, gm_sems, 4 - hop).start()

        for i in range(4):
            cols = slice(i * 256, i * 256 + 256)
            part = dot(r.act_all[origin], r.w2_all[:, :, cols].reshape(1024, 256))
            r.mo_out[origin, :, cols] = part.astype(BF16)

            @pl.when(k == 0)
            def _():
                r.mo_own[:, cols] = part

    loop(4, mlp_block)
    for k in (1, 3, 2):
        part_to(r.mo_out, r.mo_in, mo_sems, k).start()

    def outer(name, left, right, width):
        into = ref("g_", name)

        def body(i):
            rows = pl.ds(pick(i, 256), 256)
            part = dot_tn(left[:, :, rows].reshape(512, 256), right[...].reshape(512, width))
            into[pl.ds(2 * i, 2)] = part.astype(BF16).reshape(2, 2, 64, width)

        loop(4, body)

    def near_to(which):
        name = GRADS[which][0]
        return remote(
            ref("g_", name).at[:, 1 - core], ref("n_", name), r.ns_s.at[which], r.ns_r.at[which], sib
        )

    def y_peer(k):
        yh_to, yl_to = (1 - yh if k // 2 else yh), (1 - yl if k % 2 else yl)
        return (c + 2 * (yh_to - yh), s + yl_to - yl), 2 * yh_to + yl_to

    here = {"x": x, "y": 2 * yh + yl}
    order = {"two": "xy", "one": "yx", "out": "xy", "qkv": "xy"}

    def peer_of(axis, k):
        return (x_peer(k), lax.rem(x + k, 4)) if axis == "x" else y_peer(k)

    def first_to(name, k):
        device, index = peer_of(order[name][0], k)
        sems = ref("first_", name, "_s"), ref("first_", name, "_r")
        return remote(ref("a_", name).at[index], ref("b_", name).at[k], sems[0].at[k], sems[1].at[k], device)

    def second_to(name, k):
        device, index = peer_of(order[name][1], k)
        sems = ref("second_", name, "_s"), ref("second_", name, "_r")
        return remote(ref("m_", name).at[index], ref("h_", name).at[k], sems[0].at[k], sems[1].at[k], device)

    def pair_sum(which):
        name = GRADS[which][0]
        grad, near, into = ref("g_", name), ref("n_", name), ref("a_", name)
        await_block(near, r.ns_r.at[which])

        def add(j):
            y_to = lax.rem(j, 2) * 2 + j // 4
            for xh in range(2):
                x_to = 2 * xh + lax.rem(j // 2, 2)
                rows = slice(32 * xh, 32 * xh + 32)
                total = near[j, rows].astype(F32) + grad[j, core, rows].astype(F32)
                target = (x_to, y_to) if order[name] == "xy" else (y_to, x_to)
                into[target[0], target[1]] = total.astype(BF16)

        loop(8, add)
        for k in (1, 3, 2):
            first_to(name, k).start()

    def first_sum(name):
        mine, others, into = ref("a_", name), ref("b_", name), ref("m_", name)
        for k in (1, 3, 2):
            await_block(others.at[k], ref("first_", name, "_r").at[k])

        def add(j):
            total = mine[here[order[name][0]], j].astype(F32)
            for k in (1, 2, 3):
                total = total + others[k, j].astype(F32)
            into[j] = total.astype(BF16)

        loop(4, add)
        for k in (1, 3, 2):
            second_to(name, k).start()

    def second_sum(name):
        mine, others = ref("m_", name), ref("h_", name)
        for k in (1, 3, 2):
            await_block(others.at[k], ref("second_", name, "_r").at[k])
        total = mine[here[order[name][1]]].astype(F32)
        for k in (1, 2, 3):
            total = total + others[k].astype(F32)
        ref("s_", name)[...] = total

    outer("two", r.act_all, r.cot_all, 1024)
    near_to(0).start()
    outer("one", r.mlp_all, r.gp_all, 1024)
    near_to(1).start()

    total = r.gm_own[...]
    for k in (1, 3, 2):
        await_block(r.gm_in.at[k], r.gm_r.at[k])
        total = total + r.gm_in[k].astype(F32)
    normed, inverse = norm_rows(r.hidden[...])
    grad_out = r.cot_all[z].astype(F32)
    grad_hidden = grad_out + norm_back(total, normed, inverse, r.small_all[5:6, :])
    r.grad_hidden[...] = grad_hidden
    r.hidden_low[...] = grad_hidden.astype(BF16)
    for i, rows in enumerate((grad_hidden, total * normed, total, grad_out)):
        r.vec[i : i + 1, :] = jnp.sum(rows, axis=0, keepdims=True)
    for i in range(4):
        part = dot_nt(r.hidden_low[...], r.wo_all[2 * i : 2 * i + 2].reshape(256, 1024))
        r.gmix[:, :, i * 256 : i * 256 + 256] = part.astype(BF16).reshape(2, 64, 256)

    def gmix_to(k):
        peer = lax.rem(c + k, 16)
        return remote(
            r.gmix.at[slot_of(peer), :, pair_columns(peer)], r.gmixed.at[c], r.mf_s.at[k], r.mf_r.at[k], (peer, s)
        )

    loop(16, lambda k: gmix_to(k).start(), 1)
    r.gmixed[c] = r.gmix[yh, :, pair_columns(c)]

    def out_rows(i):
        rows = pl.ds(pick(i, 256), 256)
        part = dot_tn(r.mix_rows[:, :, rows].reshape(128, 256), r.hidden_low[...])
        r.g_out[pl.ds(2 * i, 2)] = part.astype(BF16).reshape(2, 2, 64, 1024)

    pair_sum(0)
    pair_sum(1)
    loop(4, out_rows)
    near_to(2).start()
    loop(16, lambda k: await_block(r.gmixed.at[lax.rem(c - k + 16, 16)], r.mf_r.at[k]), 1)

    def back_to(m, piece):
        peer = lax.rem(q4 + m, 4)
        cols = slice(256, 384) if piece else slice(0, 256)
        return remote(
            r.gparts.at[:, peer, :, cols],
            r.gback.at[q4, :, :, cols],
            r.hb_s.at[4 * piece + m],
            r.hb_r.at[4 * piece + m],
            (4 * z + peer, s),
        )

    def values_back(i):
        gm = r.gmixed[...].reshape(1024, 128)
        rows = pl.ds(pick(i, 256), 256)
        acc = dot(r.probs[0, rows], masked(gm, 0)) + dot(r.probs[1, rows], masked(gm, 1))
        r.gparts[i, :, :, 256:384] = acc.astype(BF16).reshape(4, 64, 128)
        return jnp.sum(acc, axis=0, keepdims=True)

    bias_v = lax.fori_loop(0, 4, lambda i, acc: acc + values_back(i), jnp.zeros((1, 128), F32))
    for m in (1, 2, 3):
        back_to(m, 1).start()
    products = r.gmixed[...].reshape(1024, 128).astype(F32).T * r.mix_t[...]
    for h in range(2):
        r.delta[h : h + 1, :] = jnp.sum(products[h * 64 : h * 64 + 64], axis=0, keepdims=True)
    keys_t = r.parts[:, :, :, 128:256].reshape(1024, 128).T

    def scores_back(i):
        cols = pl.ds(pick(i, 256), 256)
        values = r.parts[:, :, :, 256:384].reshape(1024, 128)
        gm = r.gmixed[pl.ds(i * 4, 4)].reshape(256, 128)
        for h in range(2):
            grad = dot_nt(values, masked(gm, h)) - r.delta[h : h + 1, cols]
            low = (r.probs[h, :, cols].astype(F32) * grad).astype(BF16)
            r.probs[h, :, cols] = low
            r.gq_t[h * 64 : h * 64 + 64, cols] = dot(keys_t[h * 64 : h * 64 + 64], low)

    loop(4, scores_back)

    def keys_back(i):
        queries = r.parts[:, :, :, 0:128].reshape(1024, 128) * jnp.asarray(0.125, BF16)
        rows = pl.ds(pick(i, 256), 256)
        acc = dot(r.probs[0, rows], masked(queries, 0)) + dot(r.probs[1, rows], masked(queries, 1))
        r.gparts[i, :, :, 128:256] = acc.astype(BF16).reshape(4, 64, 128)

    loop(4, keys_back)
    gq = r.gq_t[...].T * 0.125
    r.gparts[:, :, :, 0:128] = gq.astype(BF16).reshape(4, 4, 64, 128)
    for m in (1, 2, 3):
        back_to(m, 0).start()
    r.gback[q4] = r.gparts[:, q4]
    wide = lax.broadcasted_iota(jnp.int32, (1, 1024), 1) // 128 == 2 * z + core
    for i, sums in ((4, jnp.sum(gq, axis=0, keepdims=True)), (5, bias_v)):
        r.vec[i : i + 1, :] = jnp.where(wide, jnp.concatenate([sums] * 8, axis=1), 0.0)

    pair_sum(2)
    first_sum("two")
    first_sum("one")
    total = r.mo_own[...] + r.small_all[7:8, :]
    for k in (1, 3, 2):
        await_block(r.mo_in.at[k], r.mo_r.at[k])
        total = total + r.mo_in[k].astype(F32)
    r.layer_out[...] = (valid_of(z) * (r.hidden[...] + total)).astype(BF16)
    for m in (1, 2, 3):
        for piece, cols in ((1, slice(256, 384)), (0, slice(0, 256))):
            await_block(r.gback.at[lax.rem(q4 - m + 4, 4), :, :, cols], r.hb_r.at[4 * piece + m])

    def attn_back(k):
        hop = jnp.where(k == 0, 2, jnp.where(k == 1, 3, jnp.where(k == 2, 1, 0)))
        origin = lax.rem(z + hop, 4)
        for t in range(3):
            for j in range(2):
                for p in range(2):
                    r.gqkv[origin, j * 64 : j * 64 + 64, t * 256 + p * 128 : t * 256 + p * 128 + 128] = r.gback[
                        j * 2 + p, origin, :, t * 128 : t * 128 + 128
                    ]
        normed, _ = norm_rows(r.tok_all[origin].astype(F32))
        for i in range(4):
            cols = slice(i * 256, i * 256 + 256)
            part = dot_nt(r.gqkv[origin], r.wq_all[2 * i : 2 * i + 2].reshape(256, 768))
            r.ga_out[origin, :, cols] = part.astype(BF16)
            r.vec[6:7, cols] += jnp.sum(part * normed[:, cols], axis=0, keepdims=True)
            r.vec[7:8, cols] += jnp.sum(part, axis=0, keepdims=True)

            @pl.when(k == 3)
            def _():
                r.ga_own[:, cols] = part

        @pl.when(k < 3)
        def _():
            part_to(r.ga_out, r.ga_in, ga_sems, hop).start()

    loop(4, attn_back)
    vec_across = remote(r.vec, r.vec_sib, r.ns_s.at[4], r.ns_r.at[4], sib)
    vec_across.start()
    outer("qkv", r.attn_all, r.gqkv, 768)
    near_to(3).start()
    await_block(r.vec_sib, r.ns_r.at[4])
    vec_across.wait_send()
    r.vec[...] += r.vec_sib[...]
    chip = c // 2

    def vec_to(k):
        peer = lax.rem(chip + k, 8)
        return remote(r.vec.at[:, columns_of(peer)], r.vec_in.at[k], r.v1_s.at[k], r.v1_r.at[k], (2 * peer + core, s))

    loop(8, lambda k: vec_to(k).start(), 1)
    pair_sum(3)

    my_part = pl.ds(pick(lax.rem(x, 2) * 2 + yl, 8), 8)

    def last_to(name, k):
        rows = slice(8 * k, 8 * k + 8)
        sems = ref("last_", name, "_s"), ref("last_", name, "_r")
        device = (to_z * 4 + q4, 2 * (x // 2 * 2 + k // 2) + k % 2)
        return remote(ref("s_", name).at[rows], ref("r_", name).at[z], sems[0].at[k], sems[1].at[z], device)

    def at_owner(k):
        return at_home & (lax.rem(x, 2) == k // 2) & (yl == k % 2)

    def spread(name):
        for k in range(4):
            not_when(at_owner(k), lambda: last_to(name, k).start())

        @pl.when(at_home)
        def _():
            ref("r_", name)[z] = ref("s_", name)[my_part]

    def two_copy():
        return remote(r.s_two, r.r_two, r.last_two_s.at[0], r.last_two_r.at[0], two_to)

    second_sum("two")
    not_when(two_stays, lambda: two_copy().start())

    @pl.when(two_stays)
    def _():
        r.r_two[...] = r.s_two[...]

    second_sum("one")
    spread("one")
    first_sum("out")

    loop(8, lambda k: await_block(r.vec_in.at[k], r.v1_r.at[k]), 1)
    sums = r.vec[:, columns_of(chip)]
    for k in range(1, 8):
        sums = sums + r.vec_in[k]
    r.vec_sum[...] = sums

    def vec_rows_to(k):
        return remote(r.vec_sum, r.vec_all.at[s], r.v2_s.at[k], r.v2_r.at[k], (c, lax.rem(s + k, 8)))

    loop(8, lambda k: vec_rows_to(k).start(), 1)
    r.vec_all[s] = sums
    first_sum("qkv")
    second_sum("out")
    spread("out")

    total = r.ga_own[...]
    for k in (1, 3, 2):
        await_block(r.ga_in.at[k], r.ga_r.at[k])
        total = total + r.ga_in[k].astype(F32)
    normed, inverse = norm_rows(r.tok[...].astype(F32))
    r.input_grad[...] = (
        r.grad_hidden[...] + norm_back(total, normed, inverse, r.small_all[0:1, :])
    ).astype(BF16)

    second_sum("qkv")
    spread("qkv")

    def rows_arrived(name):
        into = ref("r_", name)
        for k in range(4):
            not_when(at_home & (z == k), lambda: await_block(into.at[k], ref("last_", name, "_r").at[k]))

    not_when(two_stays, lambda: await_block(r.r_two, r.last_two_r.at[0]))
    r.o_two[...] = r.r_two[...]
    rows_arrived("one")
    for i in range(4):
        for t in range(8):
            r.o_one[:, t * 512 + i * 128 : t * 512 + i * 128 + 128] = r.r_one[i, :, t * 128 : t * 128 + 128]
    rows_arrived("out")
    r.o_out[...] = (r.r_out[0] + r.r_out[1]) + (r.r_out[2] + r.r_out[3])
    loop(8, lambda k: await_block(r.vec_all.at[lax.rem(s - k + 8, 8)], r.v2_r.at[k]), 1)
    total = r.vec_all[0]
    for i in range(1, 8):
        total = total + r.vec_all[i]
    r.o_vec[...] = total
    rows_arrived("qkv")
    for i in range(4):
        for t in range(3):
            r.o_qkv[:, t * 1024 + i * 256 : t * 1024 + i * 256 + 256] = r.r_qkv[i, :, t * 256 : t * 256 + 256]

    def sent(k):
        small_to(k).wait_send()
        vec_to(k).wait_send()
        vec_rows_to(k).wait_send()

    loop(8, sent, 1)
    for k in range(1, 4):
        for copy in (tok_to(k), cot_to(k), mlp_to(k)):
            copy.wait_send()
        part_to(r.gm_out, r.gm_in, gm_sems, k).wait_send()
        part_to(r.mo_out, r.mo_in, mo_sems, k).wait_send()
        part_to(r.ga_out, r.ga_in, ga_sems, k).wait_send()
        for name, _ in WEIGHTS:
            weight_copy(name, "own_", k).wait_send()
            weight_copy(name, "far_", k).wait_send()
        for name, _ in GRADS:
            first_to(name, k).wait_send()
            second_to(name, k).wait_send()
        for piece in range(2):
            back_to(k, piece).wait_send()
        for origin in range(4):
            parts_to(k, origin).wait_send()
    for name, _ in WEIGHTS:
        weight_copy(name, "mate_", 0).wait_send()
        weight_copy(name, "mate_", 1).wait_send()
    for which in range(4):
        near_to(which).wait_send()
    for name in ("one", "out", "qkv"):
        for k in range(4):
            not_when(at_owner(k), lambda: last_to(name, k).wait_send())
    not_when(two_stays, lambda: two_copy().wait_send())
    loop(16, lambda k: mix_to(k).wait_send(), 1)
    loop(16, lambda k: gmix_to(k).wait_send(), 1)


def named_call(kernel, name, cid, ins, outs, scratch, operands):
    results = pl.pallas_call(
        kernel,
        name=name,
        out_shape=[jax.ShapeDtypeStruct(shape, dtype) for _, _, shape, dtype in outs],
        in_specs=[pl.BlockSpec(memory_space=space) for _, space in ins],
        out_specs=[pl.BlockSpec(memory_space=space) for _, space, _, _ in outs],
        scratch_shapes=[kind for _, kind in scratch],
        compiler_params=pltpu.CompilerParams(
            collective_id=cid, has_side_effects=True, vmem_limit_bytes=60 << 20
        ),
    )(*[operands[name] for name, _ in ins])
    return SimpleNamespace(**dict(zip([o[0] for o in outs], results, strict=True)))


def shards(
    tokens,
    lengths,
    block_pairs,
    ln1_gain,
    ln1_bias,
    w_qkv,
    query_bias,
    value_bias,
    w_out,
    out_bias,
    ln2_gain,
    ln2_bias,
    w_fc1,
    fc1_bias,
    w_fc2,
    fc2_bias,
    out_cotangent,
):
    c, s = lax.axis_index("ctx"), lax.axis_index("shard")
    f = named_call(
        layer_kernel,
        "layer",
        0,
        LAYER_IN,
        LAYER_OUT,
        LAYER_SCRATCH,
        dict(
            lengths=lengths,
            block_pairs=block_pairs,
            tok=tokens.reshape(128, 1024),
            ln1_gain=ln1_gain.reshape(1, 128),
            ln1_bias=ln1_bias.reshape(1, 128),
            query_bias=query_bias.reshape(1, 128),
            value_bias=value_bias.reshape(1, 128),
            out_bias=out_bias.reshape(1, 128),
            ln2_gain=ln2_gain.reshape(1, 128),
            ln2_bias=ln2_bias.reshape(1, 128),
            fc2_bias=fc2_bias.reshape(1, 128),
            fc1_bias=fc1_bias.reshape(4, 128),
            w_qkv=w_qkv,
            w_out=w_out,
            w_fc1=w_fc1,
            w_fc2=w_fc2,
            cot=out_cotangent.reshape(128, 1024),
        ),
    )
    mine = lax.dynamic_slice(f.o_vec, (0, (c % 2) * 64 + s * 8), (8, 8))
    up = lax.dynamic_slice(f.o_vec, (8 + c % 2 * 2 + s // 4, (s % 4) * 32), (1, 32))[0]
    return (
        f.layer_out.reshape(tokens.shape),
        f.input_grad.reshape(tokens.shape),
        mine[6],
        mine[7],
        f.o_qkv,
        mine[4],
        mine[5],
        f.o_out,
        mine[0],
        mine[1],
        mine[2],
        f.o_one,
        up,
        f.o_two,
        mine[3],
    )


def solution(mesh):
    one, both = P("shard"), P(("ctx", "shard"))
    rows, both_rows = P("shard", None), P(("ctx", "shard"), None)
    whole = P("ctx", "shard", None, None)
    return jax.shard_map(
        shards,
        mesh=mesh,
        in_specs=(
            whole, one, P(), one, one, rows, one, one, rows, one, one, one, rows, one, rows, one, whole,
        ),
        out_specs=(
            whole, whole, both, both, both_rows, both, both, both_rows, both, both, both,
            both_rows, both, both_rows, both,
        ),
        check_vma=False,
    )
```

time: 219 us -> 160 us (0.73)
  Pallas kernels: 210 us -> 152 us
    pallas_call x1, Pallas kernels: 210 us -> 152 us  [named_call(): pl.pallas_call(kernel, name=name, out_shape=[jax.ShapeDtypeStruct(shape,...]
where the time goes in v4:
time: 160 us
  Pallas kernels  152 us (95%)
  local copies, waits for them, and re-layouts  7.6 us (5%)
    pallas_call x1, Pallas kernels, named_call(): pl.pallas_call(kernel, name=name, out_shape=[jax.ShapeDtypeStruct(shape,...  152 us
    unnamed x18, local copies, waits for them, and re-layouts  5.66 us

profile of v4, /device:TPU:0, one launch (start us, length us, event | category | flops | bytes accessed | tf_op | source)
XLA Modules:
  0.0 159.9 jit_solution(12327557771543627896)
XLA Ops:
  0.7 151.6 %layer.1 = (bf16[128,1024]{1,0:T(8,128)(2,1)}, bf16[128,1024]{1,0:T(8,128)(2,1)}, f32[8,3072]{1,0:T(8,128)}, f32[8,1024]{1,0:T(8,128)}, f32[8,4096]{1,0:T(8,128)...) custom-call(s32[2]{0:T(128)} %refs_0_.1, s32[16]{0:T(128)} %refs_1_.1, bf16[128,1024]{1,0:T(8,128)(2,1)} %bitcast.33, ...), custom_call_target="tpu_custom_call" | custom-call | tf_op jit(solution)/shard_map/layer/pallas_call | solution.py:827
  152.3 0.0 copy-start.5
  152.3 1.3 dynamic-slice_bitcast_fusion
  153.6 0.0 copy-done.5
  153.6 0.1 constant_dynamic-slice_fusion
  153.7 0.5 slice_bitcast_fusion
  154.2 0.0 copy-start
  154.2 1.7 %copy.38 = bf16[1,2,64,1024]{3,2,1,0:T(8,128)(2,1)} copy(bf16[1,2,64,1024]{3,2,1,0:T(8,128)(2,1)} %bitcast.32) | data formatting | bytes 524288
  155.9 0.0 copy-done
  156.0 0.0 copy-start.3
  156.0 0.7 copy.39
  156.7 0.3 copy-done.3
  156.9 0.0 copy-start.4
  156.9 0.0 copy-start.2
  156.9 0.6 copy.40
  157.6 0.1 copy-done.4
  157.7 0.6 copy.41
  158.3 0.0 copy-done.2
  158.3 0.0 copy-start.1
  158.3 0.7 copy.42
  158.9 0.3 copy-done.1
  159.2 0.7 copy.43
Async XLA Ops:
  152.3 1.3 copy-start.5
  154.2 1.7 %copy-start = (bf16[128,1024]{1,0:T(8,128)(2,1)S(1)}, bf16[128,1024]{1,0:T(8,128)(2,1)}, u32[]{:S(2)}) copy-start(bf16[128,1024]{1,0:T(8,128)(2,1)} %get-tuple-element.23) | copy-start | bytes 786436
  156.0 1.0 copy-start.3
  156.9 0.8 copy-start.4
  156.9 1.4 copy-start.2
  158.3 1.0 copy-start.1

commit v5 on v4

--- a/solution.py
+++ b/solution.py
@@ -86,7 +86,7 @@
 LAYER_IN = (
     ("lengths", pltpu.SMEM),
     ("block_pairs", pltpu.SMEM),
-    ("tok", VMEM),
+    ("tok", ANY),
     *[(name, VMEM) for name in VECTORS],
     ("fc1_bias", VMEM),
     ("w_qkv", ANY),
@@ -97,17 +97,17 @@
 )
 
 LAYER_OUT = (
-    ("layer_out", VMEM, (128, 1024), BF16),
-    ("input_grad", VMEM, (128, 1024), BF16),
-    ("o_qkv", VMEM, (8, 3072), F32),
-    ("o_out", VMEM, (8, 1024), F32),
-    ("o_one", VMEM, (8, 4096), F32),
-    ("o_two", VMEM, (32, 1024), F32),
-    ("o_vec", VMEM, (16, 128), F32),
+    ("layer_out", ANY, (128, 1024), BF16),
+    ("input_grad", ANY, (128, 1024), BF16),
+    ("o_qkv", ANY, (8, 3072), F32),
+    ("o_out", ANY, (8, 1024), F32),
+    ("o_one", ANY, (8, 4096), F32),
+    ("o_two", ANY, (32, 1024), F32),
+    ("o_vec", ANY, (16, 128), F32),
 )
 
 WEIGHTS = (("wq", 768), ("wo", 1024), ("w1", 1024), ("w2", 1024))
-GRADS = (("two", 1024), ("one", 1024), ("out", 1024), ("qkv", 768))
+GRADS = (("two", 1024), ("one", 1024), ("out", 1024), ("qka", 384), ("qkb", 384))
 
 LAYER_SCRATCH = (
     *[(name + "_all", pltpu.VMEM((8, 128, width), BF16)) for name, width in WEIGHTS],
@@ -129,7 +129,8 @@
             ("gm_out", (4, 128, 1024)), ("mo_out", (4, 128, 1024)), ("gm_in", (4, 128, 1024)),
             ("mo_in", (4, 128, 1024)), ("hidden_low", (128, 1024)), ("gmix", (2, 64, 1024)),
             ("gmixed", (16, 64, 128)), ("gparts", (4, 4, 64, 384)), ("gback", (4, 4, 64, 384)),
-            ("gqkv", (4, 128, 768)), ("ga_out", (4, 128, 1024)), ("ga_in", (4, 128, 1024)),
+            ("gqkv", (4, 128, 768)), ("ga_out", (4, 128, 1024)), ("ga_in", (4, 128, 1024)), ("ga_via", (4, 64, 1024)),
+            ("w_layer", (128, 1024)), ("w_input", (128, 1024)),
         )
     ],
     *[
@@ -138,7 +139,9 @@
             ("small", (16, 128)), ("small_all", (16, 1024)), ("places", (1024, 128)), ("mix_t", (128, 1024)),
             ("hidden", (128, 1024)), ("gm_own", (128, 1024)), ("mo_own", (128, 1024)),
             ("grad_hidden", (128, 1024)), ("ga_own", (128, 1024)), ("gq_t", (128, 1024)), ("delta", (2, 1024)),
-            ("r_two", (32, 1024)), ("r_one", (4, 8, 1024)), ("r_out", (4, 8, 1024)), ("r_qkv", (4, 8, 768)),
+            ("r_two", (32, 1024)), ("r_one", (4, 8, 1024)), ("r_out", (4, 8, 1024)), ("r_qka", (4, 8, 384)),
+            ("r_qkb", (4, 8, 384)), ("w_qkv_out", (8, 3072)), ("w_out_out", (8, 1024)), ("w_one_out", (8, 4096)),
+            ("w_vec_out", (16, 128)),
             ("vec", (16, 1024)), ("vec_sib", (16, 1024)), ("vec_in", (8, 16, 128)), ("vec_sum", (16, 128)),
             ("vec_all", (8, 16, 128)),
         )
@@ -158,8 +161,8 @@
     *[
         (name + end, pltpu.SemaphoreType.DMA((count,)))
         for name, count in (
-            ("local", 16), ("sm", 8), ("tk", 4), ("qa", 16), ("mx", 16), ("ct", 4), ("ml", 4), ("gm", 4), ("mo", 4),
-            ("mf", 16), ("hb", 16), ("ga", 4), ("ns", 8), ("v1", 8), ("v2", 8),
+            ("local", 16), ("done", 8), ("sm", 8), ("tk", 4), ("tf", 4), ("qa", 16), ("mx", 16), ("ct", 4), ("ml", 4),
+            ("mg", 4), ("gm", 4), ("mo", 4), ("mf", 16), ("hb", 48), ("ga", 4), ("gv", 4), ("ns", 8), ("v1", 8), ("v2", 8),
         )
         for end in ("_s", "_r")
     ],
@@ -191,8 +194,7 @@
         pltpu.make_async_copy(r.w_fc2.at[half(2 * z + core)], r.w2_all.at[s, half(core)], r.local_s.at[12])
     )
     own.append(pltpu.make_async_copy(r.cot, r.cot_all.at[z], r.local_s.at[13]))
-    for copy in own:
-        copy.start()
+    own.append(pltpu.make_async_copy(r.tok, r.tok_all.at[z], r.local_s.at[14]))
 
     barrier = pltpu.get_barrier_semaphore()
 
@@ -212,6 +214,8 @@
     hail((c + 2 - 4 * yh, mate_s))
     loop(4, lambda k: not_when(at_home & (k == z), lambda: hail((k * 4 + q4, 2 * from_x + from_yl))))
     not_when(two_stays, lambda: hail(two_from))
+    for copy in own:
+        copy.start()
 
     for i, name in enumerate(VECTORS):
         r.small[i : i + 1, :] = ref(name)[...].astype(F32)
@@ -239,6 +243,25 @@
     def cot_to(k):
         return remote(r.cot, r.cot_all.at[z], r.ct_s.at[k], r.ct_r.at[k], z_peer(k))
 
+    z_of = lambda hop: lax.rem(z - hop + 4, 4)
+
+    def pass_on(whole, send_sems, recv_sems, k):
+        rows = slice(0, 64) if k == 1 else slice(64, 128)
+        block = whole.at[z_of(k), rows]
+        return remote(block, block, send_sems.at[k], recv_sems.at[k], z_peer(k))
+
+    def ring_arrived(whole, recv_sems, send_next, recv_next, k):
+        @pl.when(k == 1)
+        def _():
+            for j in (1, 3):
+                await_block(whole.at[z_of(j)], recv_sems.at[j])
+                pass_on(whole, send_next, recv_next, j).start()
+
+        @pl.when(k == 3)
+        def _():
+            for j, rows in ((1, slice(0, 64)), (3, slice(64, 128))):
+                await_block(whole.at[z_of(2), rows], recv_next.at[j])
+
     def weight_copy(name, kind, k):
         whole = ref(name, "_all")
         device = (c, mate_s) if kind == "mate_" else x_peer(k)
@@ -267,12 +290,11 @@
     def weight_ready(name):
         await_block(ref(name, "_all").at[:, half(1 - core)], ref("mate_", name, "_r").at[0])
 
+    for k in (1, 3):
+        tok_to(k).start()
     weight_own("wq")
     loop(8, lambda k: small_to(k).start(), 1)
-    for k in (1, 3, 2):
-        tok_to(k).start()
     r.small_all[:, columns_of(s)] = r.small[...]
-    r.tok_all[z] = r.tok[...]
     weight_far("wq")
 
     sub = lax.broadcasted_iota(jnp.int32, (64, 128), 0)
@@ -289,7 +311,7 @@
         1,
     )
     weight_across("wq")
-    for copy in own[3:]:
+    for copy in own[3:14]:
         copy.wait()
     weight_own("wo")
 
@@ -311,6 +333,7 @@
         normed, _ = norm_rows(r.tok_all[origin].astype(F32))
         r.attn_all[origin] = (normed * gain_one + bias_one).astype(BF16)
 
+    own[14].wait()
     norm_block(z)
     weight_ready("wq")
 
@@ -319,11 +342,11 @@
 
     def qkv_block(k):
         hop = hop_of(k)
-        origin = lax.rem(z - hop + 4, 4)
+        origin = z_of(hop)
+        ring_arrived(r.tok_all, r.tk_r, r.tf_s, r.tf_r, k)
 
         @pl.when(k > 0)
         def _():
-            await_block(r.tok_all.at[origin], r.tk_r.at[hop])
             norm_block(origin)
 
         for t in range(3):
@@ -363,7 +386,19 @@
     def masked(rows, h):
         return jnp.where(head_lane == h, rows, jnp.zeros_like(rows))
 
-    def attend(i):
+    def pair_columns(which):
+        return columns_of(which // 4 * 2 + lax.rem(which, 2))
+
+    def slot_of(which):
+        return lax.rem(which // 2, 2)
+
+    def mix_to(peer):
+        return remote(
+            r.mixed.at[peer], r.mix_rows.at[yh, :, pair_columns(c)], r.mx_s.at[peer], r.mx_r.at[c], (peer, s)
+        )
+
+    def attend(k):
+        i = lax.rem(z + k + 1, 4)
         keys = r.parts[:, :, :, 128:256].reshape(1024, 128)
         key_place = r.places[:, 0:1]
         query_place = r.places[pl.ds(pick(i, 256), 256), :].T[0:1, :]
@@ -376,23 +411,12 @@
             low = (powers * (1.0 / jnp.sum(powers, axis=0, keepdims=True))).astype(BF16)
             r.probs[h, :, cols] = low
             r.mix_t[h * 64 : h * 64 + 64, cols] = dot(value_t[h * 64 : h * 64 + 64], low)
+        r.mixed[pl.ds(4 * i, 4)] = r.mix_t[:, cols].T.astype(BF16).reshape(4, 64, 128)
+        for q in range(4):
+            not_when(4 * i + q == c, lambda: mix_to(4 * i + q).start())
 
     loop(4, attend)
-    r.mixed[...] = r.mix_t[...].T.astype(BF16).reshape(16, 64, 128)
-
-    def pair_columns(which):
-        return columns_of(which // 4 * 2 + lax.rem(which, 2))
-
-    def slot_of(which):
-        return lax.rem(which // 2, 2)
-
-    def mix_to(k):
-        peer = lax.rem(c + k, 16)
-        return remote(
-            r.mixed.at[peer], r.mix_rows.at[yh, :, pair_columns(c)], r.mx_s.at[k], r.mx_r.at[k], (peer, s)
-        )
-
-    loop(16, lambda k: mix_to(k).start(), 1)
+
     r.mix_rows[yh, :, pair_columns(c)] = r.mixed[c]
     weight_far("w2")
     weight_across("wo")
@@ -401,12 +425,12 @@
 
     def mix_arrived(k):
         origin = lax.rem(c - k + 16, 16)
-        await_block(r.mix_rows.at[slot_of(origin), :, pair_columns(origin)], r.mx_r.at[k])
+        await_block(r.mix_rows.at[slot_of(origin), :, pair_columns(origin)], r.mx_r.at[origin])
 
     loop(16, mix_arrived, 1)
 
     mix = r.mix_rows[...].reshape(128, 1024)
-    hidden = r.tok[...].astype(F32) + (dot(mix, r.wo_all[...].reshape(1024, 1024)) + r.small_all[4:5, :])
+    hidden = r.tok_all[z].astype(F32) + (dot(mix, r.wo_all[...].reshape(1024, 1024)) + r.small_all[4:5, :])
     r.hidden[...] = hidden
     normed, _ = norm_rows(hidden)
     r.mlp_all[z] = (normed * r.small_all[5:6, :] + r.small_all[6:7, :]).astype(BF16)
@@ -414,7 +438,7 @@
     def mlp_to(k):
         return remote(r.mlp_all.at[z], r.mlp_all.at[z], r.ml_s.at[k], r.ml_r.at[k], z_peer(k))
 
-    for k in (1, 3, 2):
+    for k in (1, 3):
         mlp_to(k).start()
     weight_across("w2")
     weight_ready("w1")
@@ -436,11 +460,11 @@
 
     def mlp_block(k):
         hop = hop_of(k)
-        origin = lax.rem(z - hop + 4, 4)
+        origin = z_of(hop)
+        ring_arrived(r.mlp_all, r.ml_r, r.mg_s, r.mg_r, k)
 
         @pl.when(k > 0)
         def _():
-            await_block(r.mlp_all.at[origin], r.ml_r.at[hop])
             await_block(r.cot_all.at[origin], r.ct_r.at[hop])
 
         r.cot_all[origin] = (r.cot_all[origin].astype(F32) * valid_of(origin)).astype(BF16)
@@ -466,25 +490,26 @@
         def _():
             part_to(r.gm_out, r.gm_in, gm_sems, 4 - hop).start()
 
+    loop(4, mlp_block)
+
+    def mlp_out(origin):
         for i in range(4):
             cols = slice(i * 256, i * 256 + 256)
             part = dot(r.act_all[origin], r.w2_all[:, :, cols].reshape(1024, 256))
             r.mo_out[origin, :, cols] = part.astype(BF16)
 
-            @pl.when(k == 0)
+            @pl.when(origin == z)
             def _():
                 r.mo_own[:, cols] = part
 
-    loop(4, mlp_block)
-    for k in (1, 3, 2):
-        part_to(r.mo_out, r.mo_in, mo_sems, k).start()
-
-    def outer(name, left, right, width):
+    def outer(name, left, right, width, first=0):
         into = ref("g_", name)
 
         def body(i):
             rows = pl.ds(pick(i, 256), 256)
-            part = dot_tn(left[:, :, rows].reshape(512, 256), right[...].reshape(512, width))
+            part = dot_tn(
+                left[:, :, rows].reshape(512, 256), right[:, :, first : first + width].reshape(512, width)
+            )
             into[pl.ds(2 * i, 2)] = part.astype(BF16).reshape(2, 2, 64, width)
 
         loop(4, body)
@@ -500,7 +525,7 @@
         return (c + 2 * (yh_to - yh), s + yl_to - yl), 2 * yh_to + yl_to
 
     here = {"x": x, "y": 2 * yh + yl}
-    order = {"two": "xy", "one": "yx", "out": "xy", "qkv": "xy"}
+    order = {"two": "xy", "one": "yx", "out": "xy", "qka": "xy", "qkb": "yx"}
 
     def peer_of(axis, k):
         return (x_peer(k), lax.rem(x + k, 4)) if axis == "x" else y_peer(k)
@@ -561,6 +586,7 @@
     near_to(0).start()
     outer("one", r.mlp_all, r.gp_all, 1024)
     near_to(1).start()
+    loop(4, mlp_out)
 
     total = r.gm_own[...]
     for k in (1, 3, 2):
@@ -596,28 +622,34 @@
     loop(4, out_rows)
     near_to(2).start()
     loop(16, lambda k: await_block(r.gmixed.at[lax.rem(c - k + 16, 16)], r.mf_r.at[k]), 1)
-
-    def back_to(m, piece):
+    for k in (1, 3, 2):
+        part_to(r.mo_out, r.mo_in, mo_sems, k).start()
+
+    def back_to(m, piece, i):
         peer = lax.rem(q4 + m, 4)
-        cols = slice(256, 384) if piece else slice(0, 256)
+        cols = slice(piece * 128, piece * 128 + 128)
+        sem = 16 * piece + 4 * i + m
         return remote(
-            r.gparts.at[:, peer, :, cols],
-            r.gback.at[q4, :, :, cols],
-            r.hb_s.at[4 * piece + m],
-            r.hb_r.at[4 * piece + m],
+            r.gparts.at[i, peer, :, cols],
+            r.gback.at[q4, i, :, cols],
+            r.hb_s.at[sem],
+            r.hb_r.at[sem],
             (4 * z + peer, s),
         )
+
+    def back_start(piece, i):
+        for m in (1, 2, 3):
+            back_to(m, piece, i).start()
 
     def values_back(i):
         gm = r.gmixed[...].reshape(1024, 128)
         rows = pl.ds(pick(i, 256), 256)
         acc = dot(r.probs[0, rows], masked(gm, 0)) + dot(r.probs[1, rows], masked(gm, 1))
         r.gparts[i, :, :, 256:384] = acc.astype(BF16).reshape(4, 64, 128)
+        back_start(2, i)
         return jnp.sum(acc, axis=0, keepdims=True)
 
     bias_v = lax.fori_loop(0, 4, lambda i, acc: acc + values_back(i), jnp.zeros((1, 128), F32))
-    for m in (1, 2, 3):
-        back_to(m, 1).start()
     products = r.gmixed[...].reshape(1024, 128).astype(F32).T * r.mix_t[...]
     for h in range(2):
         r.delta[h : h + 1, :] = jnp.sum(products[h * 64 : h * 64 + 64], axis=0, keepdims=True)
@@ -632,23 +664,24 @@
             low = (r.probs[h, :, cols].astype(F32) * grad).astype(BF16)
             r.probs[h, :, cols] = low
             r.gq_t[h * 64 : h * 64 + 64, cols] = dot(keys_t[h * 64 : h * 64 + 64], low)
-
-    loop(4, scores_back)
+        gq = r.gq_t[:, cols].T * 0.125
+        r.gparts[i, :, :, 0:128] = gq.astype(BF16).reshape(4, 64, 128)
+        back_start(0, i)
+        return jnp.sum(gq, axis=0, keepdims=True)
+
+    bias_q = lax.fori_loop(0, 4, lambda i, acc: acc + scores_back(i), jnp.zeros((1, 128), F32))
 
     def keys_back(i):
         queries = r.parts[:, :, :, 0:128].reshape(1024, 128) * jnp.asarray(0.125, BF16)
         rows = pl.ds(pick(i, 256), 256)
         acc = dot(r.probs[0, rows], masked(queries, 0)) + dot(r.probs[1, rows], masked(queries, 1))
         r.gparts[i, :, :, 128:256] = acc.astype(BF16).reshape(4, 64, 128)
+        back_start(1, i)
 
     loop(4, keys_back)
-    gq = r.gq_t[...].T * 0.125
-    r.gparts[:, :, :, 0:128] = gq.astype(BF16).reshape(4, 4, 64, 128)
-    for m in (1, 2, 3):
-        back_to(m, 0).start()
     r.gback[q4] = r.gparts[:, q4]
     wide = lax.broadcasted_iota(jnp.int32, (1, 1024), 1) // 128 == 2 * z + core
-    for i, sums in ((4, jnp.sum(gq, axis=0, keepdims=True)), (5, bias_v)):
+    for i, sums in ((4, bias_q), (5, bias_v)):
         r.vec[i : i + 1, :] = jnp.where(wide, jnp.concatenate([sums] * 8, axis=1), 0.0)
 
     pair_sum(2)
@@ -658,20 +691,32 @@
     for k in (1, 3, 2):
         await_block(r.mo_in.at[k], r.mo_r.at[k])
         total = total + r.mo_in[k].astype(F32)
-    r.layer_out[...] = (valid_of(z) * (r.hidden[...] + total)).astype(BF16)
-    for m in (1, 2, 3):
-        for piece, cols in ((1, slice(256, 384)), (0, slice(0, 256))):
-            await_block(r.gback.at[lax.rem(q4 - m + 4, 4), :, :, cols], r.hb_r.at[4 * piece + m])
-
-    def attn_back(k):
-        hop = jnp.where(k == 0, 2, jnp.where(k == 1, 3, jnp.where(k == 2, 1, 0)))
-        origin = lax.rem(z + hop, 4)
+    r.w_layer[...] = (valid_of(z) * (r.hidden[...] + total)).astype(BF16)
+    results = [pltpu.make_async_copy(r.w_layer, r.layer_out, r.done_s.at[0])]
+    results[0].start()
+
+    def back_arrived(i):
+        for m in (1, 2, 3):
+            for piece in (2, 0, 1):
+                await_block(
+                    r.gback.at[lax.rem(q4 - m + 4, 4), i, :, piece * 128 : piece * 128 + 128],
+                    r.hb_r.at[16 * piece + 4 * i + m],
+                )
+
+    loop(4, back_arrived)
+
+    def assemble(origin):
         for t in range(3):
             for j in range(2):
                 for p in range(2):
                     r.gqkv[origin, j * 64 : j * 64 + 64, t * 256 + p * 128 : t * 256 + p * 128 + 128] = r.gback[
                         j * 2 + p, origin, :, t * 128 : t * 128 + 128
                     ]
+
+    loop(4, assemble)
+
+    def attn_back(hop):
+        origin = lax.rem(z + hop, 4)
         normed, _ = norm_rows(r.tok_all[origin].astype(F32))
         for i in range(4):
             cols = slice(i * 256, i * 256 + 256)
@@ -680,20 +725,40 @@
             r.vec[6:7, cols] += jnp.sum(part * normed[:, cols], axis=0, keepdims=True)
             r.vec[7:8, cols] += jnp.sum(part, axis=0, keepdims=True)
 
-            @pl.when(k == 3)
+            @pl.when(hop == 0)
             def _():
                 r.ga_own[:, cols] = part
 
-        @pl.when(k < 3)
-        def _():
-            part_to(r.ga_out, r.ga_in, ga_sems, hop).start()
-
-    loop(4, attn_back)
-    vec_across = remote(r.vec, r.vec_sib, r.ns_s.at[4], r.ns_r.at[4], sib)
+    halves = {1: slice(0, 64), 3: slice(64, 128)}
+
+    def via_to(k):
+        return remote(
+            r.ga_out.at[lax.rem(z + 2, 4), halves[k]], r.ga_via.at[k], r.gv_s.at[k], r.gv_r.at[k], z_peer(k)
+        )
+
+    def via_add(k):
+        await_block(r.ga_via.at[k], r.gv_r.at[k])
+        target = lax.rem(z + k, 4)
+        total = r.ga_out[target, halves[k]].astype(F32) + r.ga_via[k].astype(F32)
+        r.ga_out[target, halves[k]] = total.astype(BF16)
+        part_to(r.ga_out, r.ga_in, ga_sems, k).start()
+
+    attn_back(2)
+    via_to(1).start()
+    via_to(3).start()
+    outer("qka", r.attn_all, r.gqkv, 384)
+    near_to(3).start()
+    outer("qkb", r.attn_all, r.gqkv, 384, 384)
+    near_to(4).start()
+    loop(2, lambda k: attn_back(1 + 2 * k))
+    via_add(1)
+    via_add(3)
+    pair_sum(3)
+    pair_sum(4)
+    attn_back(0)
+    vec_across = remote(r.vec, r.vec_sib, r.ns_s.at[5], r.ns_r.at[5], sib)
     vec_across.start()
-    outer("qkv", r.attn_all, r.gqkv, 768)
-    near_to(3).start()
-    await_block(r.vec_sib, r.ns_r.at[4])
+    await_block(r.vec_sib, r.ns_r.at[5])
     vec_across.wait_send()
     r.vec[...] += r.vec_sib[...]
     chip = c // 2
@@ -703,7 +768,6 @@
         return remote(r.vec.at[:, columns_of(peer)], r.vec_in.at[k], r.v1_s.at[k], r.v1_r.at[k], (2 * peer + core, s))
 
     loop(8, lambda k: vec_to(k).start(), 1)
-    pair_sum(3)
 
     my_part = pl.ds(pick(lax.rem(x, 2) * 2 + yl, 8), 8)
 
@@ -727,6 +791,10 @@
     def two_copy():
         return remote(r.s_two, r.r_two, r.last_two_s.at[0], r.last_two_r.at[0], two_to)
 
+    def finish(which, source, target):
+        results.append(pltpu.make_async_copy(source, target, r.done_s.at[which]))
+        results[-1].start()
+
     second_sum("two")
     not_when(two_stays, lambda: two_copy().start())
 
@@ -749,21 +817,25 @@
 
     loop(8, lambda k: vec_rows_to(k).start(), 1)
     r.vec_all[s] = sums
-    first_sum("qkv")
+    first_sum("qka")
+    first_sum("qkb")
     second_sum("out")
     spread("out")
 
     total = r.ga_own[...]
-    for k in (1, 3, 2):
+    for k in (1, 3):
         await_block(r.ga_in.at[k], r.ga_r.at[k])
         total = total + r.ga_in[k].astype(F32)
-    normed, inverse = norm_rows(r.tok[...].astype(F32))
-    r.input_grad[...] = (
+    normed, inverse = norm_rows(r.tok_all[z].astype(F32))
+    r.w_input[...] = (
         r.grad_hidden[...] + norm_back(total, normed, inverse, r.small_all[0:1, :])
     ).astype(BF16)
-
-    second_sum("qkv")
-    spread("qkv")
+    finish(1, r.w_input, r.input_grad)
+
+    second_sum("qka")
+    spread("qka")
+    second_sum("qkb")
+    spread("qkb")
 
     def rows_arrived(name):
         into = ref("r_", name)
@@ -771,22 +843,29 @@
             not_when(at_home & (z == k), lambda: await_block(into.at[k], ref("last_", name, "_r").at[k]))
 
     not_when(two_stays, lambda: await_block(r.r_two, r.last_two_r.at[0]))
-    r.o_two[...] = r.r_two[...]
+    finish(2, r.r_two, r.o_two)
     rows_arrived("one")
     for i in range(4):
         for t in range(8):
-            r.o_one[:, t * 512 + i * 128 : t * 512 + i * 128 + 128] = r.r_one[i, :, t * 128 : t * 128 + 128]
+            r.w_one_out[:, t * 512 + i * 128 : t * 512 + i * 128 + 128] = r.r_one[i, :, t * 128 : t * 128 + 128]
+    finish(3, r.w_one_out, r.o_one)
     rows_arrived("out")
-    r.o_out[...] = (r.r_out[0] + r.r_out[1]) + (r.r_out[2] + r.r_out[3])
+    r.w_out_out[...] = (r.r_out[0] + r.r_out[1]) + (r.r_out[2] + r.r_out[3])
+    finish(4, r.w_out_out, r.o_out)
     loop(8, lambda k: await_block(r.vec_all.at[lax.rem(s - k + 8, 8)], r.v2_r.at[k]), 1)
     total = r.vec_all[0]
     for i in range(1, 8):
         total = total + r.vec_all[i]
-    r.o_vec[...] = total
-    rows_arrived("qkv")
+    r.w_vec_out[...] = total
+    finish(5, r.w_vec_out, r.o_vec)
+    rows_arrived("qka")
+    rows_arrived("qkb")
     for i in range(4):
-        for t in range(3):
-            r.o_qkv[:, t * 1024 + i * 256 : t * 1024 + i * 256 + 256] = r.r_qkv[i, :, t * 256 : t * 256 + 256]
+        for t in range(6):
+            source = r.r_qka if t < 3 else r.r_qkb
+            column = t // 2 * 1024 + i * 256 + t % 2 * 128
+            r.w_qkv_out[:, column : column + 128] = source[i, :, t % 3 * 128 : t % 3 * 128 + 128]
+    finish(6, r.w_qkv_out, r.o_qkv)
 
     def sent(k):
         small_to(k).wait_send()
@@ -795,32 +874,67 @@
 
     loop(8, sent, 1)
     for k in range(1, 4):
-        for copy in (tok_to(k), cot_to(k), mlp_to(k)):
-            copy.wait_send()
+        cot_to(k).wait_send()
+        if k != 2:
+            tok_to(k).wait_send()
+            mlp_to(k).wait_send()
+            pass_on(r.tok_all, r.tf_s, r.tf_r, k).wait_send()
+            pass_on(r.mlp_all, r.mg_s, r.mg_r, k).wait_send()
+            part_to(r.ga_out, r.ga_in, ga_sems, k).wait_send()
+            via_to(k).wait_send()
         part_to(r.gm_out, r.gm_in, gm_sems, k).wait_send()
         part_to(r.mo_out, r.mo_in, mo_sems, k).wait_send()
-        part_to(r.ga_out, r.ga_in, ga_sems, k).wait_send()
         for name, _ in WEIGHTS:
             weight_copy(name, "own_", k).wait_send()
             weight_copy(name, "far_", k).wait_send()
         for name, _ in GRADS:
             first_to(name, k).wait_send()
             second_to(name, k).wait_send()
-        for piece in range(2):
-            back_to(k, piece).wait_send()
+        for piece in range(3):
+            loop(4, lambda i: back_to(k, piece, i).wait_send())
         for origin in range(4):
             parts_to(k, origin).wait_send()
     for name, _ in WEIGHTS:
         weight_copy(name, "mate_", 0).wait_send()
         weight_copy(name, "mate_", 1).wait_send()
-    for which in range(4):
+    for which in range(5):
         near_to(which).wait_send()
-    for name in ("one", "out", "qkv"):
+    for name in ("one", "out", "qka", "qkb"):
         for k in range(4):
             not_when(at_owner(k), lambda: last_to(name, k).wait_send())
     not_when(two_stays, lambda: two_copy().wait_send())
-    loop(16, lambda k: mix_to(k).wait_send(), 1)
+    loop(16, lambda k: mix_to(lax.rem(c + k, 16)).wait_send(), 1)
     loop(16, lambda k: gmix_to(k).wait_send(), 1)
+    for copy in results:
+        copy.wait()
+
+
+PLAIN = ("layer_out", "input_grad", "o_qkv", "o_out", "o_one", "o_two")
+
+
+def owner_kernel(*refs):
+    c, s, core, x, yl = place()
+    vec, outs = refs[6], refs[7:]
+    for i in range(6):
+        outs[i][...] = refs[i][...]
+    mine = pltpu.roll(vec[...], 128 - core * 64 - s * 8, 1)
+    for i in range(8):
+        outs[6 + i][...] = mine[i : i + 1, 0:8]
+    up = pltpu.roll(vec[pl.ds(8 + 2 * core + x // 2, 1), :], 128 - lax.rem(s, 4) * 32, 1)
+    outs[14][...] = up[:, 0:32]
+
+
+def owner_call(f):
+    arrays = [getattr(f, name) for name in PLAIN]
+    shapes = [jax.ShapeDtypeStruct(a.shape, a.dtype) for a in arrays]
+    shapes += [jax.ShapeDtypeStruct((1, 8), F32)] * 8 + [jax.ShapeDtypeStruct((1, 32), F32)]
+    return pl.pallas_call(
+        owner_kernel,
+        name="owner",
+        out_shape=shapes,
+        in_specs=[pl.BlockSpec(memory_space=VMEM)] * 7,
+        out_specs=[pl.BlockSpec(memory_space=VMEM)] * 15,
+    )(*arrays, f.o_vec)
 
 
 def named_call(kernel, name, cid, ins, outs, scratch, operands):
@@ -857,7 +971,6 @@
     fc2_bias,
     out_cotangent,
 ):
-    c, s = lax.axis_index("ctx"), lax.axis_index("shard")
     f = named_call(
         layer_kernel,
         "layer",
@@ -885,24 +998,24 @@
             cot=out_cotangent.reshape(128, 1024),
         ),
     )
-    mine = lax.dynamic_slice(f.o_vec, (0, (c % 2) * 64 + s * 8), (8, 8))
-    up = lax.dynamic_slice(f.o_vec, (8 + c % 2 * 2 + s // 4, (s % 4) * 32), (1, 32))[0]
+    layer_out, input_grad, g_qkv, g_out, g_one, g_two, *vecs = owner_call(f)
+    out_b, gain_two, bias_two, fc2_b, query_b, value_b, gain_one, bias_one, up = [v.reshape(-1) for v in vecs]
     return (
-        f.layer_out.reshape(tokens.shape),
-        f.input_grad.reshape(tokens.shape),
-        mine[6],
-        mine[7],
-        f.o_qkv,
-        mine[4],
-        mine[5],
-        f.o_out,
-        mine[0],
-        mine[1],
-        mine[2],
-        f.o_one,
+        layer_out.reshape(tokens.shape),
+        input_grad.reshape(tokens.shape),
+        gain_one,
+        bias_one,
+        g_qkv,
+        query_b,
+        value_b,
+        g_out,
+        out_b,
+        gain_two,
+        bias_two,
+        g_one,
         up,
-        f.o_two,
-        mine[3],
+        g_two,
+        fc2_b,
     )
 
 

time: 160 us -> 148 us (0.925)
  local copies, waits for them, and re-layouts: 7.6 us -> 0 us
  Pallas kernels: 152 us -> 147 us
    pallas_call x1, Pallas kernels: 152 us -> 145 us  [named_call(): pl.pallas_call(kernel, name=name, out_shape=[jax.ShapeDtypeStruct(shape,...]
    unnamed x18 -> x0, local copies, waits for them, and re-layouts: 5.66 us -> none
    pallas_call x0 -> x1, Pallas kernels: none -> 2.16 us  [owner_call(): pl.pallas_call(owner_kernel, name='owner', out_shape=shapes, in_specs=[pl...]
    squeeze x2 -> x0, local copies, waits for them, and re-layouts: 1.86 us -> none  [the longest x1 1.32 us: shards(): lax.dynamic_slice(f.o_vec, (8 + c % 2 * 2 + s // 4, s % 4 * 32), (1, 32))[0]]
where the time goes in v5:
time: 148 us
  Pallas kernels  147 us (99%)
    pallas_call x1, Pallas kernels, named_call(): pl.pallas_call(kernel, name=name, out_shape=[jax.ShapeDtypeStruct(shape,...  145 us

profile of v5, /device:TPU:0, one launch (start us, length us, event | category | flops | bytes accessed | tf_op | source)
XLA Modules:
  0.0 147.6 jit_solution(769214217799560837)
XLA Ops:
  0.7 144.6 %layer.1 = (bf16[128,1024]{1,0:T(8,128)(2,1)}, bf16[128,1024]{1,0:T(8,128)(2,1)}, f32[8,3072]{1,0:T(8,128)}, f32[8,1024]{1,0:T(8,128)}, f32[8,4096]{1,0:T(8,128)...) custom-call(s32[2]{0:T(128)} %refs_0_.1, s32[16]{0:T(128)} %refs_1_.1, bf16[128,1024]{1,0:T(8,128)(2,1)} %bitcast.22, ...), custom_call_target="tpu_custom_call" | custom-call | tf_op jit(solution)/shard_map/layer/pallas_call | solution.py:941
  145.3 2.2 %owner.1 = (bf16[128,1024]{1,0:T(8,128)(2,1)}, bf16[128,1024]{1,0:T(8,128)(2,1)}, f32[8,3072]{1,0:T(8,128)}, f32[8,1024]{1,0:T(8,128)}, f32[8,4096]{1,0:T(8,128)...) custom-call(bf16[128,1024]{1,0:T(8,128)(2,1)} %get-tuple-element.37., ...), custom_call_target="tpu_custom_call" | custom-call | tf_op jit(solution)/shard_map/owner/pallas_call | solution.py:931

commit v6 on v5

--- a/solution.py
+++ b/solution.py
@@ -147,24 +147,26 @@
         )
     ],
     *[
-        (prefix + name + end, pltpu.SemaphoreType.DMA((4,)))
+        (prefix + name, pltpu.SemaphoreType.DMA((count,)))
         for name, _ in WEIGHTS
-        for prefix in ("own_", "far_", "mate_")
+        for prefix, count in (("sent_", 2), ("along_", 4), ("up_", 1), ("cross_", 1))
+    ],
+    *[
+        (prefix + name, pltpu.SemaphoreType.DMA((1,)))
+        for name, _ in GRADS
+        for prefix in ("near_s_", "near_r_", "first_s_", "first_r_", "second_s_", "second_r_", "last_s_", "last_r_")
+    ],
+    *[
+        (name + end, pltpu.SemaphoreType.DMA((1,)))
+        for name in ("sm", "tf", "qa", "mx", "mg", "gm", "mo", "mf", "hb", "ga", "vs", "v1", "v2")
         for end in ("_s", "_r")
     ],
     *[
-        (prefix + name + end, pltpu.SemaphoreType.DMA((4,)))
-        for name, _ in GRADS
-        for prefix in ("first_", "second_", "last_")
-        for end in ("_s", "_r")
-    ],
-    *[
-        (name + end, pltpu.SemaphoreType.DMA((count,)))
+        (name, pltpu.SemaphoreType.DMA((count,)))
         for name, count in (
-            ("local", 16), ("done", 8), ("sm", 8), ("tk", 4), ("tf", 4), ("qa", 16), ("mx", 16), ("ct", 4), ("ml", 4),
-            ("mg", 4), ("gm", 4), ("mo", 4), ("mf", 16), ("hb", 48), ("ga", 4), ("gv", 4), ("ns", 8), ("v1", 8), ("v2", 8),
-        )
-        for end in ("_s", "_r")
+            ("local", 7), ("done", 7), ("tk_s", 1), ("tk_r", 4), ("ct_s", 1), ("ct_r", 4), ("ml_s", 1), ("ml_r", 4),
+            ("gv_r", 4),
+        )
     ],
 )
 
@@ -185,16 +187,16 @@
         pltpu.make_async_copy(
             weight.at[half(core), pl.ds(pl.multiple_of(source, 128), width)],
             whole.at[s, half(core), target : target + width],
-            r.local_s.at[i],
+            r.local.at[0 if i < 3 else 1],
         )
         for i, (weight, whole, source, target, width) in enumerate(pieces)
     ]
-    own.append(pltpu.make_async_copy(r.w_out.at[half(core)], r.wo_all.at[s, half(core)], r.local_s.at[11]))
+    own.append(pltpu.make_async_copy(r.w_out.at[half(core)], r.wo_all.at[s, half(core)], r.local.at[2]))
     own.append(
-        pltpu.make_async_copy(r.w_fc2.at[half(2 * z + core)], r.w2_all.at[s, half(core)], r.local_s.at[12])
+        pltpu.make_async_copy(r.w_fc2.at[half(2 * z + core)], r.w2_all.at[s, half(core)], r.local.at[3])
     )
-    own.append(pltpu.make_async_copy(r.cot, r.cot_all.at[z], r.local_s.at[13]))
-    own.append(pltpu.make_async_copy(r.tok, r.tok_all.at[z], r.local_s.at[14]))
+    own.append(pltpu.make_async_copy(r.cot, r.cot_all.at[z], r.local.at[4]))
+    own.append(pltpu.make_async_copy(r.tok, r.tok_all.at[z], r.local.at[5]))
 
     barrier = pltpu.get_barrier_semaphore()
 
@@ -221,12 +223,20 @@
         r.small[i : i + 1, :] = ref(name)[...].astype(F32)
     r.small[8:12, :] = r.fc1_bias[...].astype(F32)
     r.small[12:16, :] = jnp.zeros((4, 128), F32)
-    for copy in own[:3]:
-        copy.wait()
+
+
+    def own_here(whole, sem):
+        block = whole.at[s, half(core)]
+        pltpu.make_async_copy(block, block, r.local.at[sem]).wait()
+
+    own_here(r.wq_all, 0)
     pl.semaphore_wait(barrier, 28 - at_home.astype(jnp.int32) - two_stays.astype(jnp.int32))
 
     def await_block(dst, recv_sem):
-        remote(dst, dst, r.local_s.at[15], recv_sem, sib).wait_recv()
+        remote(dst, dst, r.local.at[6], recv_sem, sib).wait_recv()
+
+    def await_sent(block, send_sem):
+        remote(block, block, send_sem, r.local.at[6], sib).wait_send()
 
     columns_of = lambda which: pl.ds(pick(which, 128), 128)
     z_peer = lambda k: (lax.rem(c + 4 * k, 16), s)
@@ -234,21 +244,21 @@
 
     def small_to(k):
         return remote(
-            r.small, r.small_all.at[:, columns_of(s)], r.sm_s.at[k], r.sm_r.at[k], (c, lax.rem(s + k, 8))
+            r.small, r.small_all.at[:, columns_of(s)], r.sm_s.at[0], r.sm_r.at[0], (c, lax.rem(s + k, 8))
         )
 
     def tok_to(k):
-        return remote(r.tok, r.tok_all.at[z], r.tk_s.at[k], r.tk_r.at[k], z_peer(k))
+        return remote(r.tok, r.tok_all.at[z], r.tk_s.at[0], r.tk_r.at[k], z_peer(k))
 
     def cot_to(k):
-        return remote(r.cot, r.cot_all.at[z], r.ct_s.at[k], r.ct_r.at[k], z_peer(k))
+        return remote(r.cot, r.cot_all.at[z], r.ct_s.at[0], r.ct_r.at[k], z_peer(k))
 
     z_of = lambda hop: lax.rem(z - hop + 4, 4)
 
     def pass_on(whole, send_sems, recv_sems, k):
         rows = slice(0, 64) if k == 1 else slice(64, 128)
         block = whole.at[z_of(k), rows]
-        return remote(block, block, send_sems.at[k], recv_sems.at[k], z_peer(k))
+        return remote(block, block, send_sems.at[0], recv_sems.at[0], z_peer(k))
 
     def ring_arrived(whole, recv_sems, send_next, recv_next, k):
         @pl.when(k == 1)
@@ -259,36 +269,56 @@
 
         @pl.when(k == 3)
         def _():
-            for j, rows in ((1, slice(0, 64)), (3, slice(64, 128))):
-                await_block(whole.at[z_of(2), rows], recv_next.at[j])
-
-    def weight_copy(name, kind, k):
+            await_block(whole.at[z_of(2)], recv_next.at[0])
+
+    y_next = lambda p: (c + (2 - 4 * yh) * p, mate_s)
+    some_rows = lambda p: pl.ds(pick(2 * core + p, 32), 32)
+
+    def weight_along(name, kind, k):
         whole = ref(name, "_all")
-        device = (c, mate_s) if kind == "mate_" else x_peer(k)
-        block = whole.at[mate_s if kind == "far_" else s, half(core)]
-        if kind == "mate_" and k == 0:
-            device, block = sib, whole.at[:, half(core)]
-        return remote(block, block, ref(kind, name, "_s").at[k], ref(kind, name, "_r").at[k], device)
+        block = whole.at[s if kind == "own_" else mate_s, half(core)]
+        return remote(
+            block, block, ref("sent_", name).at[0], ref("along_", name).at[0 if name == "wo" else k], x_peer(k)
+        )
+
+    def weight_up(name, k, p):
+        block = ref(name, "_all").at[2 * lax.rem(x - k + 4, 4) + yl, some_rows(p)]
+        return remote(block, block, ref("sent_", name).at[0], ref("up_", name).at[0], y_next(p))
+
+    def weight_cross(name):
+        block = ref(name, "_all").at[:, half(core)]
+        return remote(block, block, ref("sent_", name).at[1], ref("cross_", name).at[0], sib)
 
     def weight_own(name):
-        weight_copy(name, "mate_", 1).start()
+        for p in range(2):
+            weight_up(name, 0, p).start()
         for k in (1, 3, 2):
-            weight_copy(name, "own_", k).start()
+            weight_along(name, "own_", k).start()
+
+    def await_along(name, k):
+        block = ref(name, "_all").at[2 * lax.rem(x - k + 4, 4) + yl, half(core)]
+        await_block(block, ref("along_", name).at[k])
 
     def weight_far(name):
-        await_block(ref(name, "_all").at[mate_s, half(core)], ref("mate_", name, "_r").at[1])
-        for k in (1, 3, 2):
-            weight_copy(name, "far_", k).start()
+        if name == "wo":
+            await_block(ref(name, "_all").at[mate_s, half(core)], ref("up_", name).at[0])
+            for k in (1, 3, 2):
+                weight_along(name, "far_", k).start()
+        else:
+            for k in (1, 3, 2):
+                await_along(name, k)
+                for p in range(2):
+                    weight_up(name, k, p).start()
 
     def weight_across(name):
-        for k in (1, 3, 2):
-            origin = 2 * lax.rem(x - k + 4, 4)
-            await_block(ref(name, "_all").at[origin + yl, half(core)], ref("own_", name, "_r").at[k])
-            await_block(ref(name, "_all").at[origin + 1 - yl, half(core)], ref("far_", name, "_r").at[k])
-        weight_copy(name, "mate_", 0).start()
+        if name == "wo":
+            await_block(ref(name, "_all").at[0:6, 0:64], ref("along_", name).at[0])
+        else:
+            await_block(ref(name, "_all").at[0:4, 0:64], ref("up_", name).at[0])
+        weight_cross(name).start()
 
     def weight_ready(name):
-        await_block(ref(name, "_all").at[:, half(1 - core)], ref("mate_", name, "_r").at[0])
+        await_block(ref(name, "_all").at[:, half(1 - core)], ref("cross_", name).at[0])
 
     for k in (1, 3):
         tok_to(k).start()
@@ -305,15 +335,13 @@
         r.places[pl.ds(pick(k, 64), 64), :] = (block * 32 + lax.rem(sub, 32)).astype(F32)
 
     loop(16, set_places)
-    loop(
-        8,
-        lambda k: await_block(r.small_all.at[:, columns_of(lax.rem(s - k + 8, 8))], r.sm_r.at[k]),
-        1,
-    )
+    await_block(r.small_all.at[:, 0:896], r.sm_r.at[0])
     weight_across("wq")
-    for copy in own[3:14]:
+    own_here(r.w1_all, 1)
+    for copy in own[11:14]:
         copy.wait()
     weight_own("wo")
+    weight_own("w1")
 
     gain_one, bias_one = r.small_all[0:1, :], r.small_all[1:2, :]
     head_cols = pl.ds(pick(z, 256), 256)
@@ -324,8 +352,8 @@
         return remote(
             r.qkv.at[peer, origin],
             r.parts.at[origin, q4],
-            r.qa_s.at[4 * m + origin],
-            r.qa_r.at[4 * m + origin],
+            r.qa_s.at[0],
+            r.qa_r.at[0],
             (4 * z + peer, s),
         )
 
@@ -368,16 +396,10 @@
     weight_far("wo")
     for k in (1, 3, 2):
         cot_to(k).start()
-    weight_own("w1")
-
-    def parts_arrived(k):
-        m = 1 + k // 4
-        origin = lax.rem(k, 4)
-        await_block(r.parts.at[origin, lax.rem(q4 - m + 4, 4)], r.qa_r.at[4 * m + origin])
-
-    loop(12, parts_arrived)
+    weight_own("w2")
+
+    await_block(r.parts.at[0:3], r.qa_r.at[0])
     weight_far("w1")
-    weight_own("w2")
 
     length = jnp.where(yh == 0, r.lengths[0], r.lengths[1]).astype(F32)
     head_lane = lax.broadcasted_iota(jnp.int32, (1, 128), 1) // 64
@@ -394,7 +416,7 @@
 
     def mix_to(peer):
         return remote(
-            r.mixed.at[peer], r.mix_rows.at[yh, :, pair_columns(c)], r.mx_s.at[peer], r.mx_r.at[c], (peer, s)
+            r.mixed.at[peer], r.mix_rows.at[yh, :, pair_columns(c)], r.mx_s.at[0], r.mx_r.at[0], (peer, s)
         )
 
     def attend(k):
@@ -418,16 +440,12 @@
     loop(4, attend)
 
     r.mix_rows[yh, :, pair_columns(c)] = r.mixed[c]
+    weight_across("wo")
     weight_far("w2")
-    weight_across("wo")
     weight_across("w1")
     weight_ready("wo")
 
-    def mix_arrived(k):
-        origin = lax.rem(c - k + 16, 16)
-        await_block(r.mix_rows.at[slot_of(origin), :, pair_columns(origin)], r.mx_r.at[origin])
-
-    loop(16, mix_arrived, 1)
+    await_block(r.mixed.at[0:15], r.mx_r.at[0])
 
     mix = r.mix_rows[...].reshape(128, 1024)
     hidden = r.tok_all[z].astype(F32) + (dot(mix, r.wo_all[...].reshape(1024, 1024)) + r.small_all[4:5, :])
@@ -436,7 +454,7 @@
     r.mlp_all[z] = (normed * r.small_all[5:6, :] + r.small_all[6:7, :]).astype(BF16)
 
     def mlp_to(k):
-        return remote(r.mlp_all.at[z], r.mlp_all.at[z], r.ml_s.at[k], r.ml_r.at[k], z_peer(k))
+        return remote(r.mlp_all.at[z], r.mlp_all.at[z], r.ml_s.at[0], r.ml_r.at[k], z_peer(k))
 
     for k in (1, 3):
         mlp_to(k).start()
@@ -454,7 +472,7 @@
         return (jnp.concatenate([mine, mine], axis=0) < row_length).astype(F32)
 
     def part_to(out, into, sems, k):
-        return remote(out.at[lax.rem(z + k, 4)], into.at[k], sems[0].at[k], sems[1].at[k], z_peer(k))
+        return remote(out.at[lax.rem(z + k, 4)], into.at[k], sems[0].at[0], sems[1].at[0], z_peer(k))
 
     gm_sems, mo_sems, ga_sems = (r.gm_s, r.gm_r), (r.mo_s, r.mo_r), (r.ga_s, r.ga_r)
 
@@ -517,7 +535,7 @@
     def near_to(which):
         name = GRADS[which][0]
         return remote(
-            ref("g_", name).at[:, 1 - core], ref("n_", name), r.ns_s.at[which], r.ns_r.at[which], sib
+            ref("g_", name).at[:, 1 - core], ref("n_", name), ref("near_s_", name).at[0], ref("near_r_", name).at[0], sib
         )
 
     def y_peer(k):
@@ -532,18 +550,18 @@
 
     def first_to(name, k):
         device, index = peer_of(order[name][0], k)
-        sems = ref("first_", name, "_s"), ref("first_", name, "_r")
-        return remote(ref("a_", name).at[index], ref("b_", name).at[k], sems[0].at[k], sems[1].at[k], device)
+        sems = ref("first_s_", name), ref("first_r_", name)
+        return remote(ref("a_", name).at[index], ref("b_", name).at[k], sems[0].at[0], sems[1].at[0], device)
 
     def second_to(name, k):
         device, index = peer_of(order[name][1], k)
-        sems = ref("second_", name, "_s"), ref("second_", name, "_r")
-        return remote(ref("m_", name).at[index], ref("h_", name).at[k], sems[0].at[k], sems[1].at[k], device)
+        sems = ref("second_s_", name), ref("second_r_", name)
+        return remote(ref("m_", name).at[index], ref("h_", name).at[k], sems[0].at[0], sems[1].at[0], device)
 
     def pair_sum(which):
         name = GRADS[which][0]
         grad, near, into = ref("g_", name), ref("n_", name), ref("a_", name)
-        await_block(near, r.ns_r.at[which])
+        await_block(near, ref("near_r_", name).at[0])
 
         def add(j):
             y_to = lax.rem(j, 2) * 2 + j // 4
@@ -560,8 +578,7 @@
 
     def first_sum(name):
         mine, others, into = ref("a_", name), ref("b_", name), ref("m_", name)
-        for k in (1, 3, 2):
-            await_block(others.at[k], ref("first_", name, "_r").at[k])
+        await_block(others.at[1:4], ref("first_r_", name).at[0])
 
         def add(j):
             total = mine[here[order[name][0]], j].astype(F32)
@@ -575,8 +592,7 @@
 
     def second_sum(name):
         mine, others = ref("m_", name), ref("h_", name)
-        for k in (1, 3, 2):
-            await_block(others.at[k], ref("second_", name, "_r").at[k])
+        await_block(others.at[1:4], ref("second_r_", name).at[0])
         total = mine[here[order[name][1]]].astype(F32)
         for k in (1, 2, 3):
             total = total + others[k].astype(F32)
@@ -589,8 +605,8 @@
     loop(4, mlp_out)
 
     total = r.gm_own[...]
+    await_block(r.gm_in.at[1:4], r.gm_r.at[0])
     for k in (1, 3, 2):
-        await_block(r.gm_in.at[k], r.gm_r.at[k])
         total = total + r.gm_in[k].astype(F32)
     normed, inverse = norm_rows(r.hidden[...])
     grad_out = r.cot_all[z].astype(F32)
@@ -606,7 +622,7 @@
     def gmix_to(k):
         peer = lax.rem(c + k, 16)
         return remote(
-            r.gmix.at[slot_of(peer), :, pair_columns(peer)], r.gmixed.at[c], r.mf_s.at[k], r.mf_r.at[k], (peer, s)
+            r.gmix.at[slot_of(peer), :, pair_columns(peer)], r.gmixed.at[c], r.mf_s.at[0], r.mf_r.at[0], (peer, s)
         )
 
     loop(16, lambda k: gmix_to(k).start(), 1)
@@ -618,22 +634,20 @@
         r.g_out[pl.ds(2 * i, 2)] = part.astype(BF16).reshape(2, 2, 64, 1024)
 
     pair_sum(0)
-    pair_sum(1)
     loop(4, out_rows)
     near_to(2).start()
-    loop(16, lambda k: await_block(r.gmixed.at[lax.rem(c - k + 16, 16)], r.mf_r.at[k]), 1)
+    await_block(r.gmixed.at[0:15], r.mf_r.at[0])
     for k in (1, 3, 2):
         part_to(r.mo_out, r.mo_in, mo_sems, k).start()
 
     def back_to(m, piece, i):
         peer = lax.rem(q4 + m, 4)
         cols = slice(piece * 128, piece * 128 + 128)
-        sem = 16 * piece + 4 * i + m
         return remote(
             r.gparts.at[i, peer, :, cols],
             r.gback.at[q4, i, :, cols],
-            r.hb_s.at[sem],
-            r.hb_r.at[sem],
+            r.hb_s.at[0],
+            r.hb_r.at[0],
             (4 * z + peer, s),
         )
 
@@ -684,26 +698,18 @@
     for i, sums in ((4, bias_q), (5, bias_v)):
         r.vec[i : i + 1, :] = jnp.where(wide, jnp.concatenate([sums] * 8, axis=1), 0.0)
 
+    pair_sum(1)
     pair_sum(2)
     first_sum("two")
-    first_sum("one")
     total = r.mo_own[...] + r.small_all[7:8, :]
+    await_block(r.mo_in.at[1:4], r.mo_r.at[0])
     for k in (1, 3, 2):
-        await_block(r.mo_in.at[k], r.mo_r.at[k])
         total = total + r.mo_in[k].astype(F32)
     r.w_layer[...] = (valid_of(z) * (r.hidden[...] + total)).astype(BF16)
-    results = [pltpu.make_async_copy(r.w_layer, r.layer_out, r.done_s.at[0])]
+    results = [pltpu.make_async_copy(r.w_layer, r.layer_out, r.done.at[0])]
     results[0].start()
 
-    def back_arrived(i):
-        for m in (1, 2, 3):
-            for piece in (2, 0, 1):
-                await_block(
-                    r.gback.at[lax.rem(q4 - m + 4, 4), i, :, piece * 128 : piece * 128 + 128],
-                    r.hb_r.at[16 * piece + 4 * i + m],
-                )
-
-    loop(4, back_arrived)
+    await_block(r.gback.at[0:3], r.hb_r.at[0])
 
     def assemble(origin):
         for t in range(3):
@@ -733,7 +739,7 @@
 
     def via_to(k):
         return remote(
-            r.ga_out.at[lax.rem(z + 2, 4), halves[k]], r.ga_via.at[k], r.gv_s.at[k], r.gv_r.at[k], z_peer(k)
+            r.ga_out.at[lax.rem(z + 2, 4), halves[k]], r.ga_via.at[k], r.ga_s.at[0], r.gv_r.at[k], z_peer(k)
         )
 
     def via_add(k):
@@ -756,16 +762,16 @@
     pair_sum(3)
     pair_sum(4)
     attn_back(0)
-    vec_across = remote(r.vec, r.vec_sib, r.ns_s.at[5], r.ns_r.at[5], sib)
+    vec_across = remote(r.vec, r.vec_sib, r.vs_s.at[0], r.vs_r.at[0], sib)
     vec_across.start()
-    await_block(r.vec_sib, r.ns_r.at[5])
-    vec_across.wait_send()
+    await_block(r.vec_sib, r.vs_r.at[0])
+    await_sent(r.vec_sib, r.vs_s.at[0])
     r.vec[...] += r.vec_sib[...]
     chip = c // 2
 
     def vec_to(k):
         peer = lax.rem(chip + k, 8)
-        return remote(r.vec.at[:, columns_of(peer)], r.vec_in.at[k], r.v1_s.at[k], r.v1_r.at[k], (2 * peer + core, s))
+        return remote(r.vec.at[:, columns_of(peer)], r.vec_in.at[k], r.v1_s.at[0], r.v1_r.at[0], (2 * peer + core, s))
 
     loop(8, lambda k: vec_to(k).start(), 1)
 
@@ -773,9 +779,9 @@
 
     def last_to(name, k):
         rows = slice(8 * k, 8 * k + 8)
-        sems = ref("last_", name, "_s"), ref("last_", name, "_r")
+        sems = ref("last_s_", name), ref("last_r_", name)
         device = (to_z * 4 + q4, 2 * (x // 2 * 2 + k // 2) + k % 2)
-        return remote(ref("s_", name).at[rows], ref("r_", name).at[z], sems[0].at[k], sems[1].at[z], device)
+        return remote(ref("s_", name).at[rows], ref("r_", name).at[z], sems[0].at[0], sems[1].at[0], device)
 
     def at_owner(k):
         return at_home & (lax.rem(x, 2) == k // 2) & (yl == k % 2)
@@ -789,12 +795,13 @@
             ref("r_", name)[z] = ref("s_", name)[my_part]
 
     def two_copy():
-        return remote(r.s_two, r.r_two, r.last_two_s.at[0], r.last_two_r.at[0], two_to)
+        return remote(r.s_two, r.r_two, r.last_s_two.at[0], r.last_r_two.at[0], two_to)
 
     def finish(which, source, target):
-        results.append(pltpu.make_async_copy(source, target, r.done_s.at[which]))
+        results.append(pltpu.make_async_copy(source, target, r.done.at[which]))
         results[-1].start()
 
+    first_sum("one")
     second_sum("two")
     not_when(two_stays, lambda: two_copy().start())
 
@@ -806,14 +813,14 @@
     spread("one")
     first_sum("out")
 
-    loop(8, lambda k: await_block(r.vec_in.at[k], r.v1_r.at[k]), 1)
+    await_block(r.vec_in.at[1:8], r.v1_r.at[0])
     sums = r.vec[:, columns_of(chip)]
     for k in range(1, 8):
         sums = sums + r.vec_in[k]
     r.vec_sum[...] = sums
 
     def vec_rows_to(k):
-        return remote(r.vec_sum, r.vec_all.at[s], r.v2_s.at[k], r.v2_r.at[k], (c, lax.rem(s + k, 8)))
+        return remote(r.vec_sum, r.vec_all.at[s], r.v2_s.at[0], r.v2_r.at[0], (c, lax.rem(s + k, 8)))
 
     loop(8, lambda k: vec_rows_to(k).start(), 1)
     r.vec_all[s] = sums
@@ -823,8 +830,8 @@
     spread("out")
 
     total = r.ga_own[...]
+    await_block(r.ga_in.at[0:2], r.ga_r.at[0])
     for k in (1, 3):
-        await_block(r.ga_in.at[k], r.ga_r.at[k])
         total = total + r.ga_in[k].astype(F32)
     normed, inverse = norm_rows(r.tok_all[z].astype(F32))
     r.w_input[...] = (
@@ -839,10 +846,10 @@
 
     def rows_arrived(name):
         into = ref("r_", name)
-        for k in range(4):
-            not_when(at_home & (z == k), lambda: await_block(into.at[k], ref("last_", name, "_r").at[k]))
-
-    not_when(two_stays, lambda: await_block(r.r_two, r.last_two_r.at[0]))
+        not_when(at_home, lambda: await_block(into, ref("last_r_", name).at[0]))
+        pl.when(at_home)(lambda: await_block(into.at[0:3], ref("last_r_", name).at[0]))
+
+    not_when(two_stays, lambda: await_block(r.r_two, r.last_r_two.at[0]))
     finish(2, r.r_two, r.o_two)
     rows_arrived("one")
     for i in range(4):
@@ -852,7 +859,7 @@
     rows_arrived("out")
     r.w_out_out[...] = (r.r_out[0] + r.r_out[1]) + (r.r_out[2] + r.r_out[3])
     finish(4, r.w_out_out, r.o_out)
-    loop(8, lambda k: await_block(r.vec_all.at[lax.rem(s - k + 8, 8)], r.v2_r.at[k]), 1)
+    await_block(r.vec_all.at[0:7], r.v2_r.at[0])
     total = r.vec_all[0]
     for i in range(1, 8):
         total = total + r.vec_all[i]
@@ -867,44 +874,25 @@
             r.w_qkv_out[:, column : column + 128] = source[i, :, t % 3 * 128 : t % 3 * 128 + 128]
     finish(6, r.w_qkv_out, r.o_qkv)
 
-    def sent(k):
-        small_to(k).wait_send()
-        vec_to(k).wait_send()
-        vec_rows_to(k).wait_send()
-
-    loop(8, sent, 1)
-    for k in range(1, 4):
-        cot_to(k).wait_send()
-        if k != 2:
-            tok_to(k).wait_send()
-            mlp_to(k).wait_send()
-            pass_on(r.tok_all, r.tf_s, r.tf_r, k).wait_send()
-            pass_on(r.mlp_all, r.mg_s, r.mg_r, k).wait_send()
-            part_to(r.ga_out, r.ga_in, ga_sems, k).wait_send()
-            via_to(k).wait_send()
-        part_to(r.gm_out, r.gm_in, gm_sems, k).wait_send()
-        part_to(r.mo_out, r.mo_in, mo_sems, k).wait_send()
-        for name, _ in WEIGHTS:
-            weight_copy(name, "own_", k).wait_send()
-            weight_copy(name, "far_", k).wait_send()
-        for name, _ in GRADS:
-            first_to(name, k).wait_send()
-            second_to(name, k).wait_send()
-        for piece in range(3):
-            loop(4, lambda i: back_to(k, piece, i).wait_send())
-        for origin in range(4):
-            parts_to(k, origin).wait_send()
+    await_sent(r.small_all.at[:, 0:896], r.sm_s.at[0])
+    for block, sem in (
+        (r.tok_all.at[0:2], r.tk_s), (r.tok_all.at[0], r.tf_s), (r.cot_all.at[0:3], r.ct_s), (r.mlp_all.at[0:2], r.ml_s),
+        (r.mlp_all.at[0], r.mg_s), (r.qkv.at[0:3], r.qa_s), (r.mixed.at[0:15], r.mx_s), (r.gm_out.at[0:3], r.gm_s),
+        (r.mo_out.at[0:3], r.mo_s), (r.gmixed.at[0:15], r.mf_s), (r.gparts.at[0:3], r.hb_s), (r.ga_out.at[0:3], r.ga_s),
+        (r.vec_in.at[0:7], r.v1_s), (r.vec_all.at[0:7], r.v2_s),
+    ):
+        await_sent(block, sem.at[0])
     for name, _ in WEIGHTS:
-        weight_copy(name, "mate_", 0).wait_send()
-        weight_copy(name, "mate_", 1).wait_send()
-    for which in range(5):
-        near_to(which).wait_send()
-    for name in ("one", "out", "qka", "qkb"):
-        for k in range(4):
-            not_when(at_owner(k), lambda: last_to(name, k).wait_send())
+        await_sent(ref(name, "_all").at[0:7, 0:64], ref("sent_", name).at[0])
+        await_sent(ref(name, "_all").at[:, 0:64], ref("sent_", name).at[1])
+    for name, _ in GRADS:
+        await_sent(ref("n_", name), ref("near_s_", name).at[0])
+        await_sent(ref("a_", name).at[0:3], ref("first_s_", name).at[0])
+        await_sent(ref("m_", name).at[0:3], ref("second_s_", name).at[0])
+        if name != "two":
+            not_when(at_home, lambda: await_sent(ref("r_", name), ref("last_s_", name).at[0]))
+            pl.when(at_home)(lambda: await_sent(ref("r_", name).at[0:3], ref("last_s_", name).at[0]))
     not_when(two_stays, lambda: two_copy().wait_send())
-    loop(16, lambda k: mix_to(lax.rem(c + k, 16)).wait_send(), 1)
-    loop(16, lambda k: gmix_to(k).wait_send(), 1)
     for copy in results:
         copy.wait()
 

time: 148 us -> 133 us (0.90); the launches traced: 148 us -> 131 us
  Pallas kernels: 147 us -> 130 us
    pallas_call x1, Pallas kernels: 145 us -> 128 us  [named_call(): pl.pallas_call(kernel, name=name, out_shape=[jax.ShapeDtypeStruct(shape,...]
where the time goes in v6:
time: 133 us; the launch traced here: 131 us
  Pallas kernels  130 us (98%)
    pallas_call x1, Pallas kernels, named_call(): pl.pallas_call(kernel, name=name, out_shape=[jax.ShapeDtypeStruct(shape,...  128 us

profile of v6, /device:TPU:0, one launch (start us, length us, event | category | flops | bytes accessed | tf_op | source)
XLA Modules:
  0.0 131.0 jit_solution(10169571791248305514)
XLA Ops:
  0.7 128.2 %layer.1 = (bf16[128,1024]{1,0:T(8,128)(2,1)}, bf16[128,1024]{1,0:T(8,128)(2,1)}, f32[8,3072]{1,0:T(8,128)}, f32[8,1024]{1,0:T(8,128)}, f32[8,4096]{1,0:T(8,128)...) custom-call(s32[2]{0:T(128)} %refs_0_.1, s32[16]{0:T(128)} %refs_1_.1, bf16[128,1024]{1,0:T(8,128)(2,1)} %bitcast.22, ...), custom_call_target="tpu_custom_call" | custom-call | tf_op jit(solution)/shard_map/layer/pallas_call | solution.py:929
  128.9 2.2 %owner.1 = (bf16[128,1024]{1,0:T(8,128)(2,1)}, bf16[128,1024]{1,0:T(8,128)(2,1)}, f32[8,3072]{1,0:T(8,128)}, f32[8,1024]{1,0:T(8,128)}, f32[8,4096]{1,0:T(8,128)...) custom-call(bf16[128,1024]{1,0:T(8,128)(2,1)} %get-tuple-element.37., ...), custom_call_target="tpu_custom_call" | custom-call | tf_op jit(solution)/shard_map/owner/pallas_call | solution.py:919

commit v7 on v6

--- a/solution.py
+++ b/solution.py
@@ -84,8 +84,8 @@
 )
 
 LAYER_IN = (
-    ("lengths", pltpu.SMEM),
-    ("block_pairs", pltpu.SMEM),
+    ("lengths", VMEM),
+    ("block_pairs", VMEM),
     ("tok", ANY),
     *[(name, VMEM) for name in VECTORS],
     ("fc1_bias", VMEM),
@@ -136,7 +136,7 @@
     *[
         (name, pltpu.VMEM(shape, F32))
         for name, shape in (
-            ("small", (16, 128)), ("small_all", (16, 1024)), ("places", (1024, 128)), ("mix_t", (128, 1024)),
+            ("small", (16, 128)), ("small_all", (16, 1024)), ("places", (1024, 128)), ("key_places", (1024, 128)), ("mix_t", (128, 1024)),
             ("hidden", (128, 1024)), ("gm_own", (128, 1024)), ("mo_own", (128, 1024)),
             ("grad_hidden", (128, 1024)), ("ga_own", (128, 1024)), ("gq_t", (128, 1024)), ("delta", (2, 1024)),
             ("r_two", (32, 1024)), ("r_one", (4, 8, 1024)), ("r_out", (4, 8, 1024)), ("r_qka", (4, 8, 384)),
@@ -247,8 +247,11 @@
             r.small, r.small_all.at[:, columns_of(s)], r.sm_s.at[0], r.sm_r.at[0], (c, lax.rem(s + k, 8))
         )
 
-    def tok_to(k):
-        return remote(r.tok, r.tok_all.at[z], r.tk_s.at[0], r.tk_r.at[k], z_peer(k))
+    halves = {1: (slice(0, 64), slice(64, 128)), 3: (slice(64, 128), slice(0, 64))}
+
+    def tok_to(k, h):
+        rows = halves[k][h]
+        return remote(r.tok.at[rows], r.tok_all.at[z, rows], r.tk_s.at[0], r.tk_r.at[k - h], z_peer(k))
 
     def cot_to(k):
         return remote(r.cot, r.cot_all.at[z], r.ct_s.at[0], r.ct_r.at[k], z_peer(k))
@@ -256,16 +259,17 @@
     z_of = lambda hop: lax.rem(z - hop + 4, 4)
 
     def pass_on(whole, send_sems, recv_sems, k):
-        rows = slice(0, 64) if k == 1 else slice(64, 128)
-        block = whole.at[z_of(k), rows]
+        block = whole.at[z_of(k), halves[k][0]]
         return remote(block, block, send_sems.at[0], recv_sems.at[0], z_peer(k))
 
     def ring_arrived(whole, recv_sems, send_next, recv_next, k):
         @pl.when(k == 1)
         def _():
             for j in (1, 3):
-                await_block(whole.at[z_of(j)], recv_sems.at[j])
+                await_block(whole.at[z_of(j), halves[j][0]], recv_sems.at[j])
                 pass_on(whole, send_next, recv_next, j).start()
+            for j in (1, 3):
+                await_block(whole.at[z_of(j), halves[j][1]], recv_sems.at[j - 1])
 
         @pl.when(k == 3)
         def _():
@@ -285,8 +289,8 @@
         block = ref(name, "_all").at[2 * lax.rem(x - k + 4, 4) + yl, some_rows(p)]
         return remote(block, block, ref("sent_", name).at[0], ref("up_", name).at[0], y_next(p))
 
-    def weight_cross(name):
-        block = ref(name, "_all").at[:, half(core)]
+    def weight_cross(name, k, other):
+        block = ref(name, "_all").at[2 * lax.rem(x - k + 4, 4) + (1 - yl if other else yl), half(core)]
         return remote(block, block, ref("sent_", name).at[1], ref("cross_", name).at[0], sib)
 
     def weight_own(name):
@@ -309,19 +313,25 @@
                 await_along(name, k)
                 for p in range(2):
                     weight_up(name, k, p).start()
+                weight_cross(name, k, False).start()
+            weight_cross(name, 0, False).start()
 
     def weight_across(name):
         if name == "wo":
             await_block(ref(name, "_all").at[0:6, 0:64], ref("along_", name).at[0])
+            for k in range(4):
+                weight_cross(name, k, False).start()
         else:
             await_block(ref(name, "_all").at[0:4, 0:64], ref("up_", name).at[0])
-        weight_cross(name).start()
+        for k in range(4):
+            weight_cross(name, k, True).start()
 
     def weight_ready(name):
         await_block(ref(name, "_all").at[:, half(1 - core)], ref("cross_", name).at[0])
 
-    for k in (1, 3):
-        tok_to(k).start()
+    for h in range(2):
+        for k in (1, 3):
+            tok_to(k, h).start()
     weight_own("wq")
     loop(8, lambda k: small_to(k).start(), 1)
     r.small_all[:, columns_of(s)] = r.small[...]
@@ -329,12 +339,16 @@
 
     sub = lax.broadcasted_iota(jnp.int32, (64, 128), 0)
 
+    pair_lane = lax.broadcasted_iota(jnp.int32, (1, 16), 1)
+
     def set_places(k):
-        pair = r.block_pairs[k]
+        pair = jnp.sum(jnp.where(pair_lane == k, r.block_pairs[...], 0), axis=1, keepdims=True)
         block = jnp.where(sub < 32, pair, 31 - pair)
         r.places[pl.ds(pick(k, 64), 64), :] = (block * 32 + lax.rem(sub, 32)).astype(F32)
 
     loop(16, set_places)
+    length = jnp.where(yh == 0, r.lengths[:, 0:1], r.lengths[:, 1:2]).astype(F32)
+    r.key_places[...] = jnp.where(r.places[...] < length, r.places[...], 2048.0)
     await_block(r.small_all.at[:, 0:896], r.sm_r.at[0])
     weight_across("wq")
     own_here(r.w1_all, 1)
@@ -361,22 +375,22 @@
         normed, _ = norm_rows(r.tok_all[origin].astype(F32))
         r.attn_all[origin] = (normed * gain_one + bias_one).astype(BF16)
 
+    def hop_of(k):
+        return k + (k // 2) * (1 - 2 * lax.rem(k, 2))
+
     own[14].wait()
     norm_block(z)
+
+    def norm_next(k):
+        ring_arrived(r.tok_all, r.tk_r, r.tf_s, r.tf_r, k)
+        norm_block(z_of(hop_of(k)))
+
+    loop(4, norm_next, 1)
     weight_ready("wq")
-
-    def hop_of(k):
-        return k + (k // 2) * (1 - 2 * lax.rem(k, 2))
 
     def qkv_block(k):
         hop = hop_of(k)
         origin = z_of(hop)
-        ring_arrived(r.tok_all, r.tk_r, r.tf_s, r.tf_r, k)
-
-        @pl.when(k > 0)
-        def _():
-            norm_block(origin)
-
         for t in range(3):
             cols = slice(t * 256, t * 256 + 256)
             acc = dot(r.attn_all[origin], r.wq_all[:, :, cols].reshape(1024, 256))
@@ -401,7 +415,6 @@
     await_block(r.parts.at[0:3], r.qa_r.at[0])
     weight_far("w1")
 
-    length = jnp.where(yh == 0, r.lengths[0], r.lengths[1]).astype(F32)
     head_lane = lax.broadcasted_iota(jnp.int32, (1, 128), 1) // 64
     value_t = r.parts[:, :, :, 256:384].reshape(1024, 128).T
 
@@ -422,9 +435,9 @@
     def attend(k):
         i = lax.rem(z + k + 1, 4)
         keys = r.parts[:, :, :, 128:256].reshape(1024, 128)
-        key_place = r.places[:, 0:1]
         query_place = r.places[pl.ds(pick(i, 256), 256), :].T[0:1, :]
-        allowed = (key_place < length) & (key_place <= query_place)
+        key_place = r.key_places[...]
+        allowed = jnp.concatenate([key_place, key_place], axis=1) <= query_place
         queries = r.parts[i, :, :, 0:128].reshape(256, 128) * jnp.asarray(0.125, BF16)
         cols = pl.ds(pick(i, 256), 256)
         for h in range(2):
@@ -453,11 +466,13 @@
     normed, _ = norm_rows(hidden)
     r.mlp_all[z] = (normed * r.small_all[5:6, :] + r.small_all[6:7, :]).astype(BF16)
 
-    def mlp_to(k):
-        return remote(r.mlp_all.at[z], r.mlp_all.at[z], r.ml_s.at[0], r.ml_r.at[k], z_peer(k))
-
-    for k in (1, 3):
-        mlp_to(k).start()
+    def mlp_to(k, h):
+        block = r.mlp_all.at[z, halves[k][h]]
+        return remote(block, block, r.ml_s.at[0], r.ml_r.at[k - h], z_peer(k))
+
+    for h in range(2):
+        for k in (1, 3):
+            mlp_to(k, h).start()
     weight_across("w2")
     weight_ready("w1")
     weight_ready("w2")
@@ -465,7 +480,7 @@
     r.vec[...] = jnp.zeros_like(r.vec)
     up_row = pl.ds(8 + z, 1)
     upper = lax.broadcasted_iota(jnp.int32, (128, 1), 0) < 64
-    row_length = jnp.where(upper, r.lengths[0], r.lengths[1]).astype(F32)
+    row_length = jnp.where(upper, r.lengths[:, 0:1], r.lengths[:, 1:2]).astype(F32)
 
     def valid_of(origin):
         mine = r.places[half(origin * 4 + q4), 0:1]
@@ -474,7 +489,7 @@
     def part_to(out, into, sems, k):
         return remote(out.at[lax.rem(z + k, 4)], into.at[k], sems[0].at[0], sems[1].at[0], z_peer(k))
 
-    gm_sems, mo_sems, ga_sems = (r.gm_s, r.gm_r), (r.mo_s, r.mo_r), (r.ga_s, r.ga_r)
+    gm_sems, mo_sems = (r.gm_s, r.gm_r), (r.mo_s, r.mo_r)
 
     def mlp_block(k):
         hop = hop_of(k)
@@ -613,8 +628,7 @@
     grad_hidden = grad_out + norm_back(total, normed, inverse, r.small_all[5:6, :])
     r.grad_hidden[...] = grad_hidden
     r.hidden_low[...] = grad_hidden.astype(BF16)
-    for i, rows in enumerate((grad_hidden, total * normed, total, grad_out)):
-        r.vec[i : i + 1, :] = jnp.sum(rows, axis=0, keepdims=True)
+    r.gm_own[...] = total
     for i in range(4):
         part = dot_nt(r.hidden_low[...], r.wo_all[2 * i : 2 * i + 2].reshape(256, 1024))
         r.gmix[:, :, i * 256 : i * 256 + 256] = part.astype(BF16).reshape(2, 64, 256)
@@ -634,6 +648,10 @@
         r.g_out[pl.ds(2 * i, 2)] = part.astype(BF16).reshape(2, 2, 64, 1024)
 
     pair_sum(0)
+    total = r.gm_own[...]
+    normed, _ = norm_rows(r.hidden[...])
+    for i, rows in enumerate((r.grad_hidden[...], total * normed, total, r.cot_all[z].astype(F32))):
+        r.vec[i : i + 1, :] = jnp.sum(rows, axis=0, keepdims=True)
     loop(4, out_rows)
     near_to(2).start()
     await_block(r.gmixed.at[0:15], r.mf_r.at[0])
@@ -692,6 +710,7 @@
         r.gparts[i, :, :, 128:256] = acc.astype(BF16).reshape(4, 64, 128)
         back_start(1, i)
 
+    pair_sum(2)
     loop(4, keys_back)
     r.gback[q4] = r.gparts[:, q4]
     wide = lax.broadcasted_iota(jnp.int32, (1, 1024), 1) // 128 == 2 * z + core
@@ -699,16 +718,7 @@
         r.vec[i : i + 1, :] = jnp.where(wide, jnp.concatenate([sums] * 8, axis=1), 0.0)
 
     pair_sum(1)
-    pair_sum(2)
     first_sum("two")
-    total = r.mo_own[...] + r.small_all[7:8, :]
-    await_block(r.mo_in.at[1:4], r.mo_r.at[0])
-    for k in (1, 3, 2):
-        total = total + r.mo_in[k].astype(F32)
-    r.w_layer[...] = (valid_of(z) * (r.hidden[...] + total)).astype(BF16)
-    results = [pltpu.make_async_copy(r.w_layer, r.layer_out, r.done.at[0])]
-    results[0].start()
-
     await_block(r.gback.at[0:3], r.hb_r.at[0])
 
     def assemble(origin):
@@ -735,35 +745,39 @@
             def _():
                 r.ga_own[:, cols] = part
 
-    halves = {1: slice(0, 64), 3: slice(64, 128)}
-
     def via_to(k):
         return remote(
-            r.ga_out.at[lax.rem(z + 2, 4), halves[k]], r.ga_via.at[k], r.ga_s.at[0], r.gv_r.at[k], z_peer(k)
+            r.ga_out.at[lax.rem(z + 2, 4), halves[k][0]], r.ga_via.at[k], r.ga_s.at[0], r.gv_r.at[k], z_peer(k)
         )
 
     def via_add(k):
         await_block(r.ga_via.at[k], r.gv_r.at[k])
-        target = lax.rem(z + k, 4)
-        total = r.ga_out[target, halves[k]].astype(F32) + r.ga_via[k].astype(F32)
-        r.ga_out[target, halves[k]] = total.astype(BF16)
-        part_to(r.ga_out, r.ga_in, ga_sems, k).start()
+        target, rows = lax.rem(z + k, 4), halves[k][0]
+        total = r.ga_out[target, rows].astype(F32) + r.ga_via[k].astype(F32)
+        r.ga_out[target, rows] = total.astype(BF16)
+        ga_to(k, 0).start()
+
+    def ga_to(k, h):
+        rows = halves[k][h]
+        return remote(
+            r.ga_out.at[lax.rem(z + k, 4), rows], r.ga_in.at[k, rows], r.ga_s.at[0], r.ga_r.at[0], z_peer(k)
+        )
 
     attn_back(2)
     via_to(1).start()
     via_to(3).start()
+    loop(2, lambda k: attn_back(1 + 2 * k))
+    ga_to(1, 1).start()
+    ga_to(3, 1).start()
+    attn_back(0)
+    vec_across = remote(r.vec, r.vec_sib, r.vs_s.at[0], r.vs_r.at[0], sib)
+    vec_across.start()
     outer("qka", r.attn_all, r.gqkv, 384)
     near_to(3).start()
     outer("qkb", r.attn_all, r.gqkv, 384, 384)
     near_to(4).start()
-    loop(2, lambda k: attn_back(1 + 2 * k))
     via_add(1)
     via_add(3)
-    pair_sum(3)
-    pair_sum(4)
-    attn_back(0)
-    vec_across = remote(r.vec, r.vec_sib, r.vs_s.at[0], r.vs_r.at[0], sib)
-    vec_across.start()
     await_block(r.vec_sib, r.vs_r.at[0])
     await_sent(r.vec_sib, r.vs_s.at[0])
     r.vec[...] += r.vec_sib[...]
@@ -774,6 +788,16 @@
         return remote(r.vec.at[:, columns_of(peer)], r.vec_in.at[k], r.v1_s.at[0], r.v1_r.at[0], (2 * peer + core, s))
 
     loop(8, lambda k: vec_to(k).start(), 1)
+    pair_sum(3)
+    pair_sum(4)
+    total = r.mo_own[...] + r.small_all[7:8, :]
+    await_block(r.mo_in.at[1:4], r.mo_r.at[0])
+    for k in (1, 3, 2):
+        total = total + r.mo_in[k].astype(F32)
+    r.w_layer[...] = (valid_of(z) * (r.hidden[...] + total)).astype(BF16)
+    results = [pltpu.make_async_copy(r.w_layer, r.layer_out, r.done.at[0])]
+    results[0].start()
+
 
     my_part = pl.ds(pick(lax.rem(x, 2) * 2 + yl, 8), 8)
 
@@ -967,8 +991,8 @@
         LAYER_OUT,
         LAYER_SCRATCH,
         dict(
-            lengths=lengths,
-            block_pairs=block_pairs,
+            lengths=lengths.reshape(1, 2),
+            block_pairs=block_pairs.reshape(1, 16),
             tok=tokens.reshape(128, 1024),
             ln1_gain=ln1_gain.reshape(1, 128),
             ln1_bias=ln1_bias.reshape(1, 128),

time: 133 us -> 132 us (level)
  no operation moved by 1% of the time
where the time goes in v7:
time: 132 us; the launch traced here: 131 us
  Pallas kernels  131 us (99%)
    pallas_call x1, Pallas kernels, named_call(): pl.pallas_call(kernel, name=name, out_shape=[jax.ShapeDtypeStruct(shape,...  128 us

profile of v7, /device:TPU:0, one launch (start us, length us, event | category | flops | bytes accessed | tf_op | source)
XLA Modules:
  0.0 131.3 jit_solution(12704906553741983440)
XLA Ops:
  0.7 128.4 %layer.1 = (bf16[128,1024]{1,0:T(8,128)(2,1)}, bf16[128,1024]{1,0:T(8,128)(2,1)}, f32[8,3072]{1,0:T(8,128)}, f32[8,1024]{1,0:T(8,128)}, f32[8,4096]{1,0:T(8,128)...) custom-call(s32[1,2]{1,0:T(1,128)} %bitcast.27, s32[1,16]{1,0:T(1,128)} %bitcast.28, bf16[128,1024]{1,0:T(8,128)(2,1)} %bitcast.24, ...), custom_call_target="tpu_custom_call" | custom-call | tf_op jit(solution)/shard_map/layer/pallas_call | solution.py:953
  129.1 2.2 %owner.1 = (bf16[128,1024]{1,0:T(8,128)(2,1)}, bf16[128,1024]{1,0:T(8,128)(2,1)}, f32[8,3072]{1,0:T(8,128)}, f32[8,1024]{1,0:T(8,128)}, f32[8,4096]{1,0:T(8,128)...) custom-call(bf16[128,1024]{1,0:T(8,128)(2,1)} %get-tuple-element.37., ...), custom_call_target="tpu_custom_call" | custom-call | tf_op jit(solution)/shard_map/owner/pallas_call | solution.py:943

commit v8 on v7

--- a/solution.py
+++ b/solution.py
@@ -655,8 +655,6 @@
     loop(4, out_rows)
     near_to(2).start()
     await_block(r.gmixed.at[0:15], r.mf_r.at[0])
-    for k in (1, 3, 2):
-        part_to(r.mo_out, r.mo_in, mo_sems, k).start()
 
     def back_to(m, piece, i):
         peer = lax.rem(q4 + m, 4)
@@ -701,6 +699,8 @@
         back_start(0, i)
         return jnp.sum(gq, axis=0, keepdims=True)
 
+    for k in (1, 3, 2):
+        part_to(r.mo_out, r.mo_in, mo_sems, k).start()
     bias_q = lax.fori_loop(0, 4, lambda i, acc: acc + scores_back(i), jnp.zeros((1, 128), F32))
 
     def keys_back(i):
@@ -766,16 +766,16 @@
     attn_back(2)
     via_to(1).start()
     via_to(3).start()
+    outer("qka", r.attn_all, r.gqkv, 384)
+    near_to(3).start()
+    outer("qkb", r.attn_all, r.gqkv, 384, 384)
+    near_to(4).start()
     loop(2, lambda k: attn_back(1 + 2 * k))
     ga_to(1, 1).start()
     ga_to(3, 1).start()
     attn_back(0)
     vec_across = remote(r.vec, r.vec_sib, r.vs_s.at[0], r.vs_r.at[0], sib)
     vec_across.start()
-    outer("qka", r.attn_all, r.gqkv, 384)
-    near_to(3).start()
-    outer("qkb", r.attn_all, r.gqkv, 384, 384)
-    near_to(4).start()
     via_add(1)
     via_add(3)
     await_block(r.vec_sib, r.vs_r.at[0])

time: 132 us -> 132 us (level)
  no operation moved by 1% of the time
where the time goes in v8:
time: 132 us; the launch traced here: 131 us
  Pallas kernels  131 us (99%)
    pallas_call x1, Pallas kernels, named_call(): pl.pallas_call(kernel, name=name, out_shape=[jax.ShapeDtypeStruct(shape,...  129 us

profile of v8, /device:TPU:0, one launch (start us, length us, event | category | flops | bytes accessed | tf_op | source)
XLA Modules:
  0.0 131.4 jit_solution(7346884494294815858)
XLA Ops:
  0.7 128.6 %layer.1 = (bf16[128,1024]{1,0:T(8,128)(2,1)}, bf16[128,1024]{1,0:T(8,128)(2,1)}, f32[8,3072]{1,0:T(8,128)}, f32[8,1024]{1,0:T(8,128)}, f32[8,4096]{1,0:T(8,128)...) custom-call(s32[1,2]{1,0:T(1,128)} %bitcast.27, s32[1,16]{1,0:T(1,128)} %bitcast.28, bf16[128,1024]{1,0:T(8,128)(2,1)} %bitcast.24, ...), custom_call_target="tpu_custom_call" | custom-call | tf_op jit(solution)/shard_map/layer/pallas_call | solution.py:953
  129.2 2.2 %owner.1 = (bf16[128,1024]{1,0:T(8,128)(2,1)}, bf16[128,1024]{1,0:T(8,128)(2,1)}, f32[8,3072]{1,0:T(8,128)}, f32[8,1024]{1,0:T(8,128)}, f32[8,4096]{1,0:T(8,128)...) custom-call(bf16[128,1024]{1,0:T(8,128)(2,1)} %get-tuple-element.37., ...), custom_call_target="tpu_custom_call" | custom-call | tf_op jit(solution)/shard_map/owner/pallas_call | solution.py:943
